TPU v7x, 256 devices: a whole 4x4x8 slice. The times are simulated.
256 devices in a mesh: mesh: 32 (over x, z), harm: 8 (over y, core).
Axes of the slice: x: 4, y: 4, z: 8, core: 2. Of those that a mesh axis runs over, the one named last changes fastest.
Arguments:
- adjoint_rhs: float32 [16, 6, 2, 65536], P('harm', None, None, 'mesh'), may hold values from -20 to 20
- forward_field: float32 [16, 2, 65536], P('harm', None, 'mesh'), may hold values from -6 to 6
- stiffness: float32 [64, 64, 4096], P(None, None, 'mesh'), may hold values from -1 to 3, as said below
- mass_blocks: float32 [64, 64, 4096], P(None, None, 'mesh'), may hold values from -1 to 3, as said below
- frequency: float32 [16], P('harm'), may hold values from 0.25 to 4
- edge_mass: float32 [65536], P('mesh'), may hold values from 0.5 to 2
- connectivity: int32 [64, 4096], P(None, 'mesh'), may hold values from 0 to 3071, as said below
- send_list: int32 [32, 2, 512], P('mesh'), may hold values from -1 to 2047, as said below
- node_block: int32 [32768], P('mesh'), may hold values from 0 to 127
- node_shape: float32 [3, 64, 32768], P(None, None, 'mesh'), may hold values from -0.1875 to 0.1875
Outputs:
- adjoint: float32 [16, 6, 2, 65536], P('harm', None, None, 'mesh')
- shape_gradient: float32 [6, 3, 32768], P(None, None, ('mesh', 'harm'))
Inputs may be any that keep to these rules, and one draw needn't show every extreme that they name: `stiffness`: each block is symmetric and its diagonal exceeds the sum of magnitudes of the other entries of its row. `mass_blocks`: each block is symmetric and its diagonal exceeds the sum of magnitudes of the other entries of its row. `send_list`: row 0 of a device lists owned edges shared with the device one lower along mesh, row 1 those shared with the device one higher; valid entries come first, then -1. A list holds at most 512 valid entries, and some device's row 0 and some device's row 1 hold exactly 512. The first device's row 0 and the last device's row 1 are empty. `connectivity`: an entry below 2048 is an edge the device owns; 2048 + k is entry k of the lower neighbour's row 1; 2560 + k is entry k of the upper neighbour's row 0. Only valid entries are named.
All inputs are finite; a program needn't handle non-finite values.
Results may differ from a plain program's by a relative error of at most 0.0003.
Values sent between devices are 32-bit elements; how exact they have to be, the bound alone decides.
No kernel may reach another device: no remote copies, remote signals or barrier semaphores. Data moves between devices by JAX's collectives and lax.ppermute only.
A program may use at most 128 MiB of HBM per device.

v0:
```python
import jax
import jax.numpy as jnp
from jax import lax
from jax.sharding import PartitionSpec as P

ITERS = 3


exact_mode = lax.Precision.HIGHEST


def extended_2(cells, sides, width):
    for axis, dim in sides:
        count = lax.axis_size(axis)
        ends = count - 1
        head = lax.slice_in_dim(cells, 0, width, axis=dim)
        tail = lax.slice_in_dim(cells, cells.shape[dim] - width, cells.shape[dim], axis=dim)
        cells = jnp.concatenate(
            [
                lax.ppermute(tail, axis, [(i, (i + 1) % count) for i in range(ends)]),
                cells,
                lax.ppermute(head, axis, [((i + 1) % count, i) for i in range(ends)]),
            ],
            axis=dim,
        )
    return cells


def from_behind(shard, axis, by):
    devices = lax.axis_size(axis)
    pairs = [(i, i + by) for i in range(devices) if 0 <= i + by < devices]
    return lax.ppermute(shard, axis, pairs)


def block_product(matrices, gathered):
    return jnp.einsum("ijb,rjb->rib", matrices, gathered, precision=exact_mode)


def per_device(
    adjoint_rhs,
    forward_field,
    stiffness,
    mass_blocks,
    frequency,
    edge_mass,
    connectivity,
    send_list,
    node_block,
    node_shape,
):
    harm_local, force_count, part_count, edge_count = adjoint_rhs.shape
    slot_count = send_list.shape[2]
    row_count = harm_local * force_count * part_count
    list_rows = send_list[0]
    is_listed = list_rows >= 0
    safe_rows = jnp.maximum(list_rows, 0)
    row_weights = jnp.repeat(frequency, force_count * part_count)
    field_weights = jnp.repeat(frequency, part_count)

    def fetch_rim(values_now):
        picked = jnp.where(is_listed[None], values_now[:, safe_rows], 0.0)
        send_buffer = picked.reshape(values_now.shape[0], 2 * slot_count)
        padded = extended_2(send_buffer, (("mesh", 1),), slot_count)
        return jnp.concatenate([padded[:, :slot_count], padded[:, 3 * slot_count :]], axis=1)

    def assemble(values_now, rim_now, weights):
        extended = jnp.concatenate([values_now, rim_now], axis=1)
        gathered = extended[:, connectivity]
        return block_product(stiffness, gathered) + weights[:, None, None] * block_product(
            mass_blocks, gathered
        )

    rhs_rows = adjoint_rhs.reshape(row_count, edge_count)
    field_rows = forward_field.reshape(harm_local * part_count, edge_count)
    first_rim = fetch_rim(rhs_rows)
    solution = jnp.zeros_like(rhs_rows)
    residual = rhs_rows

    def squares(values_now):
        return lax.psum(jnp.sum(values_now * values_now), ("mesh", "harm"))

    direction = residual
    norm_now = squares(residual)
    for iteration in range(ITERS):
        rim_now = first_rim if iteration == 0 else fetch_rim(direction)
        rows_now = direction.shape[0]
        local_terms = assemble(direction, rim_now, row_weights)
        totals = jnp.zeros((rows_now, edge_count + 2 * slot_count), jnp.float32)
        totals = totals.at[:, connectivity.reshape(-1)].add(local_terms.reshape(rows_now, -1))
        owned = totals[:, :edge_count]
        from_upper = from_behind(totals[:, edge_count : edge_count + slot_count], "mesh", -1)
        from_lower = from_behind(totals[:, edge_count + slot_count :], "mesh", 1)
        owned = owned.at[:, safe_rows[1]].add(jnp.where(is_listed[1][None], from_upper, 0.0))
        owned = owned.at[:, safe_rows[0]].add(jnp.where(is_listed[0][None], from_lower, 0.0))
        applied = owned + row_weights[:, None] * edge_mass[None, :] * direction
        step_size = norm_now / lax.psum(jnp.sum(direction * applied), ("mesh", "harm"))
        solution = solution + step_size * direction
        residual = residual - step_size * applied
        norm_next = squares(residual)
        direction = residual + norm_next / norm_now * direction
        norm_now = norm_next
    final_rims = fetch_rim(jnp.concatenate([solution, field_rows], axis=0))
    solution_rim = final_rims[:row_count]
    field_rim = final_rims[row_count:]
    block_edges, block_count = connectivity.shape
    field_terms = assemble(field_rows, field_rim, field_weights).reshape(
        harm_local, part_count, block_edges, block_count
    )
    adjoint_blocks = jnp.concatenate([solution, solution_rim], axis=1)[:, connectivity]
    adjoint_blocks = adjoint_blocks.reshape(
        harm_local, force_count, part_count, block_edges, block_count
    )
    energy_term = jnp.sum(
        adjoint_blocks[:, :, 0] * field_terms[:, None, 0]
        - adjoint_blocks[:, :, 1] * field_terms[:, None, 1],
        axis=0,
    )
    at_nodes = energy_term[:, :, node_block]
    local_grad = -jnp.einsum("kjn,ojn->okn", node_shape, at_nodes, precision=exact_mode)
    summed = lax.psum(local_grad, "harm")
    share_size = local_grad.shape[2] // lax.axis_size("harm")
    gradient = lax.dynamic_slice_in_dim(summed, lax.axis_index("harm") * share_size, share_size, 2)
    return (solution.reshape(adjoint_rhs.shape), gradient)


def solution(mesh):
    return jax.shard_map(
        per_device,
        mesh=mesh,
        in_specs=(
            P("harm", None, None, "mesh"),
            P("harm", None, "mesh"),
            P(None, None, "mesh"),
            P(None, None, "mesh"),
            P("harm"),
            P("mesh"),
            P(None, "mesh"),
            P("mesh", None, None),
            P("mesh"),
            P(None, None, "mesh"),
        ),
        out_specs=(P("harm", None, None, "mesh"), P(None, None, ("mesh", "harm"))),
        check_vma=False,
    )
```

profile of v0, /device:TPU:2, one launch (start us, length us, event | category | flops | bytes accessed | tf_op | source)
XLA Modules:
  0.0 1010.1 jit_solution(11621693017519007216)
XLA Ops:
  23.4 5.8 collective-permute-start.1
  31.7 4.5 copy.190
  36.4 5.6 copy.191
  44.0 27.7 %gather_fusion.1 = f32[8192,24]{1,0:T(8,128)} fusion(f32[24,3072]{0,1:T(8,128)S(1)} %pad_maximum_fusion, s32[8192]{0:T(1024)S(1)} %fusion.70), kind=kCustom, calls=%fused_computation.1 | custom fusion | bytes 1605632 | tf_op jit(solution)/shard_map/gather | solution.py:68
  75.4 8.8 fusion.12
  84.1 7.9 add_bitcast_fusion.2
  97.0 44.7 %scatter_custom_fusion = f32[24,3072]{0,1:T(8,128)S(1)} fusion(s32[8192]{0:T(1024)S(1)} %bitcast.176, f32[8192,24]{1,0:T(8,128)} %copy.193, f32[]{:T(128)} %constant.7.clone.1), kind=kCustom, calls=%fused_computation.48 | custom fusion | flops 196608 | bytes 295424 | tf_op jit(solution)/shard_map/scatter-add | solution.py:89
  160.3 15.4 %scatter_custom_fusion.2 = f32[24,2048]{0,1:T(8,128)S(1)} fusion(f32[24,2048]{0,1:T(8,128)S(1)} %scatter_custom_fusion.1, s32[512]{0:T(512)S(1)} %bitcast.180, f32[24,512]{0,1:T(8,128)S(1)} %collective-permute-done.3, f32[]{:T(128)} %constant.7.clone.1, pred[512]{0:T(512)(128)(4,1)S(1)} %get-tuple-element.14), kind=kCustom, calls=%fused_computation.74 | custom fusion | flops 24576 | bytes 459268 | tf_op jit(solution)/shard_map/scatter-add | solution.py:94
  176.8 74.8 %all-reduce = (f32[]{:T(128)}, f32[]{:T(128)}) all-reduce(f32[]{:T(128)} %multiply_reduce_fusion.5, f32[]{:T(128)} %multiply_reduce_fusion), channel_id=1, replica_groups=mesh['mesh'=32,'harm'=8] {'mesh','harm'}, use_global_device_ids=true, to_apply=%region_1.2 | all-reduce | flops 2 | bytes 16 | tf_op jit(solution)/shard_map/psum | solution.py:80
  253.4 73.6 %psum.51 = f32[]{:T(128)} all-reduce(f32[]{:T(128)} %get-tuple-element.18), channel_id=1, replica_groups=mesh['mesh'=32,'harm'=8] {'mesh','harm'}, use_global_device_ids=true, to_apply=%region_8.9 | all-reduce | flops 1 | bytes 8 | tf_op jit(solution)/shard_map/psum | solution.py:80
  335.4 4.3 collective-permute-start.5
  341.9 27.7 %gather_fusion.3 = f32[8192,24]{1,0:T(8,128)} fusion(f32[24,3072]{0,1:T(8,128)S(1)} %copy.200, s32[8192]{0:T(1024)S(1)} %fusion.70), kind=kCustom, calls=%fused_computation.3 | custom fusion | bytes 1605632 | tf_op jit(solution)/shard_map/gather | solution.py:68
  373.3 8.5 fusion.8
  381.8 6.6 add_bitcast_fusion.1
  392.1 45.1 %scatter_custom_fusion.3 = f32[24,3072]{0,1:T(8,128)S(1)} fusion(s32[8192]{0:T(1024)} %bitcast.177, f32[8192,24]{1,0:T(8,128)} %copy.205, f32[]{:T(128)} %constant.7.clone.1), kind=kCustom, calls=%fused_computation.46 | custom fusion | flops 196608 | bytes 295424 | tf_op jit(solution)/shard_map/scatter-add | solution.py:89
  437.6 6.4 collective-permute-start.6
  459.4 73.2 %psum.52 = f32[]{:T(128)} all-reduce(f32[]{:T(128)} %multiply_reduce_fusion.3), channel_id=1, replica_groups=mesh['mesh'=32,'harm'=8] {'mesh','harm'}, use_global_device_ids=true, to_apply=%region_13.14 | all-reduce | flops 1 | bytes 8 | tf_op jit(solution)/shard_map/psum | solution.py:96
  534.5 73.3 %psum.53 = f32[]{:T(128)} all-reduce(f32[]{:T(128)} %multiply_reduce_fusion.2), channel_id=1, replica_groups=mesh['mesh'=32,'harm'=8] {'mesh','harm'}, use_global_device_ids=true, to_apply=%region_15.16 | all-reduce | flops 1 | bytes 8 | tf_op jit(solution)/shard_map/psum | solution.py:80
  623.1 27.9 %gather_fusion.5 = f32[8192,24]{1,0:T(8,128)} fusion(f32[24,3072]{0,1:T(8,128)S(1)} %copy.212, s32[8192]{0:T(1024)S(1)} %copy-done.9), kind=kCustom, calls=%fused_computation.5 | custom fusion | bytes 1605632 | tf_op jit(solution)/shard_map/gather | solution.py:68
  654.6 8.5 fusion.4
  663.2 7.9 add_bitcast_fusion
  676.0 44.9 %scatter_custom_fusion.6 = f32[24,3072]{0,1:T(8,128)S(1)} fusion(s32[8192]{0:T(1024)} %bitcast.178, f32[8192,24]{1,0:T(8,128)} %copy.217, f32[]{:T(128)} %constant.7.clone.1), kind=kCustom, calls=%fused_computation.44 | custom fusion | flops 196608 | bytes 295424 | tf_op jit(solution)/shard_map/scatter-add | solution.py:89
  722.0 6.1 collective-permute-start.10
  743.7 73.5 %psum.54 = f32[]{:T(128)} all-reduce(f32[]{:T(128)} %multiply_reduce_fusion.1), channel_id=1, replica_groups=mesh['mesh'=32,'harm'=8] {'mesh','harm'}, use_global_device_ids=true, to_apply=%region_20.21 | all-reduce | flops 1 | bytes 8 | tf_op jit(solution)/shard_map/psum | solution.py:96
  825.9 5.9 collective-permute-start.13
  834.2 28.0 %gather_fusion.8 = f32[8192,4]{1,0:T(8,128)} fusion(f32[4,3072]{0,1:T(8,128)S(1)} %copy.225, s32[8192]{0:T(1024)S(1)} %copy-done.9), kind=kCustom, calls=%fused_computation.8 | custom fusion | bytes 294912 | tf_op jit(solution)/shard_map/gather | solution.py:68
  866.0 8.5 fusion.33
  874.5 6.6 fusion.22
  882.0 27.7 %gather_fusion.7 = f32[8192,24]{1,0:T(8,128)} fusion(f32[24,3072]{0,1:T(8,128)S(1)} %copy.223, s32[8192]{0:T(1024)S(1)} %copy-done.9), kind=kCustom, calls=%fused_computation.7 | custom fusion | bytes 1605632 | tf_op jit(solution)/shard_map/gather | solution.py:109
  913.3 9.1 gather_fusion.9
  922.4 10.0 negate_bitcast_fusion
  933.3 67.8 %all-reduce.3.cloned.1.call-done = f32[6,3,1024]{0,1,2:T(4,128)} async-done(((f32[6,3,1024]{0,1,2:T(4,128)}), f32[6,3,1024]{0,1,2:T(4,128)}) %all-reduce.3.cloned.1.call-update) | async-done | bytes 73744 | tf_op jit(solution)/shard_map/psum | solution.py:120
  (194 shorter events, 142.2 us)
Async XLA Ops:
  7.2 993.9 %all-reduce.3.cloned.1.call-start = ((), (), s32[]{:S(2)}) async-start(), calls=%async_computation | async-start | bytes 4194304 | tf_op jit(solution)/shard_map/psum | solution.py:120
  9.7 19.6 %copy-start.10 = (f32[2,6,2,2048]{3,2,1,0:T(2,128)S(1)}, f32[2,6,2,2048]{3,2,1,0:T(2,128)}, u32[]{:S(2)}) copy-start(f32[2,6,2,2048]{3,2,1,0:T(2,128)} %param.10) | copy-start | bytes 589828
  9.7 22.0 %copy-start.7 = (f32[64,64,128]{2,1,0:T(8,128)S(1)}, f32[64,64,128]{2,1,0:T(8,128)}, u32[]{:S(2)}) copy-start(f32[64,64,128]{2,1,0:T(8,128)} %param.12) | copy-start | bytes 6291460
  19.6 22.4 %collective-permute-start = (f32[24,512]{1,0:T(8,128)}, f32[24,512]{1,0:T(8,128)}, u32[]{:S(2)}, u32[]{:S(2)}) collective-permute-start(f32[24,512]{1,0:T(8,128)} %get-tuple-element.34), channel_id=1, source_target_pairs={{0,8},{8,16},{16,24},{24,32},{32,40},{40,48},{48,56},{56,64},{64,7... | collective-permute-start | bytes 147464 | tf_op jit(solution)/shard_map/ppermute | solution.py:20
  23.4 19.5 %collective-permute-start.1 = (f32[24,512]{1,0:T(8,128)}, f32[24,512]{1,0:T(8,128)}, u32[]{:S(2)}, u32[]{:S(2)}) collective-permute-start(f32[24,512]{1,0:T(8,128)} %get-tuple-element.35), channel_id=1, source_target_pairs={{8,0},{16,8},{24,16},{32,24},{40,32},{48,40},{56,48},{64,56},{72,6... | collective-permute-start | bytes 147464 | tf_op jit(solution)/shard_map/ppermute | solution.py:22
  30.8 311.1 %copy-start.8 = (s32[8192]{0:T(1024)}, s32[8192]{0:T(1024)S(1)}, u32[]{:S(2)}) copy-start(s32[8192]{0:T(1024)S(1)} %fusion.70) | copy-start | bytes 98308
  31.6 65.4 %copy-start.14 = (s32[8192,1]{0,1:T(1,128)}, s32[8192,1]{0,1:T(1,128)S(1)}, u32[]{:S(2)}) copy-start(s32[8192,1]{0,1:T(1,128)S(1)} %compare_select_fusion) | copy-start | bytes 98308
  31.6 123.3 %copy-start.27 = (s32[512,1]{0,1:T(1,128)}, s32[512,1]{0,1:T(1,128)S(1)}, u32[]{:S(2)}) copy-start(s32[512,1]{0,1:T(1,128)S(1)} %get-tuple-element.37) | copy-start | bytes 6148
  31.7 128.6 %copy-start.26 = (s32[512,1]{0,1:T(1,128)}, s32[512,1]{0,1:T(1,128)S(1)}, u32[]{:S(2)}) copy-start(s32[512,1]{0,1:T(1,128)S(1)} %get-tuple-element.36) | copy-start | bytes 6148
  31.7 123.3 %copy-start.22 = (pred[512]{0:T(512)(128)(4,1)}, pred[512]{0:T(512)(128)(4,1)S(1)}, u32[]{:S(2)}) copy-start(pred[512]{0:T(512)(128)(4,1)S(1)} %get-tuple-element.15) | copy-start | bytes 1540
  31.7 128.5 %copy-start.19 = (pred[512]{0:T(512)(128)(4,1)}, pred[512]{0:T(512)(128)(4,1)S(1)}, u32[]{:S(2)}) copy-start(pred[512]{0:T(512)(128)(4,1)S(1)} %get-tuple-element.14) | copy-start | bytes 1540
  36.4 114.6 %copy-start.15 = (f32[24]{0:T(128)}, f32[24]{0:T(128)S(1)}, u32[]{:S(2)}) copy-start(f32[24]{0:T(128)S(1)} %mul.153) | copy-start | bytes 292
  145.1 9.9 collective-permute-start.2
  149.0 11.2 %collective-permute-start.3 = (f32[24,512]{0,1:T(8,128)S(1)}, f32[24,512]{0,1:T(8,128)S(1)}, u32[]{:S(2)}, u32[]{:S(2)}) collective-permute-start(f32[24,512]{0,1:T(8,128)S(1)} %get-tuple-element.24), channel_id=1, source_target_pairs={{0,8},{8,16},{16,24},{24,32},{32,40},{40,48},{48,56},{56,64},{64,7... | collective-permute-start | bytes 147464 | tf_op jit(solution)/shard_map/ppermute | solution.py:32
  253.4 74.8 %copy-start.5 = (f32[24,2048]{1,0:T(8,128)}, f32[24,2048]{1,0:T(8,128)S(1)}, u32[]{:S(2)}) copy-start(f32[24,2048]{1,0:T(8,128)S(1)} %get-tuple-element.19) | copy-start | bytes 589828
  331.7 8.1 collective-permute-start.4
  335.4 6.0 collective-permute-start.5
  437.3 10.8 %copy-start.23 = (pred[512]{0:T(512)(128)(4,1)S(1)}, pred[512]{0:T(512)(128)(4,1)}, u32[]{:S(2)}) copy-start(pred[512]{0:T(512)(128)(4,1)} %copy-done.22) | copy-start | bytes 1540
  437.6 10.5 %collective-permute-start.6 = (f32[24,512]{0,1:T(8,128)S(1)}, f32[24,512]{0,1:T(8,128)S(1)}, u32[]{:S(2)}, u32[]{:S(2)}) collective-permute-start(f32[24,512]{0,1:T(8,128)S(1)} %get-tuple-element.23), channel_id=1, source_target_pairs={{8,0},{16,8},{24,16},{32,24},{40,32},{48,40},{56,48},{64,56},{72,6... | collective-permute-start | bytes 147464 | tf_op jit(solution)/shard_map/ppermute | solution.py:32
  444.0 10.4 %copy-start.20 = (pred[512]{0:T(512)(128)(4,1)S(1)}, pred[512]{0:T(512)(128)(4,1)}, u32[]{:S(2)}) copy-start(pred[512]{0:T(512)(128)(4,1)} %copy-done.19) | copy-start | bytes 1540
  444.0 10.4 %collective-permute-start.7 = (f32[24,512]{0,1:T(8,128)S(1)}, f32[24,512]{0,1:T(8,128)S(1)}, u32[]{:S(2)}, u32[]{:S(2)}) collective-permute-start(f32[24,512]{0,1:T(8,128)S(1)} %get-tuple-element.22), channel_id=1, source_target_pairs={{0,8},{8,16},{16,24},{24,32},{32,40},{40,48},{48,56},{56,64},{64,7... | collective-permute-start | bytes 147464 | tf_op jit(solution)/shard_map/ppermute | solution.py:32
  452.1 81.7 %copy-start.6 = (f32[24,2048]{1,0:T(8,128)S(1)}, f32[24,2048]{1,0:T(8,128)}, u32[]{:S(2)}) copy-start(f32[24,2048]{1,0:T(8,128)} %copy-done.5) | copy-start | bytes 589828
  612.5 10.5 %copy-start.9 = (s32[8192]{0:T(1024)S(1)}, s32[8192]{0:T(1024)}, u32[]{:S(2)}) copy-start(s32[8192]{0:T(1024)} %copy-done.8) | copy-start | bytes 98308
  612.6 8.1 collective-permute-start.8
  616.6 6.0 collective-permute-start.9
  721.7 10.9 %copy-start.24 = (pred[512]{0:T(512)(128)(4,1)S(1)}, pred[512]{0:T(512)(128)(4,1)}, u32[]{:S(2)}) copy-start(pred[512]{0:T(512)(128)(4,1)} %copy-done.22) | copy-start | bytes 1540
  722.0 10.5 %collective-permute-start.10 = (f32[24,512]{0,1:T(8,128)}, f32[24,512]{0,1:T(8,128)S(1)}, u32[]{:S(2)}, u32[]{:S(2)}) collective-permute-start(f32[24,512]{0,1:T(8,128)} %get-tuple-element.21), channel_id=1, source_target_pairs={{8,0},{16,8},{24,16},{32,24},{40,32},{48,40},{56,48},{64,56},{72,6... | collective-permute-start | bytes 147464 | tf_op jit(solution)/shard_map/ppermute | solution.py:32
  728.2 10.4 %copy-start.21 = (pred[512]{0:T(512)(128)(4,1)S(1)}, pred[512]{0:T(512)(128)(4,1)}, u32[]{:S(2)}) copy-start(pred[512]{0:T(512)(128)(4,1)} %copy-done.19) | copy-start | bytes 1540
  728.2 10.4 %collective-permute-start.11 = (f32[24,512]{0,1:T(8,128)S(1)}, f32[24,512]{0,1:T(8,128)S(1)}, u32[]{:S(2)}, u32[]{:S(2)}) collective-permute-start(f32[24,512]{0,1:T(8,128)S(1)} %get-tuple-element.20), channel_id=1, source_target_pairs={{0,8},{8,16},{16,24},{24,32},{32,40},{40,48},{48,56},{56,64},{64,7... | collective-permute-start | bytes 147464 | tf_op jit(solution)/shard_map/ppermute | solution.py:32
  821.9 9.9 collective-permute-start.12
  825.9 7.8 collective-permute-start.13
  913.3 9.1 copy-start.4
  (13 other events, 85.7 us)
Sparse Core Ops, SparseCore 0:
  932.6 68.4 all-reduce.2
where the time goes:
time: 1020 us; the launch traced here: 1010 us
  blocking collectives  368 us (36%)
  local copies, waits for them, and re-layouts  225 us (22%)
  other arithmetic  180 us (18%)
  waiting for transfers between devices  85.5 us (8%)
  matrix products  73.3 us (7%)
  starting transfers between devices  55.7 us (5%)
  between operations  21.8 us (2%)
    psum x3, blocking collectives, squares(): return lax.psum(jnp.sum(values_now * values_now), ('mesh', 'harm'))  222 us
    psum x2, blocking collectives, per_device(): lax.psum(jnp.sum(direction * applied), ('mesh', 'harm'))  147 us
    scatter-add x3, other arithmetic, per_device(): totals.at[:, connectivity.reshape(-1)]  135 us
    gather x8, local copies, waits for them, and re-layouts, assemble(): gathered = extended[:, connectivity]  126 us
    psum x1, waiting for transfers between devices, per_device(): summed = lax.psum(local_grad, 'harm')  67.8 us
    dot_general x8, matrix products, block_product(): return jnp.einsum('ijb,rjb->rib', matrices, gathered, precision=exact_mode)  63.2 us
    gather x2, local copies, waits for them, and re-layouts, per_device(): jnp.concatenate([solution, solution_rim], axis=1)[:, connectivity]  30.6 us
    scatter-add x3, other arithmetic, per_device(): owned.at[:, safe_rows[0]]  23.6 us
  transfers between devices with their start and end apart: 15, of which 12 were waited for; matrix products, arithmetic and copies ran while one was open for 3% of the time, Pallas kernels for 0%

commit v1 on v0

v1 whole, which is shorter than its diff:
```python
import functools

import jax
import jax.numpy as jnp
from jax import lax
from jax.experimental import pallas as pl
from jax.experimental.pallas import tpu as pltpu
from jax.sharding import PartitionSpec as P

f32 = jnp.float32
bf16 = jnp.bfloat16
i32 = jnp.int32
LANES = 128
EDGES = 2048
SLOTS = 512
ROWS = 24
EB = 64
OWN_T, GHOST_T = EDGES // LANES, SLOTS // LANES
BOTH = ("mesh", "harm")

VMEM = pl.BlockSpec(memory_space=pltpu.VMEM)
SMEM = pl.BlockSpec(memory_space=pltpu.SMEM)


def kernel_call(body, name, out, specs, scratch=(), flops=0, nbytes=0):
    return pl.pallas_call(
        body,
        name=name,
        out_shape=out,
        in_specs=specs,
        out_specs=jax.tree.map(lambda _: VMEM, out),
        scratch_shapes=scratch,
        compiler_params=pltpu.CompilerParams(vmem_limit_bytes=48 * 2**20),
        cost_estimate=pl.CostEstimate(flops=flops, bytes_accessed=nbytes, transcendentals=0),
    )


def arr(*shape):
    return jax.ShapeDtypeStruct(shape, f32)


def lookup(tables, index):
    lane = jnp.broadcast_to(index & (LANES - 1), (8, LANES))
    high = jnp.broadcast_to(index >> 7, (8, LANES))
    found = [jnp.take_along_axis(t, lane, axis=1, mode="promise_in_bounds") for t in tables]
    bit = 1
    while len(found) > 1:
        odd = (high & bit) != 0
        found = [
            jnp.where(odd, found[a + 1], found[a]) if a + 1 < len(found) else found[a]
            for a in range(0, len(found), 2)
        ]
        bit *= 2
    return found[0]


def tiles(ref, row, count):
    return [ref[row : row + 8, t * LANES : (t + 1) * LANES] for t in range(count)]


def gather_blocks(own, low, up, conn, out, groups):
    def body(j, carry):
        index = conn[pl.ds(j, 1), :]
        for q, g in enumerate(groups):
            tables = tiles(own, g * 8, OWN_T) + tiles(low, g * 8, GHOST_T) + tiles(up, g * 8, GHOST_T)
            out[j, q * 8 : q * 8 + 8, :] = lookup(tables, index)
        return carry

    lax.fori_loop(0, EB, body, 0, unroll=4)


def product(freq, got, stiff, mass, out, per_harm, wide):
    for h in range(2):
        weight = freq[h]

        def outer(jt, carry):
            def inner(i, sums):
                ks = []
                for q in range(wide):
                    rows = pl.ds(pl.multiple_of((jt * wide + q) * 8, 8), 8)
                    ks.append(stiff[i, rows, :] + weight * mass[i, rows, :])
                new = []
                for r in range(per_harm):
                    x = jnp.broadcast_to(got[i, pl.ds(h * per_harm + r, 1), :], (8, LANES))
                    for q in range(wide):
                        new.append(sums[r * wide + q] + ks[q] * x)
                return tuple(new)

            zero = jnp.zeros((8, LANES), f32)
            sums = lax.fori_loop(0, EB, inner, (zero,) * (per_harm * wide), unroll=4)
            for r in range(per_harm):
                for q in range(wide):
                    rows = pl.ds(pl.multiple_of((jt * wide + q) * 8, 8), 8)
                    out[h * per_harm + r, rows, :] = sums[r * wide + q]
            return carry

        lax.fori_loop(0, EB // (8 * wide), outer, 0)


def pieces(x):
    high = x.astype(bf16).astype(f32)
    return jnp.concatenate([high, x - high], axis=0).astype(bf16)


def one_hot_low(index):
    low = jnp.broadcast_to(index & 255, (256, LANES))
    return jnp.where(low == lax.broadcasted_iota(i32, (256, LANES), 0), 1.0, 0.0).astype(bf16)


def masked_stack(parts, index, count):
    high = index >> 8
    stack = []
    for t in range(count):
        mask = jnp.broadcast_to(jnp.where(high == t, 1.0, 0.0), parts.shape).astype(bf16)
        stack.append(parts * mask)
    return stack


def add_up(stack, hot):
    return lax.dot_general(stack, hot, (((1,), (1,)), ((), ())), preferred_element_type=f32)


def scatter_blocks(terms, conn, stack, hot, total):
    chunk = 16
    total[...] = jnp.zeros_like(total)

    def outer(c, carry):
        def body(jj, inner):
            j = c * chunk + jj
            index = conn[pl.ds(j, 1), :]
            cols = pl.ds(pl.multiple_of(jj * LANES, LANES), LANES)
            hot[:, cols] = one_hot_low(index)
            x = terms[:, pl.ds(j, 1), :].reshape(ROWS, LANES)
            for t, part in enumerate(masked_stack(pieces(x), index, 12)):
                stack[t * 48 : t * 48 + 48, cols] = part
            return inner

        lax.fori_loop(0, chunk, body, 0, unroll=2)
        total[...] += add_up(stack[...], hot[...])
        return carry

    lax.fori_loop(0, EB // chunk, outer, 0)


def total_tile(total, t):
    return total[t * 48 : t * 48 + 24, :] + total[t * 48 + 24 : t * 48 + 48, :]


def transposed_lists(rim):
    columns = jnp.transpose(rim[24:32, :])
    return columns[:, 4:5], columns[:, 5:6]


def finish(p, lists, rim_low, rim_up, my_low, my_up, from_low, from_up, far_low, far_up, own, low, up):
    arrived = jnp.concatenate([from_low[24:48, :], from_up[24:48, :]], axis=1)
    hots, stacks = [], []
    for c in range(2 * GHOST_T):
        index = lists[c // GHOST_T : c // GHOST_T + 1, (c % GHOST_T) * LANES : (c % GHOST_T + 1) * LANES]
        hots.append(one_hot_low(index))
        parts = pieces(arrived[:, c * LANES : (c + 1) * LANES])
        stacks.append(jnp.concatenate(masked_stack(parts, index, 8), axis=0))
    sums = add_up(jnp.concatenate(stacks, axis=1), jnp.concatenate(hots, axis=1))
    for t in range(8):
        own[0:24, t * 256 : (t + 1) * 256] = p[:, t * 256 : (t + 1) * 256] + total_tile(sums, t)

    for rim, row, first, second, sent, out in (
        (rim_low, 29, far_low[...], my_low[...], from_low, low),
        (rim_up, 28, my_up[...], far_up[...], from_up, up),
    ):
        listed = rim[row : row + 1, :]
        ghosts = sent[0:24, :]
        for column, values in zip(transposed_lists(rim), (first, second)):
            match = jnp.where(column == listed, 1.0, 0.0).astype(bf16)
            both = jnp.dot(pieces(values), match, preferred_element_type=f32)
            ghosts = ghosts + both[0:24] + both[24:48]
        out[0:24, :] = ghosts


def edge_weights(freq, rows, width):
    upper = lax.broadcasted_iota(i32, (rows, width), 0) < rows // 2
    return jnp.where(upper, freq[0], freq[1])


def partial_outputs(freq, own, mass_row, lists, total, p, to_low, to_up, far_to_low, far_to_up):
    weights = edge_weights(freq, ROWS, 256)
    for t in range(8):
        cols = slice(t * 256, (t + 1) * 256)
        p[:, cols] = total_tile(total, t) + weights * mass_row[0:1, cols] * own[0:24, cols]
    for t in range(2):
        cols = slice(t * 256, (t + 1) * 256)
        low, up = total_tile(total, 8 + t), total_tile(total, 10 + t)
        to_low[24:48, cols] = low
        far_to_low[:, cols] = low
        to_up[24:48, cols] = up
        far_to_up[:, cols] = up
    pick_listed(p, lists, (to_low, to_up), 3)


def pick_listed(source, lists, outs, groups):
    for side in range(2):
        for c in range(GHOST_T):
            cols = slice(c * LANES, (c + 1) * LANES)
            index = lists[side : side + 1, cols]
            for g in range(groups):
                value = lookup(tiles(source, g * 8, OWN_T), index)
                outs[side][g * 8 : g * 8 + 8, cols] = jnp.where(index >= 0, value, 0.0)


def fold(x):
    rows, cols = x.shape
    total = jnp.zeros((8, LANES), f32)
    for r in range(rows // 8):
        for c in range(cols // LANES):
            total = total + x[r * 8 : r * 8 + 8, c * LANES : (c + 1) * LANES]
    return total


def prep_kernel(rhs, field, lists, rows, to_low, to_up):
    for h in range(2):
        for o in range(6):
            at = h * 12 + o * 2
            rows[at : at + 2, :] = rhs[h, o]
        rows[24 + 2 * h : 26 + 2 * h, :] = field[h]
    rows[28:32, :] = jnp.zeros((4, EDGES), f32)
    pick_listed(rows, lists, (to_low, to_up), 4)
    for out in (to_low, to_up):
        out[28:30, :] = lists[...].astype(f32)


def first_kernel(
    freq, rows, low, up, conn, lists, stiff, mass, mass_row,
    p, to_low, to_up, far_to_low, far_to_up, got, terms, stack, hot, total,
):
    gather_blocks(rows, low, up, conn, got, (0, 1, 2))
    product(freq, got, stiff, mass, terms, 12, 2)
    scatter_blocks(terms, conn, stack, hot, total)
    partial_outputs(freq, rows, mass_row, lists, total, p, to_low, to_up, far_to_low, far_to_up)


def second_kernel(
    freq, rows, rim_low, rim_up, conn, lists, stiff, mass, mass_row,
    p, my_low, my_up, from_low, from_up, far_low, far_up,
    p2, to_low, to_up, far_to_low, far_to_up, got, own, moments, low, up, terms, stack, hot, total,
):
    finish(p, lists, rim_low, rim_up, my_low, my_up, from_low, from_up, far_low, far_up, own, low, up)
    b, w = rows[0:24, :], own[...]
    moments[0:8, :] = fold(b * b)
    moments[8:16, :] = fold(b * w)
    moments[16:24, :] = fold(w * w)
    gather_blocks(own, low, up, conn, got, (0, 1, 2))
    product(freq, got, stiff, mass, terms, 12, 2)
    scatter_blocks(terms, conn, stack, hot, total)
    partial_outputs(freq, own, mass_row, lists, total, p2, to_low, to_up, far_to_low, far_to_up)


def quadratic(freq, got, got_rows, stiff, mass):
    result = jnp.zeros((8, LANES), f32)
    for h in range(2):
        weight = freq[h]
        for jt in range(8):

            def inner(i, sums, scale=1.0):
                k = stiff[i, jt * 8 : jt * 8 + 8, :] + weight * mass[i, jt * 8 : jt * 8 + 8, :]
                return tuple(
                    s + k * jnp.broadcast_to(got[i, h * 12 + r : h * 12 + r + 1, :], (8, LANES))
                    for r, s in enumerate(sums)
                )

            zero = jnp.zeros((8, LANES), f32)
            sums = (zero,) * 12
            if jt < 7:
                sums = lax.fori_loop(jt * 8 + 8, EB, inner, sums, unroll=4)
                sums = tuple(s + s for s in sums)
            sums = lax.fori_loop(jt * 8, jt * 8 + 8, inner, sums, unroll=4)
            for r in range(12):
                mine = got_rows[pl.ds(jt * 8 * ROWS + h * 12 + r, 8, stride=ROWS), :]
                result = result + sums[r] * mine
    return result


def third_kernel(
    count, freq, rim_low, rim_up, conn, lists, stiff, mass, mass_row,
    p, my_low, my_up, from_low, from_up, far_low, far_up, w_ref, early,
    got_out, own, message, low, up, got,
):
    finish(p, lists, rim_low, rim_up, my_low, my_up, from_low, from_up, far_low, far_up, own, low, up)
    gather_blocks(own, low, up, conn, got, (0, 1, 2))
    got_rows = got_out
    for j in range(EB):
        got_rows[j * ROWS : (j + 1) * ROWS, :] = got[j]
    w, v = w_ref[...], own[...]
    last = quadratic(freq, got, got_rows, stiff, mass)
    weights = edge_weights(freq, ROWS, 256)
    for t in range(8):
        cols = slice(t * 256, (t + 1) * 256)
        last = last + fold(weights * mass_row[0:1, cols] * v[:, cols] * v[:, cols])
    tiles_of = [early[0:8, :], early[8:16, :], early[16:24, :], fold(w * v), fold(v * v), last]
    lane = lax.broadcasted_iota(i32, (1, LANES), 1)
    line = jnp.zeros((1, LANES), f32)
    for k, tile in enumerate(tiles_of):
        line = line + jnp.where(lane == k, jnp.sum(tile), 0.0)
    message[...] = jnp.broadcast_to(line, (count, LANES))


def field_kernel(freq, rows, low, up, conn, stiff, mass, y, got):
    gather_blocks(rows, low, up, conn, got, (3,))
    product(freq, got, stiff, mass, y, 2, 4)


def gradients(got_rows, y, node_block, node_shape, energy, out, base):
    for jt in range(8):
        ys = [y[r, jt * 8 : jt * 8 + 8, :] for r in range(4)]
        for o in range(6):
            term = jnp.zeros((8, LANES), f32)
            for h in range(2):
                for c in range(2):
                    x = got_rows[pl.ds(jt * 8 * ROWS + h * 12 + o * 2 + c, 8, stride=ROWS), :]
                    term = term - x * ys[h * 2 + c] if c else term + x * ys[h * 2 + c]
            energy[o, jt * 8 : jt * 8 + 8, :] = term

    def body(c, carry):
        index = jnp.broadcast_to(node_block[pl.ds(c, 1), :], (8, LANES))
        cols = pl.ds(pl.multiple_of(c * LANES, LANES), LANES)
        sums = [jnp.zeros((8, LANES), f32) for _ in range(18)]
        for jt in range(8):
            shape = [node_shape[k, jt * 8 : jt * 8 + 8, cols] for k in range(3)]
            for o in range(6):
                x = jnp.take_along_axis(energy[o, jt * 8 : jt * 8 + 8, :], index, axis=1, mode="promise_in_bounds")
                for k in range(3):
                    sums[o * 3 + k] = sums[o * 3 + k] - shape[k] * x
        for q in range(18):
            out[c, base + q : base + q + 1, :] = jnp.sum(sums[q], axis=0, keepdims=True)
        return carry

    lax.fori_loop(0, 8, body, 0)


def early_gradient_kernel(got0, got1, y, node_block, node_shape, out, energy):
    gradients(got0, y, node_block, node_shape, energy, out, 0)
    gradients(got1, y, node_block, node_shape, energy, out, 18)
    out[:, 36:40, :] = jnp.zeros((8, 4, LANES), f32)


def late_gradient_kernel(early, got2, y, node_block, node_shape, out, energy):
    out[:, 0:40, :] = early[...]
    gradients(got2, y, node_block, node_shape, energy, out, 40)
    out[:, 58:64, :] = jnp.zeros((8, 6, LANES), f32)


def last_kernel(messages, rows, w, v, shares, adjoint, gradient):
    line = jnp.sum(messages[...], axis=0, keepdims=True)
    lane = lax.broadcasted_iota(i32, (1, LANES), 1)

    def moment(k):
        return jnp.sum(jnp.where(lane == k, line, 0.0), axis=1, keepdims=True)

    m = [moment(k) for k in range(6)]
    a0 = m[0] / m[1]
    r1 = (None, -a0)
    rr1 = m[0] - 2.0 * a0 * m[1] + a0 * a0 * m[2]
    b0 = rr1 / m[0]
    d1 = (1.0 + b0, -a0)
    dad1 = d1[0] * d1[0] * m[1] + 2.0 * d1[0] * d1[1] * m[2] + d1[1] * d1[1] * m[3]
    a1 = rr1 / dad1
    r2 = (None, r1[1] - a1 * d1[0], -a1 * d1[1])
    rr2 = (
        m[0] + 2.0 * r2[1] * m[1] + (2.0 * r2[2] + r2[1] * r2[1]) * m[2]
        + 2.0 * r2[1] * r2[2] * m[3] + r2[2] * r2[2] * m[4]
    )
    b1 = rr2 / rr1
    d2 = (1.0 + b1 * d1[0], r2[1] + b1 * d1[1], r2[2])
    dad2 = (
        d2[0] * d2[0] * m[1] + 2.0 * d2[0] * d2[1] * m[2] + (2.0 * d2[0] * d2[2] + d2[1] * d2[1]) * m[3]
        + 2.0 * d2[1] * d2[2] * m[4] + d2[2] * d2[2] * m[5]
    )
    a2 = rr2 / dad2
    c0 = a0 + a1 * d1[0] + a2 * d2[0]
    c1 = a1 * d1[1] + a2 * d2[1]
    c2 = a2 * d2[2]
    for h in range(2):
        for o in range(6):
            at = slice(h * 12 + o * 2, h * 12 + o * 2 + 2)
            adjoint[h, o] = c0 * rows[at, :] + c1 * w[at, :] + c2 * v[at, :]
    share = shares[0]
    for d in range(1, 8):
        share = share + shares[d]
    for o in range(6):
        gradient[o] = (
            c0 * share[o * 3 : o * 3 + 3] + c1 * share[18 + o * 3 : 21 + o * 3] + c2 * share[40 + o * 3 : 43 + o * 3]
        )


def shifted(x, by):
    count = lax.axis_size("mesh")
    return lax.ppermute(x, "mesh", [(i, i + by) for i in range(count) if 0 <= i + by < count])


def per_device(
    adjoint_rhs, forward_field, stiffness, mass_blocks, frequency, edge_mass, connectivity, send_list, node_block, node_shape
):
    lists = send_list[0]
    mass_row = edge_mass.reshape(1, EDGES)
    nodes = node_block.reshape(8, LANES)
    count = lax.axis_size("mesh") * lax.axis_size("harm")
    block_scratch = [
        pltpu.VMEM((ROWS, EB, LANES), f32),
        pltpu.VMEM((12 * 48, 16 * LANES), bf16),
        pltpu.VMEM((256, 16 * LANES), bf16),
        pltpu.VMEM((12 * 48, 256), f32),
    ]
    ghost = pltpu.VMEM((ROWS, SLOTS), f32)

    rows, to_low, to_up = kernel_call(
        prep_kernel, "prep", (arr(32, EDGES), arr(32, SLOTS), arr(32, SLOTS)), [VMEM] * 3, flops=10**6, nbytes=10**6
    )(adjoint_rhs, forward_field, lists)
    rim_low, rim_up = shifted(to_up, 1), shifted(to_low, -1)

    sums = (arr(ROWS, EDGES), arr(48, SLOTS), arr(48, SLOTS), arr(ROWS, SLOTS), arr(ROWS, SLOTS))
    p, to_low, to_up, far_to_low, far_to_up, got0 = kernel_call(
        first_kernel, "first", sums + (arr(EB, ROWS, LANES),), [SMEM] + [VMEM] * 8, block_scratch,
        flops=10**8, nbytes=10**7,
    )(frequency, rows, rim_low, rim_up, connectivity, lists, stiffness, mass_blocks, mass_row)

    def exchange():
        return (
            far_to_low, far_to_up, shifted(to_up, 1), shifted(to_low, -1), shifted(far_to_up, 2), shifted(far_to_low, -2)
        )

    arrived = exchange()
    (y,) = kernel_call(
        field_kernel, "field", (arr(4, EB, LANES),), [SMEM] + [VMEM] * 6, [pltpu.VMEM((EB, 8, LANES), f32)],
        flops=10**8, nbytes=10**7,
    )(frequency, rows, rim_low, rim_up, connectivity, stiffness, mass_blocks)

    p, to_low, to_up, far_to_low, far_to_up, got1, w, early = kernel_call(
        second_kernel, "second", sums + (arr(EB, ROWS, LANES), arr(ROWS, EDGES), arr(24, LANES)),
        [SMEM] + [VMEM] * 15, [ghost, ghost] + block_scratch, flops=10**8, nbytes=10**7,
    )(
        frequency, rows, rim_low, rim_up, connectivity, lists, stiffness, mass_blocks, mass_row, p, *arrived
    )

    arrived = exchange()
    flat = lambda x: x.reshape(EB * ROWS, LANES)
    (grads,) = kernel_call(
        early_gradient_kernel, "early_gradient", (arr(8, 40, LANES),), [VMEM] * 5, [pltpu.VMEM((6, EB, LANES), f32)],
        flops=10**8, nbytes=10**7,
    )(flat(got0), flat(got1), y, nodes, node_shape)

    got2, v, message = kernel_call(
        functools.partial(third_kernel, count), "third", (arr(EB * ROWS, LANES), arr(ROWS, EDGES), arr(count, LANES)),
        [SMEM] + [VMEM] * 16, [ghost, ghost, pltpu.VMEM((EB, ROWS, LANES), f32)], flops=10**8, nbytes=10**7,
    )(
        frequency, rim_low, rim_up, connectivity, lists, stiffness, mass_blocks, mass_row, p, *arrived, w, early
    )
    messages = lax.all_to_all(message, BOTH, 0, 0, tiled=True)
    (grads,) = kernel_call(
        late_gradient_kernel, "late_gradient", (arr(8, 64, LANES),), [VMEM] * 5, [pltpu.VMEM((6, EB, LANES), f32)],
        flops=10**8, nbytes=10**7,
    )(grads, got2, y, nodes, node_shape)
    shares = lax.all_to_all(grads, "harm", 0, 0, tiled=True)
    adjoint, gradient = kernel_call(
        last_kernel, "last", (arr(*adjoint_rhs.shape), arr(6, 3, LANES)), [VMEM] * 5, flops=10**6, nbytes=10**6
    )(messages, rows, w, v, shares)
    return adjoint, gradient


def solution(mesh):
    return jax.shard_map(
        per_device,
        mesh=mesh,
        in_specs=(
            P("harm", None, None, "mesh"),
            P("harm", None, "mesh"),
            P(None, None, "mesh"),
            P(None, None, "mesh"),
            P("harm"),
            P("mesh"),
            P(None, "mesh"),
            P("mesh", None, None),
            P("mesh"),
            P(None, None, "mesh"),
        ),
        out_specs=(P("harm", None, None, "mesh"), P(None, None, ("mesh", "harm"))),
        check_vma=False,
    )
```

time: 1020 us -> 155 us (0.15)
  blocking collectives: 368 us -> 30.8 us
  local copies, waits for them, and re-layouts: 225 us -> 7.68 us
  other arithmetic: 180 us -> 0 us
  waiting for transfers between devices: 85.5 us -> 3.63 us
  matrix products: 73.3 us -> 0 us
  Pallas kernels: 0 us -> 66 us
  between operations: 21.8 us -> 0.88 us
  starting transfers between devices: 55.7 us -> 43.7 us
    psum x5 -> x0, blocking collectives: 368 us -> none  [the longest x3 222 us: squares(): return lax.psum(jnp.sum(values_now * values_now), ('mesh', 'harm'))]
    gather x19 -> x0, local copies, waits for them, and re-layouts: 181 us -> none  [the longest x8 126 us: assemble(): gathered = extended[:, connectivity]]
    scatter-add x9 -> x0, other arithmetic: 170 us -> none  [the longest x3 135 us: per_device(): totals.at[:, connectivity.reshape(-1)]]
    dot_general x9 -> x0, matrix products: 73.3 us -> none  [the longest x8 63.2 us: block_product(): return jnp.einsum('ijb,rjb->rib', matrices, gathered, precision=exact_mode)]
    psum x1 -> x0, waiting for transfers between devices: 67.8 us -> none  [per_device(): summed = lax.psum(local_grad, 'harm')]
    pallas_call x0 -> x8, Pallas kernels: none -> 66 us  [the longest x1 23.1 us: per_device(): kernel_call(second_kernel, 'second', sums + (arr(EB, ROWS, LANES), arr(RO...]
    all_to_all x0 -> x2, blocking collectives: none -> 30.8 us  [the longest x1 19 us: per_device(): messages = lax.all_to_all(message, BOTH, 0, 0, tiled=True)]
    ppermute x14 -> x10, waiting for transfers between devices: 17.7 us -> 3.63 us  [shifted(): lax.ppermute(x, 'mesh', [(i, i + by) for i in range(count) if 0 <= i + by...]
  transfers between devices with their start and end apart: 15 -> 10, of which waited for: 12 -> 4; matrix products, arithmetic and copies ran while one was open for 3% -> 0% of each run, Pallas kernels for 0% -> 5%
where the time goes in v1:
time: 155 us; the launch traced here: 153 us
  Pallas kernels  66 us (43%)
  starting transfers between devices  43.7 us (28%)
  blocking collectives  30.8 us (20%)
  local copies, waits for them, and re-layouts  7.68 us (5%)
  waiting for transfers between devices  3.63 us (2%)
    ppermute x10, starting transfers between devices, shifted(): lax.ppermute(x, 'mesh', [(i, i + by) for i in range(count) if 0 <= i + by...  43.7 us
    pallas_call x1, Pallas kernels, per_device(): kernel_call(second_kernel, 'second', sums + (arr(EB, ROWS, LANES), arr(RO...  23.1 us
    pallas_call x1, Pallas kernels, per_device(): kernel_call(first_kernel, 'first', sums + (arr(EB, ROWS, LANES),), [SMEM]...  20.5 us
    all_to_all x1, blocking collectives, per_device(): messages = lax.all_to_all(message, BOTH, 0, 0, tiled=True)  19 us
    pallas_call x1, Pallas kernels, per_device(): kernel_call(functools.partial(third_kernel, count), 'third', (arr(EB * RO...  12.1 us
    all_to_all x1, blocking collectives, per_device(): shares = lax.all_to_all(grads, 'harm', 0, 0, tiled=True)  11.8 us
    unnamed x26, local copies, waits for them, and re-layouts  7.68 us
    pallas_call x1, Pallas kernels, per_device(): kernel_call(field_kernel, 'field', (arr(4, EB, LANES),), [SMEM] + [VMEM]...  4.69 us
  transfers between devices with their start and end apart: 10, of which 4 were waited for; matrix products, arithmetic and copies ran while one was open for 0% of the time, Pallas kernels for 5%

profile of v1, /device:TPU:2, one launch (start us, length us, event | category | flops | bytes accessed | tf_op | source)
XLA Modules:
  0.0 152.6 jit_solution(3130866785851604749)
XLA Ops:
  0.6 0.9 copy-done.6
  1.6 0.7 copy-done.8
  2.2 0.8 copy-done.9
  3.0 0.7 prep.1
  3.7 3.8 %collective-permute-start = (f32[32,512]{1,0:T(8,128)S(1)}, f32[32,512]{1,0:T(8,128)S(1)}, u32[]{:S(2)}, u32[]{:S(2)}) collective-permute-start(f32[32,512]{1,0:T(8,128)S(1)} %get-tuple-element.22), channel_id=1, source_target_pairs={{0,8},{8,16},{16,24},{24,32},{32,40},{40,48},{48,56},{56,64},{64,7... | collective-permute-start | bytes 196616 | tf_op jit(solution)/shard_map/ppermute | solution.py:395
  7.5 5.8 %collective-permute-start.1 = (f32[32,512]{1,0:T(8,128)S(1)}, f32[32,512]{1,0:T(8,128)S(1)}, u32[]{:S(2)}, u32[]{:S(2)}) collective-permute-start(f32[32,512]{1,0:T(8,128)S(1)} %get-tuple-element.23), channel_id=1, source_target_pairs={{8,0},{16,8},{24,16},{32,24},{40,32},{48,40},{56,48},{64,56},{72,6... | collective-permute-start | bytes 196616 | tf_op jit(solution)/shard_map/ppermute | solution.py:395
  13.3 0.3 collective-permute-done.low.rim_low
  13.7 1.6 %collective-permute-done.1.up.rim_up = f32[32,512]{1,0:T(8,128)S(1)} collective-permute-done((f32[32,512]{1,0:T(8,128)S(1)}, f32[32,512]{1,0:T(8,128)S(1)}, u32[]{:S(2)}, u32[]{:S(2)}) %collective-permute-start.1) | collective-permute-done | bytes 65568 | tf_op jit(solution)/shard_map/ppermute | solution.py:395
  15.2 1.6 %copy-done = f32[64,64,128]{2,1,0:T(8,128)S(1)} copy-done((f32[64,64,128]{2,1,0:T(8,128)S(1)}, f32[64,64,128]{2,1,0:T(8,128)}, u32[]{:S(2)}) %copy-start) | copy-done | bytes 2097176
  16.8 1.6 %copy-done.2 = f32[64,64,128]{2,1,0:T(8,128)S(1)} copy-done((f32[64,64,128]{2,1,0:T(8,128)S(1)}, f32[64,64,128]{2,1,0:T(8,128)}, u32[]{:S(2)}) %copy-start.2) | copy-done | bytes 2097176
  18.4 0.8 copy-done.5
  19.2 0.7 copy-done.7
  19.9 0.7 copy-done.11
  20.5 20.5 %first.1 = (f32[24,2048]{1,0:T(8,128)S(1)}, f32[48,512]{1,0:T(8,128)S(1)}, f32[48,512]{1,0:T(8,128)S(1)}, f32[24,512]{1,0:T(8,128)S(1)}, f32[24,512]{1,0:T(8,128)S(1)}, /*index=5*/f32[64,24,128]{2,1,0:T(8,128)S(1)}) custom-call(f32[2]{0:T(128)S(1)} %copy-done.11, f32[32,2048]{1,0:T(8,128)S(1)} %get-tuple-element.24.rows, ...), custom_call_target="tpu_custom_call" | custom-call | flops 100000000 | bytes 10000000 | tf_op jit(solution)/shard_map/first/pallas_call | solution.py:419
  41.1 2.3 %collective-permute-start.2 = (f32[48,512]{1,0:T(8,128)S(1)}, f32[48,512]{1,0:T(8,128)S(1)}, u32[]{:S(2)}, u32[]{:S(2)}) collective-permute-start(f32[48,512]{1,0:T(8,128)S(1)} %get-tuple-element.28), channel_id=1, source_target_pairs={{0,8},{8,16},{16,24},{24,32},{32,40},{40,48},{48,56},{56,64},{64,7... | collective-permute-start | bytes 294920 | tf_op jit(solution)/shard_map/ppermute | solution.py:395
  43.3 6.0 %collective-permute-start.3 = (f32[48,512]{1,0:T(8,128)S(1)}, f32[48,512]{1,0:T(8,128)S(1)}, u32[]{:S(2)}, u32[]{:S(2)}) collective-permute-start(f32[48,512]{1,0:T(8,128)S(1)} %get-tuple-element.29), channel_id=1, source_target_pairs={{8,0},{16,8},{24,16},{32,24},{40,32},{48,40},{56,48},{64,56},{72,6... | collective-permute-start | bytes 294920 | tf_op jit(solution)/shard_map/ppermute | solution.py:395
  49.4 3.5 %collective-permute-start.4 = (f32[24,512]{1,0:T(8,128)S(1)}, f32[24,512]{1,0:T(8,128)S(1)}, u32[]{:S(2)}, u32[]{:S(2)}) collective-permute-start(f32[24,512]{1,0:T(8,128)S(1)} %get-tuple-element.27.my_up), channel_id=1, source_target_pairs={{0,16},{8,24},{16,32},{24,40},{32,48},{40,56},{48,64},{56,72},{64,... | collective-permute-start | bytes 147464 | tf_op jit(solution)/shard_map/ppermute | solution.py:395
  52.9 5.4 %collective-permute-start.5 = (f32[24,512]{1,0:T(8,128)S(1)}, f32[24,512]{1,0:T(8,128)S(1)}, u32[]{:S(2)}, u32[]{:S(2)}) collective-permute-start(f32[24,512]{1,0:T(8,128)S(1)} %get-tuple-element.26.my_low), channel_id=1, source_target_pairs={{16,0},{24,8},{32,16},{40,24},{48,32},{56,40},{64,48},{72,56},{80,... | collective-permute-start | bytes 147464 | tf_op jit(solution)/shard_map/ppermute | solution.py:395
  58.2 0.1 collective-permute-done.4.far_low
  58.4 1.6 %collective-permute-done.5.far_up = f32[24,512]{1,0:T(8,128)S(1)} collective-permute-done((f32[24,512]{1,0:T(8,128)S(1)}, f32[24,512]{1,0:T(8,128)S(1)}, u32[]{:S(2)}, u32[]{:S(2)}) %collective-permute-start.5) | collective-permute-done | bytes 49184 | tf_op jit(solution)/shard_map/ppermute | solution.py:395
  60.0 23.1 %second.1 = (f32[24,2048]{1,0:T(8,128)S(1)}, f32[48,512]{1,0:T(8,128)S(1)}, f32[48,512]{1,0:T(8,128)S(1)}, f32[24,512]{1,0:T(8,128)S(1)}, f32[24,512]{1,0:T(8,12...) custom-call(f32[2]{0:T(128)S(1)} %copy-done.11, ...), custom_call_target="tpu_custom_call" | custom-call | flops 100000000 | bytes 10000000 | tf_op jit(solution)/shard_map/second/pallas_call | solution.py:435
  83.1 3.7 %collective-permute-start.6 = (f32[48,512]{1,0:T(8,128)S(1)}, f32[48,512]{1,0:T(8,128)S(1)}, u32[]{:S(2)}, u32[]{:S(2)}) collective-permute-start(f32[48,512]{1,0:T(8,128)S(1)} %get-tuple-element.33), channel_id=1, source_target_pairs={{0,8},{8,16},{16,24},{24,32},{32,40},{40,48},{48,56},{56,64},{64,7... | collective-permute-start | bytes 294920 | tf_op jit(solution)/shard_map/ppermute | solution.py:395
  86.8 4.2 %collective-permute-start.7 = (f32[48,512]{1,0:T(8,128)S(1)}, f32[48,512]{1,0:T(8,128)S(1)}, u32[]{:S(2)}, u32[]{:S(2)}) collective-permute-start(f32[48,512]{1,0:T(8,128)S(1)} %get-tuple-element.34), channel_id=1, source_target_pairs={{8,0},{16,8},{24,16},{32,24},{40,32},{48,40},{56,48},{64,56},{72,6... | collective-permute-start | bytes 294920 | tf_op jit(solution)/shard_map/ppermute | solution.py:395
  91.1 3.6 %collective-permute-start.8 = (f32[24,512]{1,0:T(8,128)S(1)}, f32[24,512]{1,0:T(8,128)S(1)}, u32[]{:S(2)}, u32[]{:S(2)}) collective-permute-start(f32[24,512]{1,0:T(8,128)S(1)} %get-tuple-element.32.my_up), channel_id=1, source_target_pairs={{0,16},{8,24},{16,32},{24,40},{32,48},{40,56},{48,64},{56,72},{64,... | collective-permute-start | bytes 147464 | tf_op jit(solution)/shard_map/ppermute | solution.py:395
  94.7 5.4 %collective-permute-start.9 = (f32[24,512]{1,0:T(8,128)S(1)}, f32[24,512]{1,0:T(8,128)S(1)}, u32[]{:S(2)}, u32[]{:S(2)}) collective-permute-start(f32[24,512]{1,0:T(8,128)S(1)} %get-tuple-element.31.my_low), channel_id=1, source_target_pairs={{16,0},{24,8},{32,16},{40,24},{48,32},{56,40},{64,48},{72,56},{80,... | collective-permute-start | bytes 147464 | tf_op jit(solution)/shard_map/ppermute | solution.py:395
  100.1 4.7 %field.3.y = f32[4,64,128]{2,1,0:T(8,128)S(1)} custom-call(f32[2]{0:T(128)S(1)} %copy-done.12, f32[32,2048]{1,0:T(8,128)S(1)} %get-tuple-element.24.rows, f32[32,512]{1,0:T(8,128)S(1)} %collective-permute-done.low.rim_low, f32[32,512]{1,0:T(8,128)S(1)} %collective-permute-done.1.up.rim_up, s32[64,128]{1,0:T(8,128)S(1)} %copy-done.5, ...), custom_call_target="tpu_custom_call" | custom-call | flops 100000000 | bytes 10000000 | tf_op jit(solution)/shard_map/field/pallas_call | solution.py:430
  104.8 2.5 %early_gradient.1.early = f32[8,40,128]{2,1,0:T(8,128)S(1)} custom-call(f32[1536,128]{1,0:T(8,128)S(1)} %bitcast.9, f32[1536,128]{1,0:T(8,128)S(1)} %bitcast.10, f32[4,64,128]{2,1,0:T(8,128)S(1)} %field.3.y, s32[8,128]{1,0:T(8,128)S(1)} %bitcast.20, f32[3,64,1024]{2,1,0:T(8,128)S(1)} %copy-done.4), custom_call_target="tpu_custom_call" | custom-call | flops 100000000 | bytes 10000000 | tf_op jit(solution)/shard_map/early_gradient/pallas_call | solution.py:444
  107.4 12.1 %third.1 = (f32[1536,128]{1,0:T(8,128)S(1)}, f32[24,2048]{1,0:T(8,128)S(1)}, f32[256,128]{1,0:T(8,128)S(1)}) custom-call(f32[2]{0:T(128)S(1)} %copy-done.12, f32[32,512]{1,0:T(8,128)S(1)} %collective-permute-done.low.rim_low, f32[32,512]{1,0:T(8,128)S(1)} %collective-permute-done.1.up.rim_up, s32[64,128]{1,0:T(8,128)S(1)} %copy-done.5, ...), custom_call_target="tpu_custom_call" | custom-call | flops 100000000 | bytes 10000000 | tf_op jit(solution)/shard_map/third/pallas_call | solution.py:449
  119.6 1.3 late_gradient.1
  120.9 11.8 %all_to_all.16.shares = f32[8,64,128]{2,1,0:T(8,128)S(1)} all-to-all(f32[8,64,128]{2,1,0:T(8,128)S(1)} %late_gradient.1), channel_id=1, replica_groups=mesh['mesh'=32,'harm'=8] {'harm'}, dimensions={0} | all-to-all | bytes 524288 | tf_op jit(solution)/shard_map/all_to_all | solution.py:460
  132.7 19.0 %all_to_all.17 = f32[256,1,128]{2,1,0:T(1,128)S(1)} all-to-all(f32[256,1,128]{2,1,0:T(1,128)S(1)} %bitcast.12), channel_id=1, replica_groups=mesh['mesh'=32,'harm'=8] {'mesh','harm'}, dimensions={0} | all-to-all | bytes 262144 | tf_op jit(solution)/shard_map/all_to_all | solution.py:455
  151.6 1.0 last.1
  (24 shorter events, 0.1 us)
Async XLA Ops:
  0.6 0.9 copy-start.6
  1.6 0.7 copy-start.8
  2.2 0.8 copy-start.9
  3.7 10.0 %collective-permute-start = (f32[32,512]{1,0:T(8,128)S(1)}, f32[32,512]{1,0:T(8,128)S(1)}, u32[]{:S(2)}, u32[]{:S(2)}) collective-permute-start(f32[32,512]{1,0:T(8,128)S(1)} %get-tuple-element.22), channel_id=1, source_target_pairs={{0,8},{8,16},{16,24},{24,32},{32,40},{40,48},{48,56},{56,64},{64,7... | collective-permute-start | bytes 196616 | tf_op jit(solution)/shard_map/ppermute | solution.py:395
  7.5 7.7 %collective-permute-start.1 = (f32[32,512]{1,0:T(8,128)S(1)}, f32[32,512]{1,0:T(8,128)S(1)}, u32[]{:S(2)}, u32[]{:S(2)}) collective-permute-start(f32[32,512]{1,0:T(8,128)S(1)} %get-tuple-element.23), channel_id=1, source_target_pairs={{8,0},{16,8},{24,16},{32,24},{40,32},{48,40},{56,48},{64,56},{72,6... | collective-permute-start | bytes 196616 | tf_op jit(solution)/shard_map/ppermute | solution.py:395
  15.2 1.6 %copy-start = (f32[64,64,128]{2,1,0:T(8,128)S(1)}, f32[64,64,128]{2,1,0:T(8,128)}, u32[]{:S(2)}) copy-start(f32[64,64,128]{2,1,0:T(8,128)} %stiff.7) | copy-start | bytes 6291460
  16.8 1.6 %copy-start.2 = (f32[64,64,128]{2,1,0:T(8,128)S(1)}, f32[64,64,128]{2,1,0:T(8,128)}, u32[]{:S(2)}) copy-start(f32[64,64,128]{2,1,0:T(8,128)} %mass.7) | copy-start | bytes 6291460
  18.4 0.8 copy-start.5
  19.2 0.7 copy-start.7
  19.9 0.7 copy-start.11
  41.1 18.9 %collective-permute-start.2 = (f32[48,512]{1,0:T(8,128)S(1)}, f32[48,512]{1,0:T(8,128)S(1)}, u32[]{:S(2)}, u32[]{:S(2)}) collective-permute-start(f32[48,512]{1,0:T(8,128)S(1)} %get-tuple-element.28), channel_id=1, source_target_pairs={{0,8},{8,16},{16,24},{24,32},{32,40},{40,48},{48,56},{56,64},{64,7... | collective-permute-start | bytes 294920 | tf_op jit(solution)/shard_map/ppermute | solution.py:395
  43.3 16.6 %collective-permute-start.3 = (f32[48,512]{1,0:T(8,128)S(1)}, f32[48,512]{1,0:T(8,128)S(1)}, u32[]{:S(2)}, u32[]{:S(2)}) collective-permute-start(f32[48,512]{1,0:T(8,128)S(1)} %get-tuple-element.29), channel_id=1, source_target_pairs={{8,0},{16,8},{24,16},{32,24},{40,32},{48,40},{56,48},{64,56},{72,6... | collective-permute-start | bytes 294920 | tf_op jit(solution)/shard_map/ppermute | solution.py:395
  49.4 9.0 %collective-permute-start.4 = (f32[24,512]{1,0:T(8,128)S(1)}, f32[24,512]{1,0:T(8,128)S(1)}, u32[]{:S(2)}, u32[]{:S(2)}) collective-permute-start(f32[24,512]{1,0:T(8,128)S(1)} %get-tuple-element.27.my_up), channel_id=1, source_target_pairs={{0,16},{8,24},{16,32},{24,40},{32,48},{40,56},{48,64},{56,72},{64,... | collective-permute-start | bytes 147464 | tf_op jit(solution)/shard_map/ppermute | solution.py:395
  52.9 7.1 %collective-permute-start.5 = (f32[24,512]{1,0:T(8,128)S(1)}, f32[24,512]{1,0:T(8,128)S(1)}, u32[]{:S(2)}, u32[]{:S(2)}) collective-permute-start(f32[24,512]{1,0:T(8,128)S(1)} %get-tuple-element.26.my_low), channel_id=1, source_target_pairs={{16,0},{24,8},{32,16},{40,24},{48,32},{56,40},{64,48},{72,56},{80,... | collective-permute-start | bytes 147464 | tf_op jit(solution)/shard_map/ppermute | solution.py:395
  60.0 40.1 %copy-start.1 = (f32[64,64,128]{2,1,0:T(8,128)S(1)}, f32[64,64,128]{2,1,0:T(8,128)}, u32[]{:S(2)}) copy-start(f32[64,64,128]{2,1,0:T(8,128)} %stiff.7) | copy-start | bytes 6291460
  60.0 40.1 %copy-start.3 = (f32[64,64,128]{2,1,0:T(8,128)S(1)}, f32[64,64,128]{2,1,0:T(8,128)}, u32[]{:S(2)}) copy-start(f32[64,64,128]{2,1,0:T(8,128)} %mass.7) | copy-start | bytes 6291460
  60.0 40.1 %copy-start.12 = (f32[2]{0:T(128)S(1)}, f32[2]{0:T(128)}, u32[]{:S(2)}) copy-start(f32[2]{0:T(128)} %freq.7) | copy-start | bytes 28
  83.1 24.3 %collective-permute-start.6 = (f32[48,512]{1,0:T(8,128)S(1)}, f32[48,512]{1,0:T(8,128)S(1)}, u32[]{:S(2)}, u32[]{:S(2)}) collective-permute-start(f32[48,512]{1,0:T(8,128)S(1)} %get-tuple-element.33), channel_id=1, source_target_pairs={{0,8},{8,16},{16,24},{24,32},{32,40},{40,48},{48,56},{56,64},{64,7... | collective-permute-start | bytes 294920 | tf_op jit(solution)/shard_map/ppermute | solution.py:395
  86.8 20.6 %collective-permute-start.7 = (f32[48,512]{1,0:T(8,128)S(1)}, f32[48,512]{1,0:T(8,128)S(1)}, u32[]{:S(2)}, u32[]{:S(2)}) collective-permute-start(f32[48,512]{1,0:T(8,128)S(1)} %get-tuple-element.34), channel_id=1, source_target_pairs={{8,0},{16,8},{24,16},{32,24},{40,32},{48,40},{56,48},{64,56},{72,6... | collective-permute-start | bytes 294920 | tf_op jit(solution)/shard_map/ppermute | solution.py:395
  91.1 16.3 %collective-permute-start.8 = (f32[24,512]{1,0:T(8,128)S(1)}, f32[24,512]{1,0:T(8,128)S(1)}, u32[]{:S(2)}, u32[]{:S(2)}) collective-permute-start(f32[24,512]{1,0:T(8,128)S(1)} %get-tuple-element.32.my_up), channel_id=1, source_target_pairs={{0,16},{8,24},{16,32},{24,40},{32,48},{40,56},{48,64},{56,72},{64,... | collective-permute-start | bytes 147464 | tf_op jit(solution)/shard_map/ppermute | solution.py:395
  94.6 10.2 %copy-start.4 = (f32[3,64,1024]{2,1,0:T(8,128)S(1)}, f32[3,64,1024]{2,1,0:T(8,128)}, u32[]{:S(2)}) copy-start(f32[3,64,1024]{2,1,0:T(8,128)} %node_shape.3) | copy-start | bytes 2359300
  94.7 10.2 %copy-start.10 = (s32[1024]{0:T(1024)S(1)}, s32[1024]{0:T(1024)}, u32[]{:S(2)}) copy-start(s32[1024]{0:T(1024)} %param.18) | copy-start | bytes 12292
  94.7 12.7 %collective-permute-start.9 = (f32[24,512]{1,0:T(8,128)S(1)}, f32[24,512]{1,0:T(8,128)S(1)}, u32[]{:S(2)}, u32[]{:S(2)}) collective-permute-start(f32[24,512]{1,0:T(8,128)S(1)} %get-tuple-element.31.my_low), channel_id=1, source_target_pairs={{16,0},{24,8},{32,16},{40,24},{48,32},{56,40},{64,48},{72,56},{80,... | collective-permute-start | bytes 147464 | tf_op jit(solution)/shard_map/ppermute | solution.py:395

commit v2 on v1

v2 whole, which is shorter than its diff:
```python
import functools

import jax
import jax.numpy as jnp
from jax import lax
from jax.experimental import pallas as pl
from jax.experimental.pallas import tpu as pltpu
from jax.sharding import PartitionSpec as P

f32 = jnp.float32
bf16 = jnp.bfloat16
i32 = jnp.int32
LANES = 128
EDGES = 2048
SLOTS = 512
ROWS = 24
EB = 64
OWN_T, GHOST_T = EDGES // LANES, SLOTS // LANES
BOTH = ("mesh", "harm")

VMEM = pl.BlockSpec(memory_space=pltpu.VMEM)
SMEM = pl.BlockSpec(memory_space=pltpu.SMEM)


def kernel_call(body, name, out, specs, scratch=(), flops=0, nbytes=0):
    return pl.pallas_call(
        body,
        name=name,
        out_shape=out,
        in_specs=specs,
        out_specs=jax.tree.map(lambda _: VMEM, out),
        scratch_shapes=scratch,
        compiler_params=pltpu.CompilerParams(vmem_limit_bytes=20 * 2**20),
        cost_estimate=pl.CostEstimate(flops=flops, bytes_accessed=nbytes, transcendentals=0),
    )


def arr(*shape):
    return jax.ShapeDtypeStruct(shape, f32)


def lookup(tables, index):
    lane = jnp.broadcast_to(index & (LANES - 1), (8, LANES))
    high = jnp.broadcast_to(index >> 7, (8, LANES))
    found = [jnp.take_along_axis(t, lane, axis=1, mode="promise_in_bounds") for t in tables]
    bit = 1
    while len(found) > 1:
        odd = (high & bit) != 0
        found = [
            jnp.where(odd, found[a + 1], found[a]) if a + 1 < len(found) else found[a]
            for a in range(0, len(found), 2)
        ]
        bit *= 2
    return found[0]


def tiles(ref, row, count):
    return [ref[row : row + 8, t * LANES : (t + 1) * LANES] for t in range(count)]


def gather_own(own, conn, out, groups):
    def body(j, carry):
        index = conn[pl.ds(j, 1), :]
        for q, g in enumerate(groups):
            out[j, q * 8 : q * 8 + 8, :] = lookup(tiles(own, g * 8, OWN_T), index)
        return carry

    lax.fori_loop(0, EB, body, 0, unroll=4)


def gather_ghosts(got_own, low, up, conn, out, groups):
    def body(j, carry):
        index = conn[pl.ds(j, 1), :]
        ghost = jnp.broadcast_to(index >= EDGES, (8, LANES))
        for q, g in enumerate(groups):
            value = lookup(tiles(low, g * 8, GHOST_T) + tiles(up, g * 8, GHOST_T), index)
            out[j, q * 8 : q * 8 + 8, :] = jnp.where(ghost, value, got_own[j, q * 8 : q * 8 + 8, :])
        return carry

    lax.fori_loop(0, EB, body, 0, unroll=4)


def product(freq, got, stiff, mass, out, per_harm, wide):
    for h in range(2):
        weight = freq[h]

        def outer(jt, carry):
            def inner(i, sums):
                ks = []
                for q in range(wide):
                    rows = pl.ds(pl.multiple_of((jt * wide + q) * 8, 8), 8)
                    ks.append(stiff[i, rows, :] + weight * mass[i, rows, :])
                new = []
                for r in range(per_harm):
                    x = jnp.broadcast_to(got[i, pl.ds(h * per_harm + r, 1), :], (8, LANES))
                    for q in range(wide):
                        new.append(sums[r * wide + q] + ks[q] * x)
                return tuple(new)

            zero = jnp.zeros((8, LANES), f32)
            sums = lax.fori_loop(0, EB, inner, (zero,) * (per_harm * wide), unroll=4)
            for r in range(per_harm):
                for q in range(wide):
                    rows = pl.ds(pl.multiple_of((jt * wide + q) * 8, 8), 8)
                    out[h * per_harm + r, rows, :] = sums[r * wide + q]
            return carry

        lax.fori_loop(0, EB // (8 * wide), outer, 0)


def pieces(x):
    high = x.astype(bf16).astype(f32)
    return jnp.concatenate([high, x - high], axis=0).astype(bf16)


def one_hot_low(index):
    low = jnp.broadcast_to(index & 255, (256, LANES))
    return jnp.where(low == lax.broadcasted_iota(i32, (256, LANES), 0), 1.0, 0.0).astype(bf16)


def masked_stack(parts, index, first, last):
    high = index >> 8
    stack = []
    for t in range(first, last):
        mask = jnp.broadcast_to(jnp.where(high == t, 1.0, 0.0), parts.shape).astype(bf16)
        stack.append(parts * mask)
    return stack


def add_up(stack, hot):
    return lax.dot_general(stack, hot, (((1,), (1,)), ((), ())), preferred_element_type=f32)


CHUNK = 16


def scatter_blocks(terms, conn, hot, stack, total, first, last):
    total[...] = jnp.zeros_like(total)

    def outer(c, carry):
        def body(jj, inner):
            j = c * CHUNK + jj
            index = conn[pl.ds(j, 1), :]
            cols = pl.ds(pl.multiple_of(jj * LANES, LANES), LANES)
            x = terms[:, pl.ds(j, 1), :].reshape(ROWS, LANES)
            for t, part in enumerate(masked_stack(pieces(x), index, first, last)):
                stack[t * 48 : t * 48 + 48, cols] = part
            return inner

        lax.fori_loop(0, CHUNK, body, 0, unroll=2)
        wide = CHUNK * LANES
        total[...] += add_up(stack[...], hot[:, pl.ds(pl.multiple_of(c * wide, wide), wide)])
        return carry

    lax.fori_loop(0, EB // CHUNK, outer, 0)


def total_tile(total, t):
    return total[t * 48 : t * 48 + 24, :] + total[t * 48 + 24 : t * 48 + 48, :]


def edge_weights(freq, rows, width):
    upper = lax.broadcasted_iota(i32, (rows, width), 0) < rows // 2
    return jnp.where(upper, freq[0], freq[1])


def pick_listed(source, lists, outs, groups):
    for side in range(2):
        for c in range(GHOST_T):
            cols = slice(c * LANES, (c + 1) * LANES)
            index = lists[side : side + 1, cols]
            for g in range(groups):
                value = lookup(tiles(source, g * 8, OWN_T), index)
                outs[side][g * 8 : g * 8 + 8, cols] = jnp.where(index >= 0, value, 0.0)


def fold(x):
    rows, cols = x.shape
    total = jnp.zeros((8, LANES), f32)
    for r in range(rows // 8):
        for c in range(cols // LANES):
            total = total + x[r * 8 : r * 8 + 8, c * LANES : (c + 1) * LANES]
    return total


def prep_kernel(rhs, field, lists, rows, to_low, to_up):
    for h in range(2):
        for o in range(6):
            at = h * 12 + o * 2
            rows[at : at + 2, :] = rhs[h, o]
        rows[24 + 2 * h : 26 + 2 * h, :] = field[h]
    rows[28:32, :] = jnp.zeros((4, EDGES), f32)
    pick_listed(rows, lists, (to_low, to_up), 4)


def hot_kernel(conn, hot):
    def body(j, carry):
        hot[:, pl.ds(pl.multiple_of(j * LANES, LANES), LANES)] = one_hot_low(conn[pl.ds(j, 1), :])
        return carry

    lax.fori_loop(0, EB, body, 0, unroll=2)


def own_kernel(rows, conn, got):
    gather_own(rows, conn, got, (0, 1, 2))


def apply_kernel(
    freq, got_own, low, up, conn, hot, stiff, mass, got, terms, to_low, to_up, stack, total
):
    gather_ghosts(got_own, low, up, conn, got, (0, 1, 2))
    product(freq, got, stiff, mass, terms, 12, 2)
    scatter_blocks(terms, conn, hot, stack, total, 8, 12)
    for t in range(2):
        cols = slice(t * 256, (t + 1) * 256)
        to_low[:, cols] = total_tile(total, t)
        to_up[:, cols] = total_tile(total, 2 + t)


def sums_kernel(freq, terms, conn, hot, own, mass_row, p, stack, total):
    scatter_blocks(terms, conn, hot, stack, total, 0, 8)
    weights = edge_weights(freq, ROWS, 256)
    for t in range(8):
        cols = slice(t * 256, (t + 1) * 256)
        p[:, cols] = total_tile(total, t) + weights * mass_row[0:1, cols] * own[0:24, cols]


def finish_kernel(p, lists, from_low, from_up, own, to_low, to_up):
    arrived = jnp.concatenate([from_low[...], from_up[...]], axis=1)
    hots, stacks = [], []
    for c in range(2 * GHOST_T):
        index = lists[c // GHOST_T : c // GHOST_T + 1, (c % GHOST_T) * LANES : (c % GHOST_T + 1) * LANES]
        hots.append(one_hot_low(index))
        parts = pieces(arrived[:, c * LANES : (c + 1) * LANES])
        stacks.append(jnp.concatenate(masked_stack(parts, index, 0, 8), axis=0))
    sums = add_up(jnp.concatenate(stacks, axis=1), jnp.concatenate(hots, axis=1))
    for t in range(8):
        own[:, t * 256 : (t + 1) * 256] = p[:, t * 256 : (t + 1) * 256] + total_tile(sums, t)
    pick_listed(own, lists, (to_low, to_up), 3)


def quadratic(freq, got, got_rows, stiff, mass):
    result = jnp.zeros((8, LANES), f32)
    for h in range(2):
        weight = freq[h]
        for jt in range(8):

            def inner(i, sums):
                k = stiff[i, jt * 8 : jt * 8 + 8, :] + weight * mass[i, jt * 8 : jt * 8 + 8, :]
                return tuple(
                    s + k * jnp.broadcast_to(got[i, h * 12 + r : h * 12 + r + 1, :], (8, LANES))
                    for r, s in enumerate(sums)
                )

            zero = jnp.zeros((8, LANES), f32)
            sums = (zero,) * 12
            if jt < 7:
                sums = lax.fori_loop(jt * 8 + 8, EB, inner, sums, unroll=4)
                sums = tuple(s + s for s in sums)
            sums = lax.fori_loop(jt * 8, jt * 8 + 8, inner, sums, unroll=4)
            for r in range(12):
                mine = got_rows[pl.ds(jt * 8 * ROWS + h * 12 + r, 8, stride=ROWS), :]
                result = result + sums[r] * mine
    return result


def early_kernel(b_rows, w, moments):
    b = b_rows[0:24, :]
    moments[0:8, :] = fold(b * b)
    moments[8:16, :] = fold(b * w[...])
    moments[16:24, :] = fold(w[...] * w[...])


def third_kernel(
    freq, got_own, low, up, conn, stiff, mass, mass_row, w, v, early, got_rows, line_out, got
):
    gather_ghosts(got_own, low, up, conn, got, (0, 1, 2))
    for j in range(EB):
        got_rows[j * ROWS : (j + 1) * ROWS, :] = got[j]
    last = quadratic(freq, got, got_rows, stiff, mass)
    weights = edge_weights(freq, ROWS, 256)
    for t in range(8):
        cols = slice(t * 256, (t + 1) * 256)
        last = last + fold(weights * mass_row[0:1, cols] * v[:, cols] * v[:, cols])
    parts = [early[0:8, :], early[8:16, :], early[16:24, :], fold(w[...] * v[...]), fold(v[...] * v[...]), last]
    lane = lax.broadcasted_iota(i32, (1, LANES), 1)
    line = jnp.zeros((1, LANES), f32)
    for k, tile in enumerate(parts):
        line = line + jnp.where((lane & 7) == k, jnp.sum(tile), 0.0)
    line_out[...] = jnp.broadcast_to(line, (8, LANES))


def field_kernel(freq, rows, low, up, conn, stiff, mass, y, got_own, got):
    gather_own(rows, conn, got_own, (3,))
    gather_ghosts(got_own, low, up, conn, got, (3,))
    product(freq, got, stiff, mass, y, 2, 4)


def gradients(got_rows, y, node_block, node_shape, energy, out, base):
    for jt in range(8):
        ys = [y[r, jt * 8 : jt * 8 + 8, :] for r in range(4)]
        for o in range(6):
            term = jnp.zeros((8, LANES), f32)
            for h in range(2):
                for c in range(2):
                    x = got_rows[pl.ds(jt * 8 * ROWS + h * 12 + o * 2 + c, 8, stride=ROWS), :]
                    term = term - x * ys[h * 2 + c] if c else term + x * ys[h * 2 + c]
            energy[o, jt * 8 : jt * 8 + 8, :] = term

    def body(c, carry):
        index = jnp.broadcast_to(node_block[pl.ds(c, 1), :], (8, LANES))
        cols = pl.ds(pl.multiple_of(c * LANES, LANES), LANES)
        sums = [jnp.zeros((8, LANES), f32) for _ in range(18)]
        for jt in range(8):
            shape = [node_shape[k, jt * 8 : jt * 8 + 8, cols] for k in range(3)]
            for o in range(6):
                x = jnp.take_along_axis(energy[o, jt * 8 : jt * 8 + 8, :], index, axis=1, mode="promise_in_bounds")
                for k in range(3):
                    sums[o * 3 + k] = sums[o * 3 + k] - shape[k] * x
        for q in range(18):
            out[c, base + q : base + q + 1, :] = jnp.sum(sums[q], axis=0, keepdims=True)
        return carry

    lax.fori_loop(0, 8, body, 0)


def early_gradient_kernel(got0, got1, y, node_block, node_shape, out, energy):
    gradients(got0, y, node_block, node_shape, energy, out, 0)
    gradients(got1, y, node_block, node_shape, energy, out, 18)
    out[:, 36:40, :] = jnp.zeros((8, 4, LANES), f32)


def late_gradient_kernel(early, got2, y, node_block, node_shape, line, out, energy):
    out[:, 0:40, :] = early[...]
    gradients(got2, y, node_block, node_shape, energy, out, 40)
    for c in range(8):
        out[c, 58:64, :] = line[0:6, :]


def message_kernel(shares, out):
    line = shares[0, 60:61, :]
    for d in range(1, 8):
        line = line + shares[d, 60:61, :]
    out[...] = jnp.broadcast_to(line, (2, LANES))


def last_kernel(messages, rows, w, v, shares, adjoint, gradient):
    line = jnp.sum(messages[...], axis=0, keepdims=True)
    lane = lax.broadcasted_iota(i32, (1, LANES), 1)

    def moment(k):
        return jnp.sum(jnp.where((lane & 7) == k, line, 0.0), axis=1, keepdims=True)

    m = [moment(k) for k in range(6)]
    a0 = m[0] / m[1]
    r1 = (None, -a0)
    rr1 = m[0] - 2.0 * a0 * m[1] + a0 * a0 * m[2]
    b0 = rr1 / m[0]
    d1 = (1.0 + b0, -a0)
    dad1 = d1[0] * d1[0] * m[1] + 2.0 * d1[0] * d1[1] * m[2] + d1[1] * d1[1] * m[3]
    a1 = rr1 / dad1
    r2 = (None, r1[1] - a1 * d1[0], -a1 * d1[1])
    rr2 = (
        m[0] + 2.0 * r2[1] * m[1] + (2.0 * r2[2] + r2[1] * r2[1]) * m[2]
        + 2.0 * r2[1] * r2[2] * m[3] + r2[2] * r2[2] * m[4]
    )
    b1 = rr2 / rr1
    d2 = (1.0 + b1 * d1[0], r2[1] + b1 * d1[1], r2[2])
    dad2 = (
        d2[0] * d2[0] * m[1] + 2.0 * d2[0] * d2[1] * m[2] + (2.0 * d2[0] * d2[2] + d2[1] * d2[1]) * m[3]
        + 2.0 * d2[1] * d2[2] * m[4] + d2[2] * d2[2] * m[5]
    )
    a2 = rr2 / dad2
    c0 = a0 + a1 * d1[0] + a2 * d2[0]
    c1 = a1 * d1[1] + a2 * d2[1]
    c2 = a2 * d2[2]
    for h in range(2):
        for o in range(6):
            at = slice(h * 12 + o * 2, h * 12 + o * 2 + 2)
            adjoint[h, o] = c0 * rows[at, :] + c1 * w[at, :] + c2 * v[at, :]
    share = shares[0]
    for d in range(1, 8):
        share = share + shares[d]
    for o in range(6):
        gradient[o] = (
            c0 * share[o * 3 : o * 3 + 3] + c1 * share[18 + o * 3 : 21 + o * 3] + c2 * share[40 + o * 3 : 43 + o * 3]
        )


def shifted(x, by):
    count = lax.axis_size("mesh")
    return lax.ppermute(x, "mesh", [(i, i + by) for i in range(count) if 0 <= i + by < count])


def exchanged(to_low, to_up):
    return shifted(to_up, 1), shifted(to_low, -1)


def per_device(
    adjoint_rhs, forward_field, stiffness, mass_blocks, frequency, edge_mass, connectivity, send_list, node_block, node_shape
):
    lists = send_list[0]
    mass_row = edge_mass.reshape(1, EDGES)
    nodes = node_block.reshape(8, LANES)
    wide = CHUNK * LANES
    ghosts = (arr(ROWS, SLOTS), arr(ROWS, SLOTS))
    got_shape = arr(EB, ROWS, LANES)
    flat = lambda x: x.reshape(EB * ROWS, LANES)

    rows, to_low, to_up = kernel_call(
        prep_kernel, "prep", (arr(32, EDGES), arr(32, SLOTS), arr(32, SLOTS)), [VMEM] * 3,
        flops=10**6, nbytes=10**6,
    )(adjoint_rhs, forward_field, lists)
    rim_low, rim_up = exchanged(to_low, to_up)
    (hot,) = kernel_call(
        hot_kernel, "hot", (jax.ShapeDtypeStruct((256, EB * LANES), bf16),), [VMEM], flops=10**7, nbytes=4 * 10**6
    )(connectivity)

    def gathered_own(x):
        return kernel_call(own_kernel, "own", (got_shape,), [VMEM] * 2, flops=10**7, nbytes=10**7)(x, connectivity)[0]

    def applied(x, got_own, low, up):
        got, terms, to_low, to_up = kernel_call(
            apply_kernel, "apply", (got_shape, arr(ROWS, EB, LANES)) + ghosts, [SMEM] + [VMEM] * 7,
            [pltpu.VMEM((4 * 48, wide), bf16), pltpu.VMEM((4 * 48, 256), f32)],
            flops=10**8, nbytes=10**7,
        )(frequency, got_own, low, up, connectivity, hot, stiffness, mass_blocks)
        from_low, from_up = exchanged(to_low, to_up)
        (p,) = kernel_call(
            sums_kernel, "sums", (arr(ROWS, EDGES),), [SMEM] + [VMEM] * 5,
            [pltpu.VMEM((8 * 48, wide), bf16), pltpu.VMEM((8 * 48, 256), f32)], flops=10**8, nbytes=10**7,
        )(frequency, terms, connectivity, hot, x, mass_row)
        own, to_low, to_up = kernel_call(
            finish_kernel, "finish", (arr(ROWS, EDGES),) + ghosts, [VMEM] * 4, flops=10**7, nbytes=10**6
        )(p, lists, from_low, from_up)
        return got, own, exchanged(to_low, to_up)

    got0, w, (low, up) = applied(rows, gathered_own(rows), rim_low, rim_up)
    w_own = gathered_own(w)
    (y,) = kernel_call(
        field_kernel, "field", (arr(4, EB, LANES),), [SMEM] + [VMEM] * 6,
        [pltpu.VMEM((EB, 8, LANES), f32), pltpu.VMEM((EB, 8, LANES), f32)],
        flops=10**8, nbytes=10**7,
    )(frequency, rows, rim_low, rim_up, connectivity, stiffness, mass_blocks)
    got1, v, (low, up) = applied(w, w_own, low, up)
    v_own = gathered_own(v)
    (early,) = kernel_call(early_kernel, "early", (arr(24, LANES),), [VMEM] * 2, flops=10**6, nbytes=10**6)(rows, w)
    (grads,) = kernel_call(
        early_gradient_kernel, "early_gradient", (arr(8, 40, LANES),), [VMEM] * 5, [pltpu.VMEM((6, EB, LANES), f32)],
        flops=10**8, nbytes=10**7,
    )(flat(got0), flat(got1), y, nodes, node_shape)
    got2, line = kernel_call(
        third_kernel, "third", (arr(EB * ROWS, LANES), arr(8, LANES)), [SMEM] + [VMEM] * 10,
        [pltpu.VMEM((EB, ROWS, LANES), f32)], flops=10**8, nbytes=10**7,
    )(frequency, v_own, low, up, connectivity, stiffness, mass_blocks, mass_row, w, v, early)
    (grads,) = kernel_call(
        late_gradient_kernel, "late_gradient", (arr(8, 64, LANES),), [VMEM] * 6, [pltpu.VMEM((6, EB, LANES), f32)],
        flops=10**8, nbytes=10**7,
    )(grads, got2, y, nodes, node_shape, line)
    shares = lax.all_to_all(grads, "harm", 0, 0, tiled=True)
    (message,) = kernel_call(message_kernel, "message", (arr(2, LANES),), [VMEM], flops=10**3, nbytes=10**5)(shares)
    messages = lax.all_to_all(message.reshape(2 * LANES), "mesh", 0, 0, tiled=True).reshape(2, LANES)
    adjoint, gradient = kernel_call(
        last_kernel, "last", (arr(*adjoint_rhs.shape), arr(6, 3, LANES)), [VMEM] * 5, flops=10**6, nbytes=10**6
    )(messages, rows, w, v, shares)
    return adjoint, gradient


def solution(mesh):
    return jax.shard_map(
        per_device,
        mesh=mesh,
        in_specs=(
            P("harm", None, None, "mesh"),
            P("harm", None, "mesh"),
            P(None, None, "mesh"),
            P(None, None, "mesh"),
            P("harm"),
            P("mesh"),
            P(None, "mesh"),
            P("mesh", None, None),
            P("mesh"),
            P(None, None, "mesh"),
        ),
        out_specs=(P("harm", None, None, "mesh"), P(None, None, ("mesh", "harm"))),
        check_vma=False,
    )
```

time: 155 us -> 147 us (0.948); the launches traced: 153 us -> 147 us
  Pallas kernels: 66 us -> 73.7 us
  blocking collectives: 30.8 us -> 25.6 us
  local copies, waits for them, and re-layouts: 7.68 us -> 3.84 us
  waiting for transfers between devices: 3.63 us -> 0.03 us
  starting transfers between devices: 43.7 us -> 41.9 us
    pallas_call x3 -> x13, Pallas kernels: 55.7 us -> 62.1 us  [the longest x2 24.9 us: applied(): kernel_call(apply_kernel, 'apply', (got_shape, arr(ROWS, EB, LANES)) + gh...]
    all_to_all x1, blocking collectives: 19 us -> 13.8 us  [per_device(): lax.all_to_all(message.reshape(2 * LANES), 'mesh', 0, 0, tiled=True)]
    unnamed x26 -> x24, local copies, waits for them, and re-layouts: 7.68 us -> 3.16 us
    ppermute x10, waiting for transfers between devices: 3.63 us -> 0.03 us  [shifted(): lax.ppermute(x, 'mesh', [(i, i + by) for i in range(count) if 0 <= i + by...]
    ppermute x10, starting transfers between devices: 43.7 us -> 41.9 us  [shifted(): lax.ppermute(x, 'mesh', [(i, i + by) for i in range(count) if 0 <= i + by...]
  transfers between devices with their start and end apart: 10 -> 10, of which waited for: 4 -> 0; matrix products, arithmetic and copies ran while one was open for 0% -> 0% of each run, Pallas kernels for 5% -> 25%
where the time goes in v2:
time: 147 us
  Pallas kernels  73.7 us (50%)
  starting transfers between devices  41.9 us (29%)
  blocking collectives  25.6 us (17%)
  local copies, waits for them, and re-layouts  3.84 us (3%)
    ppermute x10, starting transfers between devices, shifted(): lax.ppermute(x, 'mesh', [(i, i + by) for i in range(count) if 0 <= i + by...  41.9 us
    pallas_call x2, Pallas kernels, applied(): kernel_call(apply_kernel, 'apply', (got_shape, arr(ROWS, EB, LANES)) + gh...  24.9 us
    all_to_all x1, blocking collectives, per_device(): lax.all_to_all(message.reshape(2 * LANES), 'mesh', 0, 0, tiled=True)  13.8 us
    pallas_call x3, Pallas kernels, gathered_own(): kernel_call(own_kernel, 'own', (got_shape,), [VMEM] * 2, flops=10 ** 7, n...  13.7 us
    pallas_call x2, Pallas kernels, applied(): kernel_call(sums_kernel, 'sums', (arr(ROWS, EDGES),), [SMEM] + [VMEM] * 5...  12.7 us
    all_to_all x1, blocking collectives, per_device(): shares = lax.all_to_all(grads, 'harm', 0, 0, tiled=True)  11.8 us
    pallas_call x1, Pallas kernels, per_device(): kernel_call(third_kernel, 'third', (arr(EB * ROWS, LANES), arr(8, LANES))...  6.8 us
    pallas_call x1, Pallas kernels, per_device(): kernel_call(field_kernel, 'field', (arr(4, EB, LANES),), [SMEM] + [VMEM]...  6.03 us
  transfers between devices with their start and end apart: 10, of which 0 were waited for; matrix products, arithmetic and copies ran while one was open for 0% of the time, Pallas kernels for 25%

profile of v2, /device:TPU:2, one launch (start us, length us, event | category | flops | bytes accessed | tf_op | source)
XLA Modules:
  0.0 146.7 jit_solution(12549182211239366584)
XLA Ops:
  0.6 0.9 copy-done.5
  1.6 0.7 copy-done.7
  2.2 0.8 copy-done.9
  3.7 3.8 %collective-permute-start = (f32[32,512]{1,0:T(8,128)S(1)}, f32[32,512]{1,0:T(8,128)S(1)}, u32[]{:S(2)}, u32[]{:S(2)}) collective-permute-start(f32[32,512]{1,0:T(8,128)S(1)} %get-tuple-element.22), channel_id=1, source_target_pairs={{0,8},{8,16},{16,24},{24,32},{32,40},{40,48},{48,56},{56,64},{64,7... | collective-permute-start | bytes 196616 | tf_op jit(solution)/shard_map/ppermute | solution.py:392
  7.5 6.1 %collective-permute-start.1 = (f32[32,512]{1,0:T(8,128)S(1)}, f32[32,512]{1,0:T(8,128)S(1)}, u32[]{:S(2)}, u32[]{:S(2)}) collective-permute-start(f32[32,512]{1,0:T(8,128)S(1)} %get-tuple-element.23), channel_id=1, source_target_pairs={{8,0},{16,8},{24,16},{32,24},{40,32},{48,40},{56,48},{64,56},{72,6... | collective-permute-start | bytes 196616 | tf_op jit(solution)/shard_map/ppermute | solution.py:392
  13.6 0.7 copy-done.2
  14.4 1.5 %hot.1 = bf16[256,8192]{1,0:T(8,128)(2,1)S(1)} custom-call(s32[64,128]{1,0:T(8,128)S(1)} %copy-done.2), custom_call_target="tpu_custom_call" | custom-call | flops 10000000 | bytes 4000000 | tf_op jit(solution)/shard_map/hot/pallas_call | solution.py:415
  15.9 4.6 %own.3.got_own = f32[64,24,128]{2,1,0:T(8,128)S(1)} custom-call(f32[32,2048]{1,0:T(8,128)S(1)} %get-tuple-element.21.rows.own.b_rows, s32[64,128]{1,0:T(8,128)S(1)} %copy-done.2), custom_call_target="tpu_custom_call" | custom-call | flops 10000000 | bytes 10000000 | tf_op jit(solution)/shard_map/own/pallas_call | solution.py:420
  20.5 12.5 %apply.2 = (f32[64,24,128]{2,1,0:T(8,128)S(1)}, f32[24,64,128]{2,1,0:T(8,128)S(1)}, f32[24,512]{1,0:T(8,128)S(1)}, f32[24,512]{1,0:T(8,128)S(1)}) custom-call(f32[2]{0:T(128)S(1)} %copy-done.10, f32[64,24,128]{2,1,0:T(8,128)S(1)} %own.3.got_own, f32[32,512]{1,0:T(8,128)S(1)} %collective-permute-done.low, f32[32,512]{1,0:T(8,128)S(1)} %collective-permute-done.1.up, ...), custom_call_target="tpu_custom_call" | custom-call | flops 100000000 | bytes 10000000 | tf_op jit(solution)/shard_map/apply/pallas_call | solution.py:423
  33.0 1.9 %collective-permute-start.2 = (f32[24,512]{1,0:T(8,128)S(1)}, f32[24,512]{1,0:T(8,128)S(1)}, u32[]{:S(2)}, u32[]{:S(2)}) collective-permute-start(f32[24,512]{1,0:T(8,128)S(1)} %get-tuple-element.26), channel_id=1, source_target_pairs={{0,8},{8,16},{16,24},{24,32},{32,40},{40,48},{48,56},{56,64},{64,7... | collective-permute-start | bytes 147464 | tf_op jit(solution)/shard_map/ppermute | solution.py:392
  35.0 6.0 %collective-permute-start.3 = (f32[24,512]{1,0:T(8,128)S(1)}, f32[24,512]{1,0:T(8,128)S(1)}, u32[]{:S(2)}, u32[]{:S(2)}) collective-permute-start(f32[24,512]{1,0:T(8,128)S(1)} %get-tuple-element.27), channel_id=1, source_target_pairs={{8,0},{16,8},{24,16},{32,24},{40,32},{48,40},{56,48},{64,56},{72,6... | collective-permute-start | bytes 147464 | tf_op jit(solution)/shard_map/ppermute | solution.py:392
  41.0 6.4 %sums.2.p = f32[24,2048]{1,0:T(8,128)S(1)} custom-call(f32[2]{0:T(128)S(1)} %copy-done.10, f32[24,64,128]{2,1,0:T(8,128)S(1)} %get-tuple-element.25.terms, s32[64,128]{1,0:T(8,128)S(1)} %copy-done.2, bf16[256,8192]{1,0:T(8,128)(2,1)S(1)} %hot.1, f32[32,2048]{1,0:T(8,128)S(1)} %get-tuple-element.21.rows.own.b_rows, f32[1,2048]{1,0:T(1,128)S(1)} %bitcast.9), custom_call_target="tpu_custom_call" | custom-call | flops 100000000 | bytes 10000000 | tf_op jit(solution)/shard_map/sums/pallas_call | solution.py:429
  47.4 1.2 finish.2
  48.6 1.9 %collective-permute-start.4 = (f32[24,512]{1,0:T(8,128)S(1)}, f32[24,512]{1,0:T(8,128)S(1)}, u32[]{:S(2)}, u32[]{:S(2)}) collective-permute-start(f32[24,512]{1,0:T(8,128)S(1)} %get-tuple-element.29), channel_id=1, source_target_pairs={{0,8},{8,16},{16,24},{24,32},{32,40},{40,48},{48,56},{56,64},{64,7... | collective-permute-start | bytes 147464 | tf_op jit(solution)/shard_map/ppermute | solution.py:392
  50.5 6.0 %collective-permute-start.5 = (f32[24,512]{1,0:T(8,128)S(1)}, f32[24,512]{1,0:T(8,128)S(1)}, u32[]{:S(2)}, u32[]{:S(2)}) collective-permute-start(f32[24,512]{1,0:T(8,128)S(1)} %get-tuple-element.30), channel_id=1, source_target_pairs={{8,0},{16,8},{24,16},{32,24},{40,32},{48,40},{56,48},{64,56},{72,6... | collective-permute-start | bytes 147464 | tf_op jit(solution)/shard_map/ppermute | solution.py:392
  56.6 4.6 %own.4.got_own = f32[64,24,128]{2,1,0:T(8,128)S(1)} custom-call(f32[24,2048]{1,0:T(8,128)S(1)} %get-tuple-element.28.rows.own.w, s32[64,128]{1,0:T(8,128)S(1)} %copy-done.3), custom_call_target="tpu_custom_call" | custom-call | flops 10000000 | bytes 10000000 | tf_op jit(solution)/shard_map/own/pallas_call | solution.py:420
  61.2 12.5 %apply.3 = (f32[64,24,128]{2,1,0:T(8,128)S(1)}, f32[24,64,128]{2,1,0:T(8,128)S(1)}, f32[24,512]{1,0:T(8,128)S(1)}, f32[24,512]{1,0:T(8,128)S(1)}) custom-call(f32[2]{0:T(128)S(1)} %copy-done.10, f32[64,24,128]{2,1,0:T(8,128)S(1)} %own.4.got_own, f32[24,512]{1,0:T(8,128)S(1)} %collective-permute-done.4.low, f32[24,512]{1,0:T(8,128)S(1)} %collective-permute-done.5.up, ...), custom_call_target="tpu_custom_call" | custom-call | flops 100000000 | bytes 10000000 | tf_op jit(solution)/shard_map/apply/pallas_call | solution.py:423
  73.6 1.9 %collective-permute-start.6 = (f32[24,512]{1,0:T(8,128)S(1)}, f32[24,512]{1,0:T(8,128)S(1)}, u32[]{:S(2)}, u32[]{:S(2)}) collective-permute-start(f32[24,512]{1,0:T(8,128)S(1)} %get-tuple-element.33), channel_id=1, source_target_pairs={{0,8},{8,16},{16,24},{24,32},{32,40},{40,48},{48,56},{56,64},{64,7... | collective-permute-start | bytes 147464 | tf_op jit(solution)/shard_map/ppermute | solution.py:392
  75.6 6.0 %collective-permute-start.7 = (f32[24,512]{1,0:T(8,128)S(1)}, f32[24,512]{1,0:T(8,128)S(1)}, u32[]{:S(2)}, u32[]{:S(2)}) collective-permute-start(f32[24,512]{1,0:T(8,128)S(1)} %get-tuple-element.34), channel_id=1, source_target_pairs={{8,0},{16,8},{24,16},{32,24},{40,32},{48,40},{56,48},{64,56},{72,6... | collective-permute-start | bytes 147464 | tf_op jit(solution)/shard_map/ppermute | solution.py:392
  81.6 6.4 %sums.3.p = f32[24,2048]{1,0:T(8,128)S(1)} custom-call(f32[2]{0:T(128)S(1)} %copy-done.10, f32[24,64,128]{2,1,0:T(8,128)S(1)} %get-tuple-element.32.terms, s32[64,128]{1,0:T(8,128)S(1)} %copy-done.3, bf16[256,8192]{1,0:T(8,128)(2,1)S(1)} %hot.1, f32[24,2048]{1,0:T(8,128)S(1)} %get-tuple-element.28.rows.own.w, f32[1,2048]{1,0:T(1,128)S(1)} %bitcast.10), custom_call_target="tpu_custom_call" | custom-call | flops 100000000 | bytes 10000000 | tf_op jit(solution)/shard_map/sums/pallas_call | solution.py:429
  88.0 1.2 finish.3
  89.2 1.9 %collective-permute-start.8 = (f32[24,512]{1,0:T(8,128)S(1)}, f32[24,512]{1,0:T(8,128)S(1)}, u32[]{:S(2)}, u32[]{:S(2)}) collective-permute-start(f32[24,512]{1,0:T(8,128)S(1)} %get-tuple-element.36), channel_id=1, source_target_pairs={{0,8},{8,16},{16,24},{24,32},{32,40},{40,48},{48,56},{56,64},{64,7... | collective-permute-start | bytes 147464 | tf_op jit(solution)/shard_map/ppermute | solution.py:392
  91.2 6.2 %collective-permute-start.9 = (f32[24,512]{1,0:T(8,128)S(1)}, f32[24,512]{1,0:T(8,128)S(1)}, u32[]{:S(2)}, u32[]{:S(2)}) collective-permute-start(f32[24,512]{1,0:T(8,128)S(1)} %get-tuple-element.37), channel_id=1, source_target_pairs={{8,0},{16,8},{24,16},{32,24},{40,32},{48,40},{56,48},{64,56},{72,6... | collective-permute-start | bytes 147464 | tf_op jit(solution)/shard_map/ppermute | solution.py:392
  97.4 6.0 %field.3.y = f32[4,64,128]{2,1,0:T(8,128)S(1)} custom-call(f32[2]{0:T(128)S(1)} %copy-done.10, f32[32,2048]{1,0:T(8,128)S(1)} %get-tuple-element.21.rows.own.b_rows, f32[32,512]{1,0:T(8,128)S(1)} %collective-permute-done.low, f32[32,512]{1,0:T(8,128)S(1)} %collective-permute-done.1.up, s32[64,128]{1,0:T(8,128)S(1)} %copy-done.3, f32[64,64,128]{2,1,0:T(8,128)S(1)} %copy-done, ...), custom_call_target="tpu_custom_call" | custom-call | flops 100000000 | bytes 10000000 | tf_op jit(solution)/shard_map/field/pallas_call | solution.py:440
  103.5 2.5 %early_gradient.1.early = f32[8,40,128]{2,1,0:T(8,128)S(1)} custom-call(f32[1536,128]{1,0:T(8,128)S(1)} %bitcast.7, f32[1536,128]{1,0:T(8,128)S(1)} %bitcast.8, f32[4,64,128]{2,1,0:T(8,128)S(1)} %field.3.y, s32[8,128]{1,0:T(8,128)S(1)} %bitcast.15, f32[3,64,1024]{2,1,0:T(8,128)S(1)} %copy-done.4), custom_call_target="tpu_custom_call" | custom-call | flops 100000000 | bytes 10000000 | tf_op jit(solution)/shard_map/early_gradient/pallas_call | solution.py:448
  106.0 4.6 %own.5.got_own = f32[64,24,128]{2,1,0:T(8,128)S(1)} custom-call(f32[24,2048]{1,0:T(8,128)S(1)} %get-tuple-element.35.rows.v, s32[64,128]{1,0:T(8,128)S(1)} %copy-done.3), custom_call_target="tpu_custom_call" | custom-call | flops 10000000 | bytes 10000000 | tf_op jit(solution)/shard_map/own/pallas_call | solution.py:420
  110.6 6.8 %third.1 = (f32[1536,128]{1,0:T(8,128)S(1)}, f32[8,128]{1,0:T(8,128)S(1)}) custom-call(f32[2]{0:T(128)S(1)} %copy-done.10, f32[64,24,128]{2,1,0:T(8,128)S(1)} %own.5.got_own, f32[24,512]{1,0:T(8,128)S(1)} %collective-permute-done.8.low, f32[24,512]{1,0:T(8,128)S(1)} %collective-permute-done.9.up, s32[64,128]{1,0:T(8,128)S(1)} %copy-done.3, ...), custom_call_target="tpu_custom_call" | custom-call | flops 100000000 | bytes 10000000 | tf_op jit(solution)/shard_map/third/pallas_call | solution.py:452
  117.4 1.3 late_gradient.1
  118.7 11.8 %all_to_all.14.shares = f32[8,64,128]{2,1,0:T(8,128)S(1)} all-to-all(f32[8,64,128]{2,1,0:T(8,128)S(1)} %late_gradient.1), channel_id=1, replica_groups=mesh['mesh'=32,'harm'=8] {'harm'}, dimensions={0} | all-to-all | bytes 524288 | tf_op jit(solution)/shard_map/all_to_all | solution.py:460
  130.6 13.8 %all_to_all.15 = f32[32,8,1]{1,2,0:T(1,128)S(1)} all-to-all(f32[32,8,1]{1,2,0:T(1,128)S(1)} %bitcast.17), channel_id=1, replica_groups=mesh['mesh'=32,'harm'=8] {'mesh'}, dimensions={0} | all-to-all | bytes 2048 | tf_op jit(solution)/shard_map/all_to_all | solution.py:462
  145.0 0.7 reduce.3
  145.8 1.0 last.1
  (36 shorter events, 1.5 us)
Async XLA Ops:
  0.6 0.9 copy-start.5
  1.6 0.7 copy-start.7
  2.2 0.8 copy-start.9
  3.7 16.8 %collective-permute-start = (f32[32,512]{1,0:T(8,128)S(1)}, f32[32,512]{1,0:T(8,128)S(1)}, u32[]{:S(2)}, u32[]{:S(2)}) collective-permute-start(f32[32,512]{1,0:T(8,128)S(1)} %get-tuple-element.22), channel_id=1, source_target_pairs={{0,8},{8,16},{16,24},{24,32},{32,40},{40,48},{48,56},{56,64},{64,7... | collective-permute-start | bytes 196616 | tf_op jit(solution)/shard_map/ppermute | solution.py:392
  7.5 13.0 %copy-start = (f32[64,64,128]{2,1,0:T(8,128)S(1)}, f32[64,64,128]{2,1,0:T(8,128)}, u32[]{:S(2)}) copy-start(f32[64,64,128]{2,1,0:T(8,128)} %stiff.7) | copy-start | bytes 6291460
  7.5 13.0 %copy-start.1 = (f32[64,64,128]{2,1,0:T(8,128)S(1)}, f32[64,64,128]{2,1,0:T(8,128)}, u32[]{:S(2)}) copy-start(f32[64,64,128]{2,1,0:T(8,128)} %mass.7) | copy-start | bytes 6291460
  7.5 13.0 %collective-permute-start.1 = (f32[32,512]{1,0:T(8,128)S(1)}, f32[32,512]{1,0:T(8,128)S(1)}, u32[]{:S(2)}, u32[]{:S(2)}) collective-permute-start(f32[32,512]{1,0:T(8,128)S(1)} %get-tuple-element.23), channel_id=1, source_target_pairs={{8,0},{16,8},{24,16},{32,24},{40,32},{48,40},{56,48},{64,56},{72,6... | collective-permute-start | bytes 196616 | tf_op jit(solution)/shard_map/ppermute | solution.py:392
  13.6 0.8 copy-start.2
  14.4 6.1 %copy-start.10 = (f32[2]{0:T(128)S(1)}, f32[2]{0:T(128)}, u32[]{:S(2)}) copy-start(f32[2]{0:T(128)} %freq.11) | copy-start | bytes 28
  20.5 20.5 %copy-start.6 = (f32[2048]{0:T(1024)S(1)}, f32[2048]{0:T(1024)}, u32[]{:S(2)}) copy-start(f32[2048]{0:T(1024)} %param.15) | copy-start | bytes 24580
  33.0 14.4 %collective-permute-start.2 = (f32[24,512]{1,0:T(8,128)S(1)}, f32[24,512]{1,0:T(8,128)S(1)}, u32[]{:S(2)}, u32[]{:S(2)}) collective-permute-start(f32[24,512]{1,0:T(8,128)S(1)} %get-tuple-element.26), channel_id=1, source_target_pairs={{0,8},{8,16},{16,24},{24,32},{32,40},{40,48},{48,56},{56,64},{64,7... | collective-permute-start | bytes 147464 | tf_op jit(solution)/shard_map/ppermute | solution.py:392
  35.0 12.4 %collective-permute-start.3 = (f32[24,512]{1,0:T(8,128)S(1)}, f32[24,512]{1,0:T(8,128)S(1)}, u32[]{:S(2)}, u32[]{:S(2)}) collective-permute-start(f32[24,512]{1,0:T(8,128)S(1)} %get-tuple-element.27), channel_id=1, source_target_pairs={{8,0},{16,8},{24,16},{32,24},{40,32},{48,40},{56,48},{64,56},{72,6... | collective-permute-start | bytes 147464 | tf_op jit(solution)/shard_map/ppermute | solution.py:392
  41.0 15.6 %copy-start.3 = (s32[64,128]{1,0:T(8,128)S(1)}, s32[64,128]{1,0:T(8,128)}, u32[]{:S(2)}) copy-start(s32[64,128]{1,0:T(8,128)} %conn.19) | copy-start | bytes 98308
  48.6 12.6 %collective-permute-start.4 = (f32[24,512]{1,0:T(8,128)S(1)}, f32[24,512]{1,0:T(8,128)S(1)}, u32[]{:S(2)}, u32[]{:S(2)}) collective-permute-start(f32[24,512]{1,0:T(8,128)S(1)} %get-tuple-element.29), channel_id=1, source_target_pairs={{0,8},{8,16},{16,24},{24,32},{32,40},{40,48},{48,56},{56,64},{64,7... | collective-permute-start | bytes 147464 | tf_op jit(solution)/shard_map/ppermute | solution.py:392
  50.5 10.6 %collective-permute-start.5 = (f32[24,512]{1,0:T(8,128)S(1)}, f32[24,512]{1,0:T(8,128)S(1)}, u32[]{:S(2)}, u32[]{:S(2)}) collective-permute-start(f32[24,512]{1,0:T(8,128)S(1)} %get-tuple-element.30), channel_id=1, source_target_pairs={{8,0},{16,8},{24,16},{32,24},{40,32},{48,40},{56,48},{64,56},{72,6... | collective-permute-start | bytes 147464 | tf_op jit(solution)/shard_map/ppermute | solution.py:392
  73.6 14.4 %collective-permute-start.6 = (f32[24,512]{1,0:T(8,128)S(1)}, f32[24,512]{1,0:T(8,128)S(1)}, u32[]{:S(2)}, u32[]{:S(2)}) collective-permute-start(f32[24,512]{1,0:T(8,128)S(1)} %get-tuple-element.33), channel_id=1, source_target_pairs={{0,8},{8,16},{16,24},{24,32},{32,40},{40,48},{48,56},{56,64},{64,7... | collective-permute-start | bytes 147464 | tf_op jit(solution)/shard_map/ppermute | solution.py:392
  75.6 12.4 %collective-permute-start.7 = (f32[24,512]{1,0:T(8,128)S(1)}, f32[24,512]{1,0:T(8,128)S(1)}, u32[]{:S(2)}, u32[]{:S(2)}) collective-permute-start(f32[24,512]{1,0:T(8,128)S(1)} %get-tuple-element.34), channel_id=1, source_target_pairs={{8,0},{16,8},{24,16},{32,24},{40,32},{48,40},{56,48},{64,56},{72,6... | collective-permute-start | bytes 147464 | tf_op jit(solution)/shard_map/ppermute | solution.py:392
  81.6 6.4 %copy-start.8 = (s32[1,2,512]{2,1,0:T(2,128)S(1)}, s32[1,2,512]{2,1,0:T(2,128)}, u32[]{:S(2)}) copy-start(s32[1,2,512]{2,1,0:T(2,128)} %param.17) | copy-start | bytes 12292
  89.2 21.4 %collective-permute-start.8 = (f32[24,512]{1,0:T(8,128)S(1)}, f32[24,512]{1,0:T(8,128)S(1)}, u32[]{:S(2)}, u32[]{:S(2)}) collective-permute-start(f32[24,512]{1,0:T(8,128)S(1)} %get-tuple-element.36), channel_id=1, source_target_pairs={{0,8},{8,16},{16,24},{24,32},{32,40},{40,48},{48,56},{56,64},{64,7... | collective-permute-start | bytes 147464 | tf_op jit(solution)/shard_map/ppermute | solution.py:392
  91.2 12.3 %copy-start.4 = (f32[3,64,1024]{2,1,0:T(8,128)S(1)}, f32[3,64,1024]{2,1,0:T(8,128)}, u32[]{:S(2)}) copy-start(f32[3,64,1024]{2,1,0:T(8,128)} %node_shape.3) | copy-start | bytes 2359300
  91.2 12.3 %copy-start.11 = (s32[1024]{0:T(1024)S(1)}, s32[1024]{0:T(1024)}, u32[]{:S(2)}) copy-start(s32[1024]{0:T(1024)} %param.18) | copy-start | bytes 12292
  91.2 19.4 %collective-permute-start.9 = (f32[24,512]{1,0:T(8,128)S(1)}, f32[24,512]{1,0:T(8,128)S(1)}, u32[]{:S(2)}, u32[]{:S(2)}) collective-permute-start(f32[24,512]{1,0:T(8,128)S(1)} %get-tuple-element.37), channel_id=1, source_target_pairs={{8,0},{16,8},{24,16},{32,24},{40,32},{48,40},{56,48},{64,56},{72,6... | collective-permute-start | bytes 147464 | tf_op jit(solution)/shard_map/ppermute | solution.py:392

commit v3 on v2

--- a/solution.py
+++ b/solution.py
@@ -58,51 +58,58 @@
     return [ref[row : row + 8, t * LANES : (t + 1) * LANES] for t in range(count)]
 
 
-def gather_own(own, conn, out, groups):
-    def body(j, carry):
-        index = conn[pl.ds(j, 1), :]
-        for q, g in enumerate(groups):
-            out[j, q * 8 : q * 8 + 8, :] = lookup(tiles(own, g * 8, OWN_T), index)
+WIDE = 512
+PARTS = (EDGES + 2 * SLOTS) // WIDE
+CHUNK = 16
+
+
+def gather_blocks(own, low, up, conn, hot, stack, outs):
+    count = own.shape[0]
+    for t in range(PARTS):
+        x = own[:, t * WIDE : (t + 1) * WIDE] if t < PARTS - 2 else (low if t == PARTS - 2 else up)[...]
+        stack[t * 2 * count : (t + 1) * 2 * count, :] = pieces(x)
+
+    def body(c, carry):
+        cols = pl.ds(pl.multiple_of(c * CHUNK * LANES, CHUNK * LANES), CHUNK * LANES)
+        found = jnp.dot(stack[...], hot[:, cols], preferred_element_type=f32)
+        for jj in range(CHUNK):
+            j = c * CHUNK + jj
+            high = conn[pl.ds(j, 1), :] >> 9
+            for out, first, rows in outs:
+                value = None
+                for t in range(PARTS):
+                    at = t * 2 * count + first
+                    lanes = slice(jj * LANES, (jj + 1) * LANES)
+                    x = found[at : at + rows, lanes] + found[at + count : at + count + rows, lanes]
+                    value = x if t == 0 else jnp.where(jnp.broadcast_to(high, x.shape) == t, x, value)
+                out[pl.ds(pl.multiple_of(j * rows, 8), rows), :] = value
         return carry
 
-    lax.fori_loop(0, EB, body, 0, unroll=4)
-
-
-def gather_ghosts(got_own, low, up, conn, out, groups):
-    def body(j, carry):
-        index = conn[pl.ds(j, 1), :]
-        ghost = jnp.broadcast_to(index >= EDGES, (8, LANES))
-        for q, g in enumerate(groups):
-            value = lookup(tiles(low, g * 8, GHOST_T) + tiles(up, g * 8, GHOST_T), index)
-            out[j, q * 8 : q * 8 + 8, :] = jnp.where(ghost, value, got_own[j, q * 8 : q * 8 + 8, :])
-        return carry
-
-    lax.fori_loop(0, EB, body, 0, unroll=4)
-
-
-def product(freq, got, stiff, mass, out, per_harm, wide):
+    lax.fori_loop(0, EB // CHUNK, body, 0)
+
+
+def product(blocks, got, out, per_harm, per_edge, wide):
     for h in range(2):
-        weight = freq[h]
 
         def outer(jt, carry):
             def inner(i, sums):
                 ks = []
                 for q in range(wide):
                     rows = pl.ds(pl.multiple_of((jt * wide + q) * 8, 8), 8)
-                    ks.append(stiff[i, rows, :] + weight * mass[i, rows, :])
+                    ks.append(blocks[h, i, rows, :])
                 new = []
                 for r in range(per_harm):
-                    x = jnp.broadcast_to(got[i, pl.ds(h * per_harm + r, 1), :], (8, LANES))
+                    x = jnp.broadcast_to(got[pl.ds(i * per_edge + h * per_harm + r, 1), :], (8, LANES))
                     for q in range(wide):
                         new.append(sums[r * wide + q] + ks[q] * x)
                 return tuple(new)
 
             zero = jnp.zeros((8, LANES), f32)
-            sums = lax.fori_loop(0, EB, inner, (zero,) * (per_harm * wide), unroll=4)
+            sums = lax.fori_loop(0, EB, inner, (zero,) * (per_harm * wide), unroll=8)
             for r in range(per_harm):
                 for q in range(wide):
-                    rows = pl.ds(pl.multiple_of((jt * wide + q) * 8, 8), 8)
-                    out[h * per_harm + r, rows, :] = sums[r * wide + q]
+                    at = (h * per_harm + r) * EB + (jt * wide + q) * 8
+                    out[pl.ds(pl.multiple_of(at, 8), 8), :] = sums[r * wide + q]
             return carry
 
         lax.fori_loop(0, EB // (8 * wide), outer, 0)
@@ -131,28 +138,25 @@
     return lax.dot_general(stack, hot, (((1,), (1,)), ((), ())), preferred_element_type=f32)
 
 
-CHUNK = 16
-
-
-def scatter_blocks(terms, conn, hot, stack, total, first, last):
+def scatter_blocks(terms, conn, hot, stack, total):
     total[...] = jnp.zeros_like(total)
-
-    def outer(c, carry):
-        def body(jj, inner):
+    for c in range(EB // CHUNK):
+
+        def body(jj, carry):
             j = c * CHUNK + jj
-            index = conn[pl.ds(j, 1), :]
             cols = pl.ds(pl.multiple_of(jj * LANES, LANES), LANES)
-            x = terms[:, pl.ds(j, 1), :].reshape(ROWS, LANES)
-            for t, part in enumerate(masked_stack(pieces(x), index, first, last)):
-                stack[t * 48 : t * 48 + 48, cols] = part
-            return inner
-
-        lax.fori_loop(0, CHUNK, body, 0, unroll=2)
-        wide = CHUNK * LANES
-        total[...] += add_up(stack[...], hot[:, pl.ds(pl.multiple_of(c * wide, wide), wide)])
-        return carry
-
-    lax.fori_loop(0, EB // CHUNK, outer, 0)
+            x = terms[pl.ds(j, ROWS, stride=EB), :]
+            first = x.astype(bf16).astype(f32)
+            rest = x - first
+            high = jnp.broadcast_to(conn[pl.ds(j, 1), :] >> 9, (ROWS, LANES))
+            for t in range(PARTS):
+                here = high == t
+                both = jnp.concatenate([jnp.where(here, first, 0.0), jnp.where(here, rest, 0.0)], axis=0)
+                stack[t * 48 : t * 48 + 48, cols] = both.astype(bf16)
+            return carry
+
+        lax.fori_loop(0, CHUNK, body, 0, unroll=CHUNK)
+        total[...] += add_up(stack[...], hot[:, c * CHUNK * LANES : (c + 1) * CHUNK * LANES])
 
 
 def total_tile(total, t):
@@ -195,34 +199,37 @@
 
 def hot_kernel(conn, hot):
     def body(j, carry):
-        hot[:, pl.ds(pl.multiple_of(j * LANES, LANES), LANES)] = one_hot_low(conn[pl.ds(j, 1), :])
+        low = jnp.broadcast_to(conn[pl.ds(j, 1), :] & (WIDE - 1), (WIDE, LANES))
+        one = jnp.where(low == lax.broadcasted_iota(i32, (WIDE, LANES), 0), 1.0, 0.0).astype(bf16)
+        hot[:, pl.ds(pl.multiple_of(j * LANES, LANES), LANES)] = one
         return carry
 
+    lax.fori_loop(0, EB, body, 0, unroll=4)
+
+
+def blocks_kernel(freq, stiff, mass, blocks):
+    def body(i, carry):
+        for h in range(2):
+            blocks[h, i] = stiff[i] + freq[h] * mass[i]
+        return carry
+
     lax.fori_loop(0, EB, body, 0, unroll=2)
 
 
-def own_kernel(rows, conn, got):
-    gather_own(rows, conn, got, (0, 1, 2))
-
-
-def apply_kernel(
-    freq, got_own, low, up, conn, hot, stiff, mass, got, terms, to_low, to_up, stack, total
-):
-    gather_ghosts(got_own, low, up, conn, got, (0, 1, 2))
-    product(freq, got, stiff, mass, terms, 12, 2)
-    scatter_blocks(terms, conn, hot, stack, total, 8, 12)
-    for t in range(2):
-        cols = slice(t * 256, (t + 1) * 256)
-        to_low[:, cols] = total_tile(total, t)
-        to_up[:, cols] = total_tile(total, 2 + t)
-
-
-def sums_kernel(freq, terms, conn, hot, own, mass_row, p, stack, total):
-    scatter_blocks(terms, conn, hot, stack, total, 0, 8)
-    weights = edge_weights(freq, ROWS, 256)
-    for t in range(8):
-        cols = slice(t * 256, (t + 1) * 256)
-        p[:, cols] = total_tile(total, t) + weights * mass_row[0:1, cols] * own[0:24, cols]
+def apply_kernel(with_field, freq, own, low, up, conn, hot, blocks, mass_row, p, to_low, to_up, got, *refs):
+    stack, terms, masked, total = refs[-4:]
+    outs = [(got, 0, ROWS)] + ([(refs[0], ROWS, 8)] if with_field else [])
+    gather_blocks(own, low, up, conn, hot, stack, outs)
+    product(blocks, got, terms, 12, ROWS, 2)
+    scatter_blocks(terms, conn, hot, masked, total)
+    weights = edge_weights(freq, ROWS, WIDE)
+    for t in range(PARTS):
+        sums = total[t * 48 : t * 48 + 24, :] + total[t * 48 + 24 : t * 48 + 48, :]
+        if t < PARTS - 2:
+            cols = slice(t * WIDE, (t + 1) * WIDE)
+            p[:, cols] = sums + weights * mass_row[0:1, cols] * own[0:ROWS, cols]
+        else:
+            (to_low if t == PARTS - 2 else to_up)[...] = sums
 
 
 def finish_kernel(p, lists, from_low, from_up, own, to_low, to_up):
@@ -239,16 +246,15 @@
     pick_listed(own, lists, (to_low, to_up), 3)
 
 
-def quadratic(freq, got, got_rows, stiff, mass):
+def quadratic(blocks, got):
     result = jnp.zeros((8, LANES), f32)
     for h in range(2):
-        weight = freq[h]
         for jt in range(8):
 
             def inner(i, sums):
-                k = stiff[i, jt * 8 : jt * 8 + 8, :] + weight * mass[i, jt * 8 : jt * 8 + 8, :]
+                k = blocks[h, i, jt * 8 : jt * 8 + 8, :]
                 return tuple(
-                    s + k * jnp.broadcast_to(got[i, h * 12 + r : h * 12 + r + 1, :], (8, LANES))
+                    s + k * jnp.broadcast_to(got[pl.ds(i * ROWS + h * 12 + r, 1), :], (8, LANES))
                     for r, s in enumerate(sums)
                 )
 
@@ -259,7 +265,7 @@
                 sums = tuple(s + s for s in sums)
             sums = lax.fori_loop(jt * 8, jt * 8 + 8, inner, sums, unroll=4)
             for r in range(12):
-                mine = got_rows[pl.ds(jt * 8 * ROWS + h * 12 + r, 8, stride=ROWS), :]
+                mine = got[pl.ds(jt * 8 * ROWS + h * 12 + r, 8, stride=ROWS), :]
                 result = result + sums[r] * mine
     return result
 
@@ -271,13 +277,9 @@
     moments[16:24, :] = fold(w[...] * w[...])
 
 
-def third_kernel(
-    freq, got_own, low, up, conn, stiff, mass, mass_row, w, v, early, got_rows, line_out, got
-):
-    gather_ghosts(got_own, low, up, conn, got, (0, 1, 2))
-    for j in range(EB):
-        got_rows[j * ROWS : (j + 1) * ROWS, :] = got[j]
-    last = quadratic(freq, got, got_rows, stiff, mass)
+def third_kernel(freq, v, low, up, conn, hot, blocks, mass_row, w, early, got, line_out, stack):
+    gather_blocks(v, low, up, conn, hot, stack, [(got, 0, ROWS)])
+    last = quadratic(blocks, got)
     weights = edge_weights(freq, ROWS, 256)
     for t in range(8):
         cols = slice(t * 256, (t + 1) * 256)
@@ -290,15 +292,13 @@
     line_out[...] = jnp.broadcast_to(line, (8, LANES))
 
 
-def field_kernel(freq, rows, low, up, conn, stiff, mass, y, got_own, got):
-    gather_own(rows, conn, got_own, (3,))
-    gather_ghosts(got_own, low, up, conn, got, (3,))
-    product(freq, got, stiff, mass, y, 2, 4)
+def field_kernel(blocks, got, y):
+    product(blocks, got, y, 2, 8, 4)
 
 
 def gradients(got_rows, y, node_block, node_shape, energy, out, base):
     for jt in range(8):
-        ys = [y[r, jt * 8 : jt * 8 + 8, :] for r in range(4)]
+        ys = [y[r * EB + jt * 8 : r * EB + jt * 8 + 8, :] for r in range(4)]
         for o in range(6):
             term = jnp.zeros((8, LANES), f32)
             for h in range(2):
@@ -341,7 +341,7 @@
     line = shares[0, 60:61, :]
     for d in range(1, 8):
         line = line + shares[d, 60:61, :]
-    out[...] = jnp.broadcast_to(line, (2, LANES))
+    out[...] = jnp.broadcast_to(line, (32, LANES))
 
 
 def last_kernel(messages, rows, w, v, shares, adjoint, gradient):
@@ -402,64 +402,57 @@
     lists = send_list[0]
     mass_row = edge_mass.reshape(1, EDGES)
     nodes = node_block.reshape(8, LANES)
-    wide = CHUNK * LANES
     ghosts = (arr(ROWS, SLOTS), arr(ROWS, SLOTS))
-    got_shape = arr(EB, ROWS, LANES)
-    flat = lambda x: x.reshape(EB * ROWS, LANES)
+    got_shape = arr(EB * ROWS, LANES)
+    medium = dict(flops=10**9, nbytes=10**7)
 
     rows, to_low, to_up = kernel_call(
-        prep_kernel, "prep", (arr(32, EDGES), arr(32, SLOTS), arr(32, SLOTS)), [VMEM] * 3,
-        flops=10**6, nbytes=10**6,
+        prep_kernel, "prep", (arr(32, EDGES), arr(32, SLOTS), arr(32, SLOTS)), [VMEM] * 3, flops=10**6, nbytes=10**6
     )(adjoint_rhs, forward_field, lists)
-    rim_low, rim_up = exchanged(to_low, to_up)
+    low, up = exchanged(to_low, to_up)
     (hot,) = kernel_call(
-        hot_kernel, "hot", (jax.ShapeDtypeStruct((256, EB * LANES), bf16),), [VMEM], flops=10**7, nbytes=4 * 10**6
+        hot_kernel, "hot", (jax.ShapeDtypeStruct((WIDE, EB * LANES), bf16),), [VMEM], **medium
     )(connectivity)
-
-    def gathered_own(x):
-        return kernel_call(own_kernel, "own", (got_shape,), [VMEM] * 2, flops=10**7, nbytes=10**7)(x, connectivity)[0]
-
-    def applied(x, got_own, low, up):
-        got, terms, to_low, to_up = kernel_call(
-            apply_kernel, "apply", (got_shape, arr(ROWS, EB, LANES)) + ghosts, [SMEM] + [VMEM] * 7,
-            [pltpu.VMEM((4 * 48, wide), bf16), pltpu.VMEM((4 * 48, 256), f32)],
-            flops=10**8, nbytes=10**7,
-        )(frequency, got_own, low, up, connectivity, hot, stiffness, mass_blocks)
+    (blocks,) = kernel_call(blocks_kernel, "blocks", (arr(2, EB, EB, LANES),), [SMEM] + [VMEM] * 2, **medium)(
+        frequency, stiffness, mass_blocks
+    )
+
+    def applied(x, low, up, with_field):
+        count = 2 * PARTS * x.shape[0]
+        p, to_low, to_up, *got = kernel_call(
+            functools.partial(apply_kernel, with_field), "apply",
+            (arr(ROWS, EDGES),) + ghosts + (got_shape,) + (arr(EB * 8, LANES),) * with_field, [SMEM] + [VMEM] * 7,
+            [
+                pltpu.VMEM((count, WIDE), bf16),
+                pltpu.VMEM((ROWS * EB, LANES), f32),
+                pltpu.VMEM((PARTS * 48, CHUNK * LANES), bf16),
+                pltpu.VMEM((PARTS * 48, WIDE), f32),
+            ],
+            **medium,
+        )(frequency, x, low, up, connectivity, hot, blocks, mass_row)
         from_low, from_up = exchanged(to_low, to_up)
-        (p,) = kernel_call(
-            sums_kernel, "sums", (arr(ROWS, EDGES),), [SMEM] + [VMEM] * 5,
-            [pltpu.VMEM((8 * 48, wide), bf16), pltpu.VMEM((8 * 48, 256), f32)], flops=10**8, nbytes=10**7,
-        )(frequency, terms, connectivity, hot, x, mass_row)
         own, to_low, to_up = kernel_call(
             finish_kernel, "finish", (arr(ROWS, EDGES),) + ghosts, [VMEM] * 4, flops=10**7, nbytes=10**6
         )(p, lists, from_low, from_up)
         return got, own, exchanged(to_low, to_up)
 
-    got0, w, (low, up) = applied(rows, gathered_own(rows), rim_low, rim_up)
-    w_own = gathered_own(w)
-    (y,) = kernel_call(
-        field_kernel, "field", (arr(4, EB, LANES),), [SMEM] + [VMEM] * 6,
-        [pltpu.VMEM((EB, 8, LANES), f32), pltpu.VMEM((EB, 8, LANES), f32)],
-        flops=10**8, nbytes=10**7,
-    )(frequency, rows, rim_low, rim_up, connectivity, stiffness, mass_blocks)
-    got1, v, (low, up) = applied(w, w_own, low, up)
-    v_own = gathered_own(v)
+    (got0, got_field), w, (low, up) = applied(rows, low, up, True)
+    (y,) = kernel_call(field_kernel, "field", (arr(4 * EB, LANES),), [VMEM] * 2, **medium)(blocks, got_field)
+    (got1,), v, (low, up) = applied(w, low, up, False)
+    (grads,) = kernel_call(
+        early_gradient_kernel, "early_gradient", (arr(8, 40, LANES),), [VMEM] * 5, [pltpu.VMEM((6, EB, LANES), f32)], **medium
+    )(got0, got1, y, nodes, node_shape)
     (early,) = kernel_call(early_kernel, "early", (arr(24, LANES),), [VMEM] * 2, flops=10**6, nbytes=10**6)(rows, w)
+    got2, line = kernel_call(
+        third_kernel, "third", (got_shape, arr(8, LANES)), [SMEM] + [VMEM] * 9,
+        [pltpu.VMEM((PARTS * 48, WIDE), bf16)], **medium,
+    )(frequency, v, low, up, connectivity, hot, blocks, mass_row, w, early)
     (grads,) = kernel_call(
-        early_gradient_kernel, "early_gradient", (arr(8, 40, LANES),), [VMEM] * 5, [pltpu.VMEM((6, EB, LANES), f32)],
-        flops=10**8, nbytes=10**7,
-    )(flat(got0), flat(got1), y, nodes, node_shape)
-    got2, line = kernel_call(
-        third_kernel, "third", (arr(EB * ROWS, LANES), arr(8, LANES)), [SMEM] + [VMEM] * 10,
-        [pltpu.VMEM((EB, ROWS, LANES), f32)], flops=10**8, nbytes=10**7,
-    )(frequency, v_own, low, up, connectivity, stiffness, mass_blocks, mass_row, w, v, early)
-    (grads,) = kernel_call(
-        late_gradient_kernel, "late_gradient", (arr(8, 64, LANES),), [VMEM] * 6, [pltpu.VMEM((6, EB, LANES), f32)],
-        flops=10**8, nbytes=10**7,
+        late_gradient_kernel, "late_gradient", (arr(8, 64, LANES),), [VMEM] * 6, [pltpu.VMEM((6, EB, LANES), f32)], **medium
     )(grads, got2, y, nodes, node_shape, line)
     shares = lax.all_to_all(grads, "harm", 0, 0, tiled=True)
-    (message,) = kernel_call(message_kernel, "message", (arr(2, LANES),), [VMEM], flops=10**3, nbytes=10**5)(shares)
-    messages = lax.all_to_all(message.reshape(2 * LANES), "mesh", 0, 0, tiled=True).reshape(2, LANES)
+    (message,) = kernel_call(message_kernel, "message", (arr(32, LANES),), [VMEM], flops=10**3, nbytes=10**5)(shares)
+    messages = lax.all_to_all(message.reshape(32 * LANES), "mesh", 0, 0, tiled=True).reshape(32, LANES)
     adjoint, gradient = kernel_call(
         last_kernel, "last", (arr(*adjoint_rhs.shape), arr(6, 3, LANES)), [VMEM] * 5, flops=10**6, nbytes=10**6
     )(messages, rows, w, v, shares)

time: 147 us -> 122 us (0.83)
  Pallas kernels: 73.7 us -> 42.1 us
  waiting for transfers between devices: 0.03 us -> 4.4 us
  blocking collectives: 25.6 us -> 28.1 us
    pallas_call x11 -> x7, Pallas kernels: 65.7 us -> 34.2 us  [the longest x2 22.7 us: applied(): kernel_call(functools.partial(apply_kernel, with_field), 'apply', (arr(RO...]
    ppermute x10, waiting for transfers between devices: 0.03 us -> 4.4 us  [shifted(): lax.ppermute(x, 'mesh', [(i, i + by) for i in range(count) if 0 <= i + by...]
    all_to_all x1, blocking collectives: 13.8 us -> 16.3 us  [per_device(): lax.all_to_all(message.reshape(32 * LANES), 'mesh', 0, 0, tiled=True)]
  transfers between devices with their start and end apart: 10 -> 10, of which waited for: 0 -> 5; matrix products, arithmetic and copies ran while one was open for 0% -> 0% of each run, Pallas kernels for 25% -> 6%
where the time goes in v3:
time: 122 us
  starting transfers between devices  43 us (35%)
  Pallas kernels  42.1 us (35%)
  blocking collectives  28.1 us (23%)
  waiting for transfers between devices  4.4 us (4%)
  local copies, waits for them, and re-layouts  3.16 us (3%)
    ppermute x10, starting transfers between devices, shifted(): lax.ppermute(x, 'mesh', [(i, i + by) for i in range(count) if 0 <= i + by...  43 us
    pallas_call x2, Pallas kernels, applied(): kernel_call(functools.partial(apply_kernel, with_field), 'apply', (arr(RO...  22.7 us
    all_to_all x1, blocking collectives, per_device(): lax.all_to_all(message.reshape(32 * LANES), 'mesh', 0, 0, tiled=True)  16.3 us
    all_to_all x1, blocking collectives, per_device(): shares = lax.all_to_all(grads, 'harm', 0, 0, tiled=True)  11.8 us
    pallas_call x1, Pallas kernels, per_device(): kernel_call(third_kernel, 'third', (got_shape, arr(8, LANES)), [SMEM] + [...  6.65 us
    ppermute x10, waiting for transfers between devices, shifted(): lax.ppermute(x, 'mesh', [(i, i + by) for i in range(count) if 0 <= i + by...  4.4 us
    unnamed x24, local copies, waits for them, and re-layouts  3.16 us
    pallas_call x1, Pallas kernels, per_device(): kernel_call(hot_kernel, 'hot', (jax.ShapeDtypeStruct((WIDE, EB * LANES),...  3.04 us
  transfers between devices with their start and end apart: 10, of which 5 were waited for; matrix products, arithmetic and copies ran while one was open for 0% of the time, Pallas kernels for 6%

profile of v3, /device:TPU:2, one launch (start us, length us, event | category | flops | bytes accessed | tf_op | source)
XLA Modules:
  0.0 121.8 jit_solution(11354251293955468985)
XLA Ops:
  0.6 0.9 copy-done.4
  1.6 0.7 copy-done.6
  2.2 0.8 copy-done.8
  3.0 0.7 prep.1
  3.7 3.8 %collective-permute-start = (f32[32,512]{1,0:T(8,128)S(1)}, f32[32,512]{1,0:T(8,128)S(1)}, u32[]{:S(2)}, u32[]{:S(2)}) collective-permute-start(f32[32,512]{1,0:T(8,128)S(1)} %get-tuple-element.23), channel_id=1, source_target_pairs={{0,8},{8,16},{16,24},{24,32},{32,40},{40,48},{48,56},{56,64},{64,7... | collective-permute-start | bytes 196616 | tf_op jit(solution)/shard_map/ppermute | solution.py:392
  7.5 6.1 %collective-permute-start.1 = (f32[32,512]{1,0:T(8,128)S(1)}, f32[32,512]{1,0:T(8,128)S(1)}, u32[]{:S(2)}, u32[]{:S(2)}) collective-permute-start(f32[32,512]{1,0:T(8,128)S(1)} %get-tuple-element.24), channel_id=1, source_target_pairs={{8,0},{16,8},{24,16},{32,24},{40,32},{48,40},{56,48},{64,56},{72,6... | collective-permute-start | bytes 196616 | tf_op jit(solution)/shard_map/ppermute | solution.py:392
  13.6 0.7 copy-done.2
  14.4 3.0 %hot.1 = bf16[512,8192]{1,0:T(8,128)(2,1)S(1)} custom-call(s32[64,128]{1,0:T(8,128)S(1)} %copy-done.2), custom_call_target="tpu_custom_call" | custom-call | flops 1000000000 | bytes 10000000 | tf_op jit(solution)/shard_map/hot/pallas_call | solution.py:413
  17.5 1.0 blocks.1
  18.6 11.9 %apply.2 = (f32[24,2048]{1,0:T(8,128)S(1)}, f32[24,512]{1,0:T(8,128)S(1)}, f32[24,512]{1,0:T(8,128)S(1)}, f32[1536,128]{1,0:T(8,128)S(1)}, f32[512,128]{1,0:T(8,128)S(1)}) custom-call(f32[2]{0:T(128)S(1)} %copy-done.9, f32[32,2048]{1,0:T(8,128)S(1)} %get-tuple-element.22.own.b_rows.rows, f32[32,512]{1,0:T(8,128)S(1)} %collective-permute-done.low, ...), custom_call_target="tpu_custom_call" | custom-call | flops 1000000000 | bytes 10000000 | tf_op jit(solution)/shard_map/apply/pallas_call | solution.py:422
  30.5 1.9 %collective-permute-start.2 = (f32[24,512]{1,0:T(8,128)S(1)}, f32[24,512]{1,0:T(8,128)S(1)}, u32[]{:S(2)}, u32[]{:S(2)}) collective-permute-start(f32[24,512]{1,0:T(8,128)S(1)} %get-tuple-element.27), channel_id=1, source_target_pairs={{0,8},{8,16},{16,24},{24,32},{32,40},{40,48},{48,56},{56,64},{64,7... | collective-permute-start | bytes 147464 | tf_op jit(solution)/shard_map/ppermute | solution.py:392
  32.4 6.0 %collective-permute-start.3 = (f32[24,512]{1,0:T(8,128)S(1)}, f32[24,512]{1,0:T(8,128)S(1)}, u32[]{:S(2)}, u32[]{:S(2)}) collective-permute-start(f32[24,512]{1,0:T(8,128)S(1)} %get-tuple-element.28), channel_id=1, source_target_pairs={{8,0},{16,8},{24,16},{32,24},{40,32},{48,40},{56,48},{64,56},{72,6... | collective-permute-start | bytes 147464 | tf_op jit(solution)/shard_map/ppermute | solution.py:392
  38.5 0.1 collective-permute-done.2.from_low
  38.6 1.6 %collective-permute-done.3.from_up = f32[24,512]{1,0:T(8,128)S(1)} collective-permute-done((f32[24,512]{1,0:T(8,128)S(1)}, f32[24,512]{1,0:T(8,128)S(1)}, u32[]{:S(2)}, u32[]{:S(2)}) %collective-permute-start.3) | collective-permute-done | bytes 49184 | tf_op jit(solution)/shard_map/ppermute | solution.py:392
  40.2 1.2 finish.2
  41.4 1.9 %collective-permute-start.4 = (f32[24,512]{1,0:T(8,128)S(1)}, f32[24,512]{1,0:T(8,128)S(1)}, u32[]{:S(2)}, u32[]{:S(2)}) collective-permute-start(f32[24,512]{1,0:T(8,128)S(1)} %get-tuple-element.30), channel_id=1, source_target_pairs={{0,8},{8,16},{16,24},{24,32},{32,40},{40,48},{48,56},{56,64},{64,7... | collective-permute-start | bytes 147464 | tf_op jit(solution)/shard_map/ppermute | solution.py:392
  43.3 6.4 %collective-permute-start.5 = (f32[24,512]{1,0:T(8,128)S(1)}, f32[24,512]{1,0:T(8,128)S(1)}, u32[]{:S(2)}, u32[]{:S(2)}) collective-permute-start(f32[24,512]{1,0:T(8,128)S(1)} %get-tuple-element.31), channel_id=1, source_target_pairs={{8,0},{16,8},{24,16},{32,24},{40,32},{48,40},{56,48},{64,56},{72,6... | collective-permute-start | bytes 147464 | tf_op jit(solution)/shard_map/ppermute | solution.py:392
  49.8 1.6 %collective-permute-done.5.up = f32[24,512]{1,0:T(8,128)S(1)} collective-permute-done((f32[24,512]{1,0:T(8,128)S(1)}, f32[24,512]{1,0:T(8,128)S(1)}, u32[]{:S(2)}, u32[]{:S(2)}) %collective-permute-start.5) | collective-permute-done | bytes 49184 | tf_op jit(solution)/shard_map/ppermute | solution.py:392
  51.4 10.9 %apply.3 = (f32[24,2048]{1,0:T(8,128)S(1)}, f32[24,512]{1,0:T(8,128)S(1)}, f32[24,512]{1,0:T(8,128)S(1)}, f32[1536,128]{1,0:T(8,128)S(1)}) custom-call(f32[2]{0:T(128)S(1)} %copy-done.9, f32[24,2048]{1,0:T(8,128)S(1)} %get-tuple-element.29.own.w, f32[24,512]{1,0:T(8,128)S(1)} %collective-permute-done.4.low, f32[24,512]{1,0:T(8,128)S(1)} %collective-permute-done.5.up, ...), custom_call_target="tpu_custom_call" | custom-call | flops 1000000000 | bytes 10000000 | tf_op jit(solution)/shard_map/apply/pallas_call | solution.py:422
  62.3 3.6 %collective-permute-start.6 = (f32[24,512]{1,0:T(8,128)S(1)}, f32[24,512]{1,0:T(8,128)S(1)}, u32[]{:S(2)}, u32[]{:S(2)}) collective-permute-start(f32[24,512]{1,0:T(8,128)S(1)} %get-tuple-element.35), channel_id=1, source_target_pairs={{0,8},{8,16},{16,24},{24,32},{32,40},{40,48},{48,56},{56,64},{64,7... | collective-permute-start | bytes 147464 | tf_op jit(solution)/shard_map/ppermute | solution.py:392
  65.9 4.8 %collective-permute-start.7 = (f32[24,512]{1,0:T(8,128)S(1)}, f32[24,512]{1,0:T(8,128)S(1)}, u32[]{:S(2)}, u32[]{:S(2)}) collective-permute-start(f32[24,512]{1,0:T(8,128)S(1)} %get-tuple-element.36), channel_id=1, source_target_pairs={{8,0},{16,8},{24,16},{32,24},{40,32},{48,40},{56,48},{64,56},{72,6... | collective-permute-start | bytes 147464 | tf_op jit(solution)/shard_map/ppermute | solution.py:392
  70.7 0.7 field.3.y
  71.5 0.9 collective-permute-done.7.from_up
  72.5 1.2 finish.3
  73.7 3.4 %collective-permute-start.8 = (f32[24,512]{1,0:T(8,128)S(1)}, f32[24,512]{1,0:T(8,128)S(1)}, u32[]{:S(2)}, u32[]{:S(2)}) collective-permute-start(f32[24,512]{1,0:T(8,128)S(1)} %get-tuple-element.38), channel_id=1, source_target_pairs={{0,8},{8,16},{16,24},{24,32},{32,40},{40,48},{48,56},{56,64},{64,7... | collective-permute-start | bytes 147464 | tf_op jit(solution)/shard_map/ppermute | solution.py:392
  77.0 5.1 %collective-permute-start.9 = (f32[24,512]{1,0:T(8,128)S(1)}, f32[24,512]{1,0:T(8,128)S(1)}, u32[]{:S(2)}, u32[]{:S(2)}) collective-permute-start(f32[24,512]{1,0:T(8,128)S(1)} %get-tuple-element.39), channel_id=1, source_target_pairs={{8,0},{16,8},{24,16},{32,24},{40,32},{48,40},{56,48},{64,56},{72,6... | collective-permute-start | bytes 147464 | tf_op jit(solution)/shard_map/ppermute | solution.py:392
  82.2 2.5 %early_gradient.1.early = f32[8,40,128]{2,1,0:T(8,128)S(1)} custom-call(f32[1536,128]{1,0:T(8,128)S(1)} %get-tuple-element.25.got0, f32[1536,128]{1,0:T(8,128)S(1)} %get-tuple-element.32.got1, f32[256,128]{1,0:T(8,128)S(1)} %field.3.y, s32[8,128]{1,0:T(8,128)S(1)} %bitcast.15, f32[3,64,1024]{2,1,0:T(8,128)S(1)} %copy-done.10), custom_call_target="tpu_custom_call" | custom-call | flops 1000000000 | bytes 10000000 | tf_op jit(solution)/shard_map/early_gradient/pallas_call | solution.py:442
  84.7 6.7 %third.1 = (f32[1536,128]{1,0:T(8,128)S(1)}, f32[8,128]{1,0:T(8,128)S(1)}) custom-call(f32[2]{0:T(128)S(1)} %copy-done.9, f32[24,2048]{1,0:T(8,128)S(1)} %get-tuple-element.37.v, f32[24,512]{1,0:T(8,128)S(1)} %collective-permute-done.8.low, f32[24,512]{1,0:T(8,128)S(1)} %collective-permute-done.9.up, s32[64,128]{1,0:T(8,128)S(1)} %copy-done.3, ...), custom_call_target="tpu_custom_call" | custom-call | flops 1000000000 | bytes 10000000 | tf_op jit(solution)/shard_map/third/pallas_call | solution.py:446
  91.4 1.3 %late_gradient.1 = f32[8,64,128]{2,1,0:T(8,128)S(1)} custom-call(f32[8,40,128]{2,1,0:T(8,128)S(1)} %early_gradient.1.early, f32[1536,128]{1,0:T(8,128)S(1)} %get-tuple-element.40.got2, f32[256,128]{1,0:T(8,128)S(1)} %field.3.y, s32[8,128]{1,0:T(8,128)S(1)} %bitcast.16, f32[3,64,1024]{2,1,0:T(8,128)S(1)} %copy-done.10, f32[8,128]{1,0:T(8,128)S(1)} %get-tuple-element.41.line), custom_call_target="tpu_custom_call" | custom-call | flops 1000000000 | bytes 10000000 | tf_op jit(solution)/shard_map/late_gradient/pallas_call | solution.py:450
  92.7 11.8 %all_to_all.14.shares = f32[8,64,128]{2,1,0:T(8,128)S(1)} all-to-all(f32[8,64,128]{2,1,0:T(8,128)S(1)} %late_gradient.1), channel_id=1, replica_groups=mesh['mesh'=32,'harm'=8] {'harm'}, dimensions={0} | all-to-all | bytes 524288 | tf_op jit(solution)/shard_map/all_to_all | solution.py:453
  104.5 16.3 %all_to_all.15 = f32[32,128,1]{1,2,0:T(1,128)S(1)} all-to-all(f32[32,128,1]{1,2,0:T(1,128)S(1)} %bitcast.11), channel_id=1, replica_groups=mesh['mesh'=32,'harm'=8] {'mesh'}, dimensions={0} | all-to-all | bytes 32768 | tf_op jit(solution)/shard_map/all_to_all | solution.py:455
  120.8 1.0 last.1
  (28 shorter events, 0.3 us)
Async XLA Ops:
  0.6 0.9 copy-start.4
  1.6 0.7 copy-start.6
  2.2 0.8 copy-start.8
  3.7 14.9 %collective-permute-start = (f32[32,512]{1,0:T(8,128)S(1)}, f32[32,512]{1,0:T(8,128)S(1)}, u32[]{:S(2)}, u32[]{:S(2)}) collective-permute-start(f32[32,512]{1,0:T(8,128)S(1)} %get-tuple-element.23), channel_id=1, source_target_pairs={{0,8},{8,16},{16,24},{24,32},{32,40},{40,48},{48,56},{56,64},{64,7... | collective-permute-start | bytes 196616 | tf_op jit(solution)/shard_map/ppermute | solution.py:392
  7.5 9.9 %copy-start = (f32[64,64,128]{2,1,0:T(8,128)S(1)}, f32[64,64,128]{2,1,0:T(8,128)}, u32[]{:S(2)}) copy-start(f32[64,64,128]{2,1,0:T(8,128)} %stiff.1) | copy-start | bytes 6291460
  7.5 9.9 %copy-start.1 = (f32[64,64,128]{2,1,0:T(8,128)S(1)}, f32[64,64,128]{2,1,0:T(8,128)}, u32[]{:S(2)}) copy-start(f32[64,64,128]{2,1,0:T(8,128)} %mass.1) | copy-start | bytes 6291460
  7.5 11.0 %collective-permute-start.1 = (f32[32,512]{1,0:T(8,128)S(1)}, f32[32,512]{1,0:T(8,128)S(1)}, u32[]{:S(2)}, u32[]{:S(2)}) collective-permute-start(f32[32,512]{1,0:T(8,128)S(1)} %get-tuple-element.24), channel_id=1, source_target_pairs={{8,0},{16,8},{24,16},{32,24},{40,32},{48,40},{56,48},{64,56},{72,6... | collective-permute-start | bytes 196616 | tf_op jit(solution)/shard_map/ppermute | solution.py:392
  13.6 0.8 copy-start.2
  14.4 3.1 %copy-start.9 = (f32[2]{0:T(128)S(1)}, f32[2]{0:T(128)}, u32[]{:S(2)}) copy-start(f32[2]{0:T(128)} %freq.7) | copy-start | bytes 28
  17.5 1.1 copy-start.3
  17.5 1.1 copy-start.5
  18.6 21.6 %copy-start.7 = (s32[1,2,512]{2,1,0:T(2,128)S(1)}, s32[1,2,512]{2,1,0:T(2,128)}, u32[]{:S(2)}) copy-start(s32[1,2,512]{2,1,0:T(2,128)} %param.17) | copy-start | bytes 12292
  30.5 8.1 %collective-permute-start.2 = (f32[24,512]{1,0:T(8,128)S(1)}, f32[24,512]{1,0:T(8,128)S(1)}, u32[]{:S(2)}, u32[]{:S(2)}) collective-permute-start(f32[24,512]{1,0:T(8,128)S(1)} %get-tuple-element.27), channel_id=1, source_target_pairs={{0,8},{8,16},{16,24},{24,32},{32,40},{40,48},{48,56},{56,64},{64,7... | collective-permute-start | bytes 147464 | tf_op jit(solution)/shard_map/ppermute | solution.py:392
  32.4 7.8 %collective-permute-start.3 = (f32[24,512]{1,0:T(8,128)S(1)}, f32[24,512]{1,0:T(8,128)S(1)}, u32[]{:S(2)}, u32[]{:S(2)}) collective-permute-start(f32[24,512]{1,0:T(8,128)S(1)} %get-tuple-element.28), channel_id=1, source_target_pairs={{8,0},{16,8},{24,16},{32,24},{40,32},{48,40},{56,48},{64,56},{72,6... | collective-permute-start | bytes 147464 | tf_op jit(solution)/shard_map/ppermute | solution.py:392
  41.4 8.4 %collective-permute-start.4 = (f32[24,512]{1,0:T(8,128)S(1)}, f32[24,512]{1,0:T(8,128)S(1)}, u32[]{:S(2)}, u32[]{:S(2)}) collective-permute-start(f32[24,512]{1,0:T(8,128)S(1)} %get-tuple-element.30), channel_id=1, source_target_pairs={{0,8},{8,16},{16,24},{24,32},{32,40},{40,48},{48,56},{56,64},{64,7... | collective-permute-start | bytes 147464 | tf_op jit(solution)/shard_map/ppermute | solution.py:392
  43.3 8.1 %collective-permute-start.5 = (f32[24,512]{1,0:T(8,128)S(1)}, f32[24,512]{1,0:T(8,128)S(1)}, u32[]{:S(2)}, u32[]{:S(2)}) collective-permute-start(f32[24,512]{1,0:T(8,128)S(1)} %get-tuple-element.31), channel_id=1, source_target_pairs={{8,0},{16,8},{24,16},{32,24},{40,32},{48,40},{56,48},{64,56},{72,6... | collective-permute-start | bytes 147464 | tf_op jit(solution)/shard_map/ppermute | solution.py:392
  62.3 19.8 %copy-start.10 = (f32[3,64,1024]{2,1,0:T(8,128)S(1)}, f32[3,64,1024]{2,1,0:T(8,128)}, u32[]{:S(2)}) copy-start(f32[3,64,1024]{2,1,0:T(8,128)} %node_shape.3) | copy-start | bytes 2359300
  62.3 19.8 %copy-start.11 = (s32[1024]{0:T(1024)S(1)}, s32[1024]{0:T(1024)}, u32[]{:S(2)}) copy-start(s32[1024]{0:T(1024)} %param.18) | copy-start | bytes 12292
  62.3 9.2 %collective-permute-start.6 = (f32[24,512]{1,0:T(8,128)S(1)}, f32[24,512]{1,0:T(8,128)S(1)}, u32[]{:S(2)}, u32[]{:S(2)}) collective-permute-start(f32[24,512]{1,0:T(8,128)S(1)} %get-tuple-element.35), channel_id=1, source_target_pairs={{0,8},{8,16},{16,24},{24,32},{32,40},{40,48},{48,56},{56,64},{64,7... | collective-permute-start | bytes 147464 | tf_op jit(solution)/shard_map/ppermute | solution.py:392
  65.9 6.5 %collective-permute-start.7 = (f32[24,512]{1,0:T(8,128)S(1)}, f32[24,512]{1,0:T(8,128)S(1)}, u32[]{:S(2)}, u32[]{:S(2)}) collective-permute-start(f32[24,512]{1,0:T(8,128)S(1)} %get-tuple-element.36), channel_id=1, source_target_pairs={{8,0},{16,8},{24,16},{32,24},{40,32},{48,40},{56,48},{64,56},{72,6... | collective-permute-start | bytes 147464 | tf_op jit(solution)/shard_map/ppermute | solution.py:392
  73.7 11.0 %collective-permute-start.8 = (f32[24,512]{1,0:T(8,128)S(1)}, f32[24,512]{1,0:T(8,128)S(1)}, u32[]{:S(2)}, u32[]{:S(2)}) collective-permute-start(f32[24,512]{1,0:T(8,128)S(1)} %get-tuple-element.38), channel_id=1, source_target_pairs={{0,8},{8,16},{16,24},{24,32},{32,40},{40,48},{48,56},{56,64},{64,7... | collective-permute-start | bytes 147464 | tf_op jit(solution)/shard_map/ppermute | solution.py:392
  77.0 7.7 %collective-permute-start.9 = (f32[24,512]{1,0:T(8,128)S(1)}, f32[24,512]{1,0:T(8,128)S(1)}, u32[]{:S(2)}, u32[]{:S(2)}) collective-permute-start(f32[24,512]{1,0:T(8,128)S(1)} %get-tuple-element.39), channel_id=1, source_target_pairs={{8,0},{16,8},{24,16},{32,24},{40,32},{48,40},{56,48},{64,56},{72,6... | collective-permute-start | bytes 147464 | tf_op jit(solution)/shard_map/ppermute | solution.py:392

commit v4 on v3

--- a/solution.py
+++ b/solution.py
@@ -20,9 +20,10 @@
 
 VMEM = pl.BlockSpec(memory_space=pltpu.VMEM)
 SMEM = pl.BlockSpec(memory_space=pltpu.SMEM)
-
-
-def kernel_call(body, name, out, specs, scratch=(), flops=0, nbytes=0):
+HBM = pl.BlockSpec(memory_space=pltpu.HBM)
+
+
+def kernel_call(body, name, out, specs, scratch=(), flops=0, nbytes=0, limit=20):
     return pl.pallas_call(
         body,
         name=name,
@@ -30,7 +31,7 @@
         in_specs=specs,
         out_specs=jax.tree.map(lambda _: VMEM, out),
         scratch_shapes=scratch,
-        compiler_params=pltpu.CompilerParams(vmem_limit_bytes=20 * 2**20),
+        compiler_params=pltpu.CompilerParams(vmem_limit_bytes=limit * 2**20),
         cost_estimate=pl.CostEstimate(flops=flops, bytes_accessed=nbytes, transcendentals=0),
     )
 
@@ -138,7 +139,7 @@
     return lax.dot_general(stack, hot, (((1,), (1,)), ((), ())), preferred_element_type=f32)
 
 
-def scatter_blocks(terms, conn, hot, stack, total):
+def scatter_blocks(terms, conn, hot, stack, total, first, last):
     total[...] = jnp.zeros_like(total)
     for c in range(EB // CHUNK):
 
@@ -146,13 +147,14 @@
             j = c * CHUNK + jj
             cols = pl.ds(pl.multiple_of(jj * LANES, LANES), LANES)
             x = terms[pl.ds(j, ROWS, stride=EB), :]
-            first = x.astype(bf16).astype(f32)
-            rest = x - first
+            head = x.astype(bf16).astype(f32)
+            rest = x - head
             high = jnp.broadcast_to(conn[pl.ds(j, 1), :] >> 9, (ROWS, LANES))
-            for t in range(PARTS):
+            for t in range(first, last):
                 here = high == t
-                both = jnp.concatenate([jnp.where(here, first, 0.0), jnp.where(here, rest, 0.0)], axis=0)
-                stack[t * 48 : t * 48 + 48, cols] = both.astype(bf16)
+                both = jnp.concatenate([jnp.where(here, head, 0.0), jnp.where(here, rest, 0.0)], axis=0)
+                at = (t - first) * 48
+                stack[at : at + 48, cols] = both.astype(bf16)
             return carry
 
         lax.fori_loop(0, CHUNK, body, 0, unroll=CHUNK)
@@ -187,7 +189,15 @@
     return total
 
 
-def prep_kernel(rhs, field, lists, rows, to_low, to_up):
+def prep_kernel(rhs_in, field_in, lists_in, rows, to_low, to_up, rhs, field, lists, sems):
+    copies = [
+        pltpu.make_async_copy(a, b, sems.at[k])
+        for k, (a, b) in enumerate(((rhs_in, rhs), (field_in, field), (lists_in, lists)))
+    ]
+    for copy in copies:
+        copy.start()
+    for copy in copies:
+        copy.wait()
     for h in range(2):
         for o in range(6):
             at = h * 12 + o * 2
@@ -200,8 +210,9 @@
 def hot_kernel(conn, hot):
     def body(j, carry):
         low = jnp.broadcast_to(conn[pl.ds(j, 1), :] & (WIDE - 1), (WIDE, LANES))
-        one = jnp.where(low == lax.broadcasted_iota(i32, (WIDE, LANES), 0), 1.0, 0.0).astype(bf16)
-        hot[:, pl.ds(pl.multiple_of(j * LANES, LANES), LANES)] = one
+        one = jnp.where(low == lax.broadcasted_iota(i32, (WIDE, LANES), 0), 1.0, 0.0)
+        cols = pl.ds(pl.multiple_of(j * LANES, LANES), LANES)
+        hot[:, cols] = one.astype(bf16)
         return carry
 
     lax.fori_loop(0, EB, body, 0, unroll=4)
@@ -216,20 +227,22 @@
     lax.fori_loop(0, EB, body, 0, unroll=2)
 
 
-def apply_kernel(with_field, freq, own, low, up, conn, hot, blocks, mass_row, p, to_low, to_up, got, *refs):
-    stack, terms, masked, total = refs[-4:]
+def apply_kernel(with_field, own, low, up, conn, hot, blocks, terms, to_low, to_up, got, *refs):
+    stack, masked, total = refs[-3:]
     outs = [(got, 0, ROWS)] + ([(refs[0], ROWS, 8)] if with_field else [])
     gather_blocks(own, low, up, conn, hot, stack, outs)
     product(blocks, got, terms, 12, ROWS, 2)
-    scatter_blocks(terms, conn, hot, masked, total)
+    scatter_blocks(terms, conn, hot, masked, total, 4, 6)
+    to_low[...] = total_tile(total, 0)
+    to_up[...] = total_tile(total, 1)
+
+
+def sums_kernel(freq, terms, conn, hot, own, mass_row, p, masked, total):
+    scatter_blocks(terms, conn, hot, masked, total, 0, 4)
     weights = edge_weights(freq, ROWS, WIDE)
-    for t in range(PARTS):
-        sums = total[t * 48 : t * 48 + 24, :] + total[t * 48 + 24 : t * 48 + 48, :]
-        if t < PARTS - 2:
-            cols = slice(t * WIDE, (t + 1) * WIDE)
-            p[:, cols] = sums + weights * mass_row[0:1, cols] * own[0:ROWS, cols]
-        else:
-            (to_low if t == PARTS - 2 else to_up)[...] = sums
+    for t in range(4):
+        cols = slice(t * WIDE, (t + 1) * WIDE)
+        p[:, cols] = total_tile(total, t) + weights * mass_row[0:1, cols] * own[0:ROWS, cols]
 
 
 def finish_kernel(p, lists, from_low, from_up, own, to_low, to_up):
@@ -407,7 +420,14 @@
     medium = dict(flops=10**9, nbytes=10**7)
 
     rows, to_low, to_up = kernel_call(
-        prep_kernel, "prep", (arr(32, EDGES), arr(32, SLOTS), arr(32, SLOTS)), [VMEM] * 3, flops=10**6, nbytes=10**6
+        prep_kernel, "prep", (arr(32, EDGES), arr(32, SLOTS), arr(32, SLOTS)), [HBM] * 3,
+        [
+            pltpu.VMEM(adjoint_rhs.shape, f32),
+            pltpu.VMEM(forward_field.shape, f32),
+            pltpu.VMEM(lists.shape, i32),
+            pltpu.SemaphoreType.DMA((3,)),
+        ],
+        flops=10**6, nbytes=10**6, limit=62,
     )(adjoint_rhs, forward_field, lists)
     low, up = exchanged(to_low, to_up)
     (hot,) = kernel_call(
@@ -419,18 +439,21 @@
 
     def applied(x, low, up, with_field):
         count = 2 * PARTS * x.shape[0]
-        p, to_low, to_up, *got = kernel_call(
+        terms, to_low, to_up, *got = kernel_call(
             functools.partial(apply_kernel, with_field), "apply",
-            (arr(ROWS, EDGES),) + ghosts + (got_shape,) + (arr(EB * 8, LANES),) * with_field, [SMEM] + [VMEM] * 7,
+            (arr(ROWS * EB, LANES),) + ghosts + (got_shape,) + (arr(EB * 8, LANES),) * with_field, [VMEM] * 6,
             [
                 pltpu.VMEM((count, WIDE), bf16),
-                pltpu.VMEM((ROWS * EB, LANES), f32),
-                pltpu.VMEM((PARTS * 48, CHUNK * LANES), bf16),
-                pltpu.VMEM((PARTS * 48, WIDE), f32),
+                pltpu.VMEM((2 * 48, CHUNK * LANES), bf16),
+                pltpu.VMEM((2 * 48, WIDE), f32),
             ],
             **medium,
-        )(frequency, x, low, up, connectivity, hot, blocks, mass_row)
+        )(x, low, up, connectivity, hot, blocks)
         from_low, from_up = exchanged(to_low, to_up)
+        (p,) = kernel_call(
+            sums_kernel, "sums", (arr(ROWS, EDGES),), [SMEM] + [VMEM] * 5,
+            [pltpu.VMEM((4 * 48, CHUNK * LANES), bf16), pltpu.VMEM((4 * 48, WIDE), f32)], **medium,
+        )(frequency, terms, connectivity, hot, x, mass_row)
         own, to_low, to_up = kernel_call(
             finish_kernel, "finish", (arr(ROWS, EDGES),) + ghosts, [VMEM] * 4, flops=10**7, nbytes=10**6
         )(p, lists, from_low, from_up)

time: 122 us -> 123 us (level)
  Pallas kernels: 42.1 us -> 49.4 us
  waiting for transfers between devices: 4.4 us -> 0.95 us
  local copies, waits for them, and re-layouts: 3.16 us -> 0.81 us
    pallas_call x0 -> x2, Pallas kernels: none -> 7.66 us  [applied(): kernel_call(sums_kernel, 'sums', (arr(ROWS, EDGES),), [SMEM] + [VMEM] * 5...]
    ppermute x10, waiting for transfers between devices: 4.4 us -> 0.95 us  [shifted(): lax.ppermute(x, 'mesh', [(i, i + by) for i in range(count) if 0 <= i + by...]
    unnamed x24 -> x20, local copies, waits for them, and re-layouts: 3.16 us -> 0.81 us
    pallas_call x2, Pallas kernels: 22.7 us -> 20.6 us  [applied(): kernel_call(functools.partial(apply_kernel, with_field), 'apply', (arr(RO...]
    pallas_call x1, Pallas kernels: 0.66 us -> 2.26 us  [per_device(): kernel_call(prep_kernel, 'prep', (arr(32, EDGES), arr(32, SLOTS), arr(32,...]
  transfers between devices with their start and end apart: 10 -> 10, of which waited for: 5 -> 1; matrix products, arithmetic and copies ran while one was open for 0% -> 0% of each run, Pallas kernels for 6% -> 12%
where the time goes in v4:
time: 123 us
  Pallas kernels  49.4 us (40%)
  starting transfers between devices  42.2 us (34%)
  blocking collectives  28.3 us (23%)
    ppermute x10, starting transfers between devices, shifted(): lax.ppermute(x, 'mesh', [(i, i + by) for i in range(count) if 0 <= i + by...  42.2 us
    pallas_call x2, Pallas kernels, applied(): kernel_call(functools.partial(apply_kernel, with_field), 'apply', (arr(RO...  20.6 us
    all_to_all x1, blocking collectives, per_device(): lax.all_to_all(message.reshape(32 * LANES), 'mesh', 0, 0, tiled=True)  16.4 us
    all_to_all x1, blocking collectives, per_device(): shares = lax.all_to_all(grads, 'harm', 0, 0, tiled=True)  11.8 us
    pallas_call x2, Pallas kernels, applied(): kernel_call(sums_kernel, 'sums', (arr(ROWS, EDGES),), [SMEM] + [VMEM] * 5...  7.66 us
    pallas_call x1, Pallas kernels, per_device(): kernel_call(third_kernel, 'third', (got_shape, arr(8, LANES)), [SMEM] + [...  6.57 us
    pallas_call x1, Pallas kernels, per_device(): kernel_call(hot_kernel, 'hot', (jax.ShapeDtypeStruct((WIDE, EB * LANES),...  3.18 us
    pallas_call x1, Pallas kernels, per_device(): kernel_call(early_gradient_kernel, 'early_gradient', (arr(8, 40, LANES),)...  2.54 us
  transfers between devices with their start and end apart: 10, of which 1 were waited for; matrix products, arithmetic and copies ran while one was open for 0% of the time, Pallas kernels for 12%

profile of v4, /device:TPU:2, one launch (start us, length us, event | category | flops | bytes accessed | tf_op | source)
XLA Modules:
  0.0 122.6 jit_solution(8906509574568111554)
XLA Ops:
  0.6 2.3 %prep.1 = (f32[32,2048]{1,0:T(8,128)}, f32[32,512]{1,0:T(8,128)}, f32[32,512]{1,0:T(8,128)}) custom-call(f32[2,6,2,2048]{3,2,1,0:T(2,128)} %rhs_in.1, f32[2,2,2048]{2,1,0:T(2,128)} %field_in.1, s32[2,512]{1,0:T(2,128)} %bitcast.12), custom_call_target="tpu_custom_call" | custom-call | flops 1000000 | bytes 1000000 | tf_op jit(solution)/shard_map/prep/pallas_call | solution.py:422
  2.9 3.8 %collective-permute-start = (f32[32,512]{1,0:T(8,128)}, f32[32,512]{1,0:T(8,128)S(1)}, u32[]{:S(2)}, u32[]{:S(2)}) collective-permute-start(f32[32,512]{1,0:T(8,128)} %get-tuple-element.23), channel_id=1, source_target_pairs={{0,8},{8,16},{16,24},{24,32},{32,40},{40,48},{48,56},{56,64},{64,7... | collective-permute-start | bytes 196616 | tf_op jit(solution)/shard_map/ppermute | solution.py:405
  6.7 0.0 copy-start.2
  6.8 6.1 %collective-permute-start.1 = (f32[32,512]{1,0:T(8,128)}, f32[32,512]{1,0:T(8,128)S(1)}, u32[]{:S(2)}, u32[]{:S(2)}) collective-permute-start(f32[32,512]{1,0:T(8,128)} %get-tuple-element.24), channel_id=1, source_target_pairs={{8,0},{16,8},{24,16},{32,24},{40,32},{48,40},{56,48},{64,56},{72,6... | collective-permute-start | bytes 196616 | tf_op jit(solution)/shard_map/ppermute | solution.py:405
  12.9 0.0 copy-start.3
  12.9 0.7 copy-done.3
  13.6 3.2 %hot.1 = bf16[512,8192]{1,0:T(8,128)(2,1)S(1)} custom-call(s32[64,128]{1,0:T(8,128)S(1)} %copy-done.3), custom_call_target="tpu_custom_call" | custom-call | flops 1000000000 | bytes 10000000 | tf_op jit(solution)/shard_map/hot/pallas_call | solution.py:433
  16.9 1.0 blocks.1
  18.0 10.9 %apply.2 = (f32[1536,128]{1,0:T(8,128)S(1)}, f32[24,512]{1,0:T(8,128)S(1)}, f32[24,512]{1,0:T(8,128)S(1)}, f32[1536,128]{1,0:T(8,128)S(1)}, f32[512,128]{1,0:T(8,128)S(1)}) custom-call(f32[32,2048]{1,0:T(8,128)S(1)} %copy-done, f32[32,512]{1,0:T(8,128)S(1)} %collective-permute-done.low, f32[32,512]{1,0:T(8,128)S(1)} %collective-permute-done.1.up, ...), custom_call_target="tpu_custom_call" | custom-call | flops 1000000000 | bytes 10000000 | tf_op jit(solution)/shard_map/apply/pallas_call | solution.py:442
  28.9 1.9 %collective-permute-start.2 = (f32[24,512]{1,0:T(8,128)S(1)}, f32[24,512]{1,0:T(8,128)S(1)}, u32[]{:S(2)}, u32[]{:S(2)}) collective-permute-start(f32[24,512]{1,0:T(8,128)S(1)} %get-tuple-element.27), channel_id=1, source_target_pairs={{0,8},{8,16},{16,24},{24,32},{32,40},{40,48},{48,56},{56,64},{64,7... | collective-permute-start | bytes 147464 | tf_op jit(solution)/shard_map/ppermute | solution.py:405
  30.8 6.0 %collective-permute-start.3 = (f32[24,512]{1,0:T(8,128)S(1)}, f32[24,512]{1,0:T(8,128)S(1)}, u32[]{:S(2)}, u32[]{:S(2)}) collective-permute-start(f32[24,512]{1,0:T(8,128)S(1)} %get-tuple-element.28), channel_id=1, source_target_pairs={{8,0},{16,8},{24,16},{32,24},{40,32},{48,40},{56,48},{64,56},{72,6... | collective-permute-start | bytes 147464 | tf_op jit(solution)/shard_map/ppermute | solution.py:405
  36.8 3.9 %sums.2.p = f32[24,2048]{1,0:T(8,128)S(1)} custom-call(f32[2]{0:T(128)S(1)} %copy-done.7, f32[1536,128]{1,0:T(8,128)S(1)} %get-tuple-element.26.terms, s32[64,128]{1,0:T(8,128)S(1)} %copy-done.4, bf16[512,8192]{1,0:T(8,128)(2,1)S(1)} %hot.1, f32[32,2048]{1,0:T(8,128)S(1)} %copy-done, f32[1,2048]{1,0:T(1,128)S(1)} %bitcast.7), custom_call_target="tpu_custom_call" | custom-call | flops 1000000000 | bytes 10000000 | tf_op jit(solution)/shard_map/sums/pallas_call | solution.py:453
  40.7 1.2 finish.2
  41.9 1.9 %collective-permute-start.4 = (f32[24,512]{1,0:T(8,128)S(1)}, f32[24,512]{1,0:T(8,128)S(1)}, u32[]{:S(2)}, u32[]{:S(2)}) collective-permute-start(f32[24,512]{1,0:T(8,128)S(1)} %get-tuple-element.30), channel_id=1, source_target_pairs={{0,8},{8,16},{16,24},{24,32},{32,40},{40,48},{48,56},{56,64},{64,7... | collective-permute-start | bytes 147464 | tf_op jit(solution)/shard_map/ppermute | solution.py:405
  43.9 6.0 %collective-permute-start.5 = (f32[24,512]{1,0:T(8,128)S(1)}, f32[24,512]{1,0:T(8,128)S(1)}, u32[]{:S(2)}, u32[]{:S(2)}) collective-permute-start(f32[24,512]{1,0:T(8,128)S(1)} %get-tuple-element.31), channel_id=1, source_target_pairs={{8,0},{16,8},{24,16},{32,24},{40,32},{48,40},{56,48},{64,56},{72,6... | collective-permute-start | bytes 147464 | tf_op jit(solution)/shard_map/ppermute | solution.py:405
  49.9 0.7 field.1.y
  50.6 0.1 early.1
  50.7 0.9 collective-permute-done.5.up
  51.6 9.8 %apply.3 = (f32[1536,128]{1,0:T(8,128)S(1)}, f32[24,512]{1,0:T(8,128)S(1)}, f32[24,512]{1,0:T(8,128)S(1)}, f32[1536,128]{1,0:T(8,128)S(1)}) custom-call(f32[24,2048]{1,0:T(8,128)S(1)} %get-tuple-element.29.own.w, f32[24,512]{1,0:T(8,128)S(1)} %collective-permute-done.4.low, f32[24,512]{1,0:T(8,128)S(1)} %collective-permute-done.5.up, ...), custom_call_target="tpu_custom_call" | custom-call | flops 1000000000 | bytes 10000000 | tf_op jit(solution)/shard_map/apply/pallas_call | solution.py:442
  61.4 1.9 %collective-permute-start.6 = (f32[24,512]{1,0:T(8,128)S(1)}, f32[24,512]{1,0:T(8,128)S(1)}, u32[]{:S(2)}, u32[]{:S(2)}) collective-permute-start(f32[24,512]{1,0:T(8,128)S(1)} %get-tuple-element.35), channel_id=1, source_target_pairs={{0,8},{8,16},{16,24},{24,32},{32,40},{40,48},{48,56},{56,64},{64,7... | collective-permute-start | bytes 147464 | tf_op jit(solution)/shard_map/ppermute | solution.py:405
  63.4 6.5 %collective-permute-start.7 = (f32[24,512]{1,0:T(8,128)S(1)}, f32[24,512]{1,0:T(8,128)S(1)}, u32[]{:S(2)}, u32[]{:S(2)}) collective-permute-start(f32[24,512]{1,0:T(8,128)S(1)} %get-tuple-element.36), channel_id=1, source_target_pairs={{8,0},{16,8},{24,16},{32,24},{40,32},{48,40},{56,48},{64,56},{72,6... | collective-permute-start | bytes 147464 | tf_op jit(solution)/shard_map/ppermute | solution.py:405
  69.9 0.0 copy-start.9
  69.9 3.8 %sums.3.p = f32[24,2048]{1,0:T(8,128)S(1)} custom-call(f32[2]{0:T(128)S(1)} %copy-done.7, f32[1536,128]{1,0:T(8,128)S(1)} %get-tuple-element.34.terms, s32[64,128]{1,0:T(8,128)S(1)} %copy-done.4, bf16[512,8192]{1,0:T(8,128)(2,1)S(1)} %hot.1, f32[24,2048]{1,0:T(8,128)S(1)} %get-tuple-element.29.own.w, f32[1,2048]{1,0:T(1,128)S(1)} %bitcast.8), custom_call_target="tpu_custom_call" | custom-call | flops 1000000000 | bytes 10000000 | tf_op jit(solution)/shard_map/sums/pallas_call | solution.py:453
  73.7 1.2 finish.3
  74.9 1.9 %collective-permute-start.8 = (f32[24,512]{1,0:T(8,128)S(1)}, f32[24,512]{1,0:T(8,128)S(1)}, u32[]{:S(2)}, u32[]{:S(2)}) collective-permute-start(f32[24,512]{1,0:T(8,128)S(1)} %get-tuple-element.38), channel_id=1, source_target_pairs={{0,8},{8,16},{16,24},{24,32},{32,40},{40,48},{48,56},{56,64},{64,7... | collective-permute-start | bytes 147464 | tf_op jit(solution)/shard_map/ppermute | solution.py:405
  76.9 6.0 %collective-permute-start.9 = (f32[24,512]{1,0:T(8,128)S(1)}, f32[24,512]{1,0:T(8,128)S(1)}, u32[]{:S(2)}, u32[]{:S(2)}) collective-permute-start(f32[24,512]{1,0:T(8,128)S(1)} %get-tuple-element.39), channel_id=1, source_target_pairs={{8,0},{16,8},{24,16},{32,24},{40,32},{48,40},{56,48},{64,56},{72,6... | collective-permute-start | bytes 147464 | tf_op jit(solution)/shard_map/ppermute | solution.py:405
  82.9 2.5 %early_gradient.1.early = f32[8,40,128]{2,1,0:T(8,128)S(1)} custom-call(f32[1536,128]{1,0:T(8,128)S(1)} %get-tuple-element.25.got0, f32[1536,128]{1,0:T(8,128)S(1)} %get-tuple-element.32.got1, f32[256,128]{1,0:T(8,128)S(1)} %field.1.y, s32[8,128]{1,0:T(8,128)S(1)} %bitcast.15, f32[3,64,1024]{2,1,0:T(8,128)S(1)} %copy-done.8), custom_call_target="tpu_custom_call" | custom-call | flops 1000000000 | bytes 10000000 | tf_op jit(solution)/shard_map/early_gradient/pallas_call | solution.py:465
  85.5 6.6 %third.1 = (f32[1536,128]{1,0:T(8,128)S(1)}, f32[8,128]{1,0:T(8,128)S(1)}) custom-call(f32[2]{0:T(128)S(1)} %copy-done.7, f32[24,2048]{1,0:T(8,128)S(1)} %get-tuple-element.37.v, f32[24,512]{1,0:T(8,128)S(1)} %collective-permute-done.8.low, f32[24,512]{1,0:T(8,128)S(1)} %collective-permute-done.9.up, s32[64,128]{1,0:T(8,128)S(1)} %copy-done.4, ...), custom_call_target="tpu_custom_call" | custom-call | flops 1000000000 | bytes 10000000 | tf_op jit(solution)/shard_map/third/pallas_call | solution.py:469
  92.1 1.3 %late_gradient.1 = f32[8,64,128]{2,1,0:T(8,128)S(1)} custom-call(f32[8,40,128]{2,1,0:T(8,128)S(1)} %early_gradient.1.early, f32[1536,128]{1,0:T(8,128)S(1)} %get-tuple-element.40.got2, f32[256,128]{1,0:T(8,128)S(1)} %field.1.y, s32[8,128]{1,0:T(8,128)S(1)} %bitcast.16, f32[3,64,1024]{2,1,0:T(8,128)S(1)} %copy-done.8, f32[8,128]{1,0:T(8,128)S(1)} %get-tuple-element.41.line), custom_call_target="tpu_custom_call" | custom-call | flops 1000000000 | bytes 10000000 | tf_op jit(solution)/shard_map/late_gradient/pallas_call | solution.py:473
  93.4 11.8 %all_to_all.14.shares = f32[8,64,128]{2,1,0:T(8,128)S(1)} all-to-all(f32[8,64,128]{2,1,0:T(8,128)S(1)} %late_gradient.1), channel_id=1, replica_groups=mesh['mesh'=32,'harm'=8] {'harm'}, dimensions={0} | all-to-all | bytes 524288 | tf_op jit(solution)/shard_map/all_to_all | solution.py:476
  105.2 16.4 %all_to_all.15 = f32[32,128,1]{1,2,0:T(1,128)S(1)} all-to-all(f32[32,128,1]{1,2,0:T(1,128)S(1)} %bitcast.11), channel_id=1, replica_groups=mesh['mesh'=32,'harm'=8] {'mesh'}, dimensions={0} | all-to-all | bytes 32768 | tf_op jit(solution)/shard_map/all_to_all | solution.py:478
  121.6 1.0 last.1
  (26 shorter events, 0.1 us)
Async XLA Ops:
  2.9 15.0 %collective-permute-start = (f32[32,512]{1,0:T(8,128)}, f32[32,512]{1,0:T(8,128)S(1)}, u32[]{:S(2)}, u32[]{:S(2)}) collective-permute-start(f32[32,512]{1,0:T(8,128)} %get-tuple-element.23), channel_id=1, source_target_pairs={{0,8},{8,16},{16,24},{24,32},{32,40},{40,48},{48,56},{56,64},{64,7... | collective-permute-start | bytes 196616 | tf_op jit(solution)/shard_map/ppermute | solution.py:405
  6.7 10.1 %copy-start.1 = (f32[64,64,128]{2,1,0:T(8,128)S(1)}, f32[64,64,128]{2,1,0:T(8,128)}, u32[]{:S(2)}) copy-start(f32[64,64,128]{2,1,0:T(8,128)} %stiff.1) | copy-start | bytes 6291460
  6.7 10.1 %copy-start.2 = (f32[64,64,128]{2,1,0:T(8,128)S(1)}, f32[64,64,128]{2,1,0:T(8,128)}, u32[]{:S(2)}) copy-start(f32[64,64,128]{2,1,0:T(8,128)} %mass.1) | copy-start | bytes 6291460
  6.8 11.2 %collective-permute-start.1 = (f32[32,512]{1,0:T(8,128)}, f32[32,512]{1,0:T(8,128)S(1)}, u32[]{:S(2)}, u32[]{:S(2)}) collective-permute-start(f32[32,512]{1,0:T(8,128)} %get-tuple-element.24), channel_id=1, source_target_pairs={{8,0},{16,8},{24,16},{32,24},{40,32},{48,40},{56,48},{64,56},{72,6... | collective-permute-start | bytes 196616 | tf_op jit(solution)/shard_map/ppermute | solution.py:405
  12.9 0.8 copy-start.3
  13.6 3.2 %copy-start.7 = (f32[2]{0:T(128)S(1)}, f32[2]{0:T(128)}, u32[]{:S(2)}) copy-start(f32[2]{0:T(128)} %freq.7) | copy-start | bytes 28
  16.8 1.1 copy-start
  16.8 1.1 copy-start.4
  18.0 18.9 %copy-start.5 = (f32[2048]{0:T(1024)S(1)}, f32[2048]{0:T(1024)}, u32[]{:S(2)}) copy-start(f32[2048]{0:T(1024)} %param.15) | copy-start | bytes 24580
  28.9 11.9 %collective-permute-start.2 = (f32[24,512]{1,0:T(8,128)S(1)}, f32[24,512]{1,0:T(8,128)S(1)}, u32[]{:S(2)}, u32[]{:S(2)}) collective-permute-start(f32[24,512]{1,0:T(8,128)S(1)} %get-tuple-element.27), channel_id=1, source_target_pairs={{0,8},{8,16},{16,24},{24,32},{32,40},{40,48},{48,56},{56,64},{64,7... | collective-permute-start | bytes 147464 | tf_op jit(solution)/shard_map/ppermute | solution.py:405
  30.8 10.0 %collective-permute-start.3 = (f32[24,512]{1,0:T(8,128)S(1)}, f32[24,512]{1,0:T(8,128)S(1)}, u32[]{:S(2)}, u32[]{:S(2)}) collective-permute-start(f32[24,512]{1,0:T(8,128)S(1)} %get-tuple-element.28), channel_id=1, source_target_pairs={{8,0},{16,8},{24,16},{32,24},{40,32},{48,40},{56,48},{64,56},{72,6... | collective-permute-start | bytes 147464 | tf_op jit(solution)/shard_map/ppermute | solution.py:405
  36.8 3.9 %copy-start.6 = (s32[1,2,512]{2,1,0:T(2,128)S(1)}, s32[1,2,512]{2,1,0:T(2,128)}, u32[]{:S(2)}) copy-start(s32[1,2,512]{2,1,0:T(2,128)} %param.17) | copy-start | bytes 12292
  41.9 8.8 %collective-permute-start.4 = (f32[24,512]{1,0:T(8,128)S(1)}, f32[24,512]{1,0:T(8,128)S(1)}, u32[]{:S(2)}, u32[]{:S(2)}) collective-permute-start(f32[24,512]{1,0:T(8,128)S(1)} %get-tuple-element.30), channel_id=1, source_target_pairs={{0,8},{8,16},{16,24},{24,32},{32,40},{40,48},{48,56},{56,64},{64,7... | collective-permute-start | bytes 147464 | tf_op jit(solution)/shard_map/ppermute | solution.py:405
  43.9 7.8 %collective-permute-start.5 = (f32[24,512]{1,0:T(8,128)S(1)}, f32[24,512]{1,0:T(8,128)S(1)}, u32[]{:S(2)}, u32[]{:S(2)}) collective-permute-start(f32[24,512]{1,0:T(8,128)S(1)} %get-tuple-element.31), channel_id=1, source_target_pairs={{8,0},{16,8},{24,16},{32,24},{40,32},{48,40},{56,48},{64,56},{72,6... | collective-permute-start | bytes 147464 | tf_op jit(solution)/shard_map/ppermute | solution.py:405
  61.4 12.3 %collective-permute-start.6 = (f32[24,512]{1,0:T(8,128)S(1)}, f32[24,512]{1,0:T(8,128)S(1)}, u32[]{:S(2)}, u32[]{:S(2)}) collective-permute-start(f32[24,512]{1,0:T(8,128)S(1)} %get-tuple-element.35), channel_id=1, source_target_pairs={{0,8},{8,16},{16,24},{24,32},{32,40},{40,48},{48,56},{56,64},{64,7... | collective-permute-start | bytes 147464 | tf_op jit(solution)/shard_map/ppermute | solution.py:405
  63.4 10.4 %collective-permute-start.7 = (f32[24,512]{1,0:T(8,128)S(1)}, f32[24,512]{1,0:T(8,128)S(1)}, u32[]{:S(2)}, u32[]{:S(2)}) collective-permute-start(f32[24,512]{1,0:T(8,128)S(1)} %get-tuple-element.36), channel_id=1, source_target_pairs={{8,0},{16,8},{24,16},{32,24},{40,32},{48,40},{56,48},{64,56},{72,6... | collective-permute-start | bytes 147464 | tf_op jit(solution)/shard_map/ppermute | solution.py:405
  69.9 13.0 %copy-start.8 = (f32[3,64,1024]{2,1,0:T(8,128)S(1)}, f32[3,64,1024]{2,1,0:T(8,128)}, u32[]{:S(2)}) copy-start(f32[3,64,1024]{2,1,0:T(8,128)} %node_shape.3) | copy-start | bytes 2359300
  69.9 13.0 %copy-start.9 = (s32[1024]{0:T(1024)S(1)}, s32[1024]{0:T(1024)}, u32[]{:S(2)}) copy-start(s32[1024]{0:T(1024)} %param.18) | copy-start | bytes 12292
  74.9 10.5 %collective-permute-start.8 = (f32[24,512]{1,0:T(8,128)S(1)}, f32[24,512]{1,0:T(8,128)S(1)}, u32[]{:S(2)}, u32[]{:S(2)}) collective-permute-start(f32[24,512]{1,0:T(8,128)S(1)} %get-tuple-element.38), channel_id=1, source_target_pairs={{0,8},{8,16},{16,24},{24,32},{32,40},{40,48},{48,56},{56,64},{64,7... | collective-permute-start | bytes 147464 | tf_op jit(solution)/shard_map/ppermute | solution.py:405
  76.9 8.6 %collective-permute-start.9 = (f32[24,512]{1,0:T(8,128)S(1)}, f32[24,512]{1,0:T(8,128)S(1)}, u32[]{:S(2)}, u32[]{:S(2)}) collective-permute-start(f32[24,512]{1,0:T(8,128)S(1)} %get-tuple-element.39), channel_id=1, source_target_pairs={{8,0},{16,8},{24,16},{32,24},{40,32},{48,40},{56,48},{64,56},{72,6... | collective-permute-start | bytes 147464 | tf_op jit(solution)/shard_map/ppermute | solution.py:405

commit v5 on v3

--- a/solution.py
+++ b/solution.py
@@ -20,9 +20,10 @@
 
 VMEM = pl.BlockSpec(memory_space=pltpu.VMEM)
 SMEM = pl.BlockSpec(memory_space=pltpu.SMEM)
-
-
-def kernel_call(body, name, out, specs, scratch=(), flops=0, nbytes=0):
+HBM = pl.BlockSpec(memory_space=pltpu.HBM)
+
+
+def kernel_call(body, name, out, specs, scratch=(), flops=0, nbytes=0, limit=20):
     return pl.pallas_call(
         body,
         name=name,
@@ -30,7 +31,7 @@
         in_specs=specs,
         out_specs=jax.tree.map(lambda _: VMEM, out),
         scratch_shapes=scratch,
-        compiler_params=pltpu.CompilerParams(vmem_limit_bytes=20 * 2**20),
+        compiler_params=pltpu.CompilerParams(vmem_limit_bytes=limit * 2**20),
         cost_estimate=pl.CostEstimate(flops=flops, bytes_accessed=nbytes, transcendentals=0),
     )
 
@@ -187,7 +188,15 @@
     return total
 
 
-def prep_kernel(rhs, field, lists, rows, to_low, to_up):
+def prep_kernel(rhs_in, field_in, lists_in, rows, to_low, to_up, rhs, field, lists, sems):
+    copies = [
+        pltpu.make_async_copy(a, b, sems.at[k])
+        for k, (a, b) in enumerate(((rhs_in, rhs), (field_in, field), (lists_in, lists)))
+    ]
+    for copy in copies:
+        copy.start()
+    for copy in copies:
+        copy.wait()
     for h in range(2):
         for o in range(6):
             at = h * 12 + o * 2
@@ -198,13 +207,22 @@
 
 
 def hot_kernel(conn, hot):
+    half = WIDE // 2
+
     def body(j, carry):
-        low = jnp.broadcast_to(conn[pl.ds(j, 1), :] & (WIDE - 1), (WIDE, LANES))
-        one = jnp.where(low == lax.broadcasted_iota(i32, (WIDE, LANES), 0), 1.0, 0.0).astype(bf16)
-        hot[:, pl.ds(pl.multiple_of(j * LANES, LANES), LANES)] = one
+        index = conn[pl.ds(j, 1), :]
+        cols = pl.ds(pl.multiple_of(j * LANES, LANES), LANES)
+        low = jnp.broadcast_to(index & (half - 1), (half, LANES))
+        one = jnp.where(low == lax.broadcasted_iota(i32, (half, LANES), 0), 1.0, 0.0).astype(bf16)
+        upper = jnp.broadcast_to(jnp.where((index & half) != 0, 1.0, 0.0), (16, LANES))
+        upper, lower = upper.astype(bf16), (1.0 - upper).astype(bf16)
+        for q in range(half // 16):
+            part = one[q * 16 : q * 16 + 16]
+            hot[q * 16 : q * 16 + 16, cols] = part * lower
+            hot[half + q * 16 : half + q * 16 + 16, cols] = part * upper
         return carry
 
-    lax.fori_loop(0, EB, body, 0, unroll=4)
+    lax.fori_loop(0, EB, body, 0, unroll=8)
 
 
 def blocks_kernel(freq, stiff, mass, blocks):
@@ -407,7 +425,14 @@
     medium = dict(flops=10**9, nbytes=10**7)
 
     rows, to_low, to_up = kernel_call(
-        prep_kernel, "prep", (arr(32, EDGES), arr(32, SLOTS), arr(32, SLOTS)), [VMEM] * 3, flops=10**6, nbytes=10**6
+        prep_kernel, "prep", (arr(32, EDGES), arr(32, SLOTS), arr(32, SLOTS)), [HBM] * 3,
+        [
+            pltpu.VMEM(adjoint_rhs.shape, f32),
+            pltpu.VMEM(forward_field.shape, f32),
+            pltpu.VMEM(lists.shape, i32),
+            pltpu.SemaphoreType.DMA((3,)),
+        ],
+        flops=10**6, nbytes=10**6, limit=62,
     )(adjoint_rhs, forward_field, lists)
     low, up = exchanged(to_low, to_up)
     (hot,) = kernel_call(

time: 122 us -> 122 us (level)
  local copies, waits for them, and re-layouts: 3.16 us -> 0.81 us
  Pallas kernels: 42.1 us -> 43.9 us
    unnamed x24 -> x20, local copies, waits for them, and re-layouts: 3.16 us -> 0.81 us
    pallas_call x1, Pallas kernels: 0.66 us -> 2.26 us  [per_device(): kernel_call(prep_kernel, 'prep', (arr(32, EDGES), arr(32, SLOTS), arr(32,...]
where the time goes in v5:
time: 122 us; the launch traced here: 121 us
  Pallas kernels  43.9 us (36%)
  starting transfers between devices  43 us (35%)
  blocking collectives  28.1 us (23%)
  waiting for transfers between devices  4.4 us (4%)
    ppermute x10, starting transfers between devices, shifted(): lax.ppermute(x, 'mesh', [(i, i + by) for i in range(count) if 0 <= i + by...  43 us
    pallas_call x2, Pallas kernels, applied(): kernel_call(functools.partial(apply_kernel, with_field), 'apply', (arr(RO...  22.7 us
    all_to_all x1, blocking collectives, per_device(): lax.all_to_all(message.reshape(32 * LANES), 'mesh', 0, 0, tiled=True)  16.3 us
    all_to_all x1, blocking collectives, per_device(): shares = lax.all_to_all(grads, 'harm', 0, 0, tiled=True)  11.8 us
    pallas_call x1, Pallas kernels, per_device(): kernel_call(third_kernel, 'third', (got_shape, arr(8, LANES)), [SMEM] + [...  6.65 us
    ppermute x10, waiting for transfers between devices, shifted(): lax.ppermute(x, 'mesh', [(i, i + by) for i in range(count) if 0 <= i + by...  4.4 us
    pallas_call x1, Pallas kernels, per_device(): kernel_call(hot_kernel, 'hot', (jax.ShapeDtypeStruct((WIDE, EB * LANES),...  3.17 us
    pallas_call x1, Pallas kernels, per_device(): kernel_call(early_gradient_kernel, 'early_gradient', (arr(8, 40, LANES),)...  2.54 us
  transfers between devices with their start and end apart: 10, of which 5 were waited for; matrix products, arithmetic and copies ran while one was open for 0% of the time, Pallas kernels for 6%

profile of v5, /device:TPU:2, one launch (start us, length us, event | category | flops | bytes accessed | tf_op | source)
XLA Modules:
  0.0 121.1 jit_solution(8046068947720217723)
XLA Ops:
  0.6 2.3 %prep.1 = (f32[32,2048]{1,0:T(8,128)}, f32[32,512]{1,0:T(8,128)}, f32[32,512]{1,0:T(8,128)}) custom-call(f32[2,6,2,2048]{3,2,1,0:T(2,128)} %rhs_in.1, f32[2,2,2048]{2,1,0:T(2,128)} %field_in.1, s32[2,512]{1,0:T(2,128)} %bitcast.12), custom_call_target="tpu_custom_call" | custom-call | flops 1000000 | bytes 1000000 | tf_op jit(solution)/shard_map/prep/pallas_call | solution.py:427
  2.9 3.8 %collective-permute-start = (f32[32,512]{1,0:T(8,128)}, f32[32,512]{1,0:T(8,128)S(1)}, u32[]{:S(2)}, u32[]{:S(2)}) collective-permute-start(f32[32,512]{1,0:T(8,128)} %get-tuple-element.23), channel_id=1, source_target_pairs={{0,8},{8,16},{16,24},{24,32},{32,40},{40,48},{48,56},{56,64},{64,7... | collective-permute-start | bytes 196616 | tf_op jit(solution)/shard_map/ppermute | solution.py:410
  6.7 0.0 copy-start.2
  6.8 6.1 %collective-permute-start.1 = (f32[32,512]{1,0:T(8,128)}, f32[32,512]{1,0:T(8,128)S(1)}, u32[]{:S(2)}, u32[]{:S(2)}) collective-permute-start(f32[32,512]{1,0:T(8,128)} %get-tuple-element.24), channel_id=1, source_target_pairs={{8,0},{16,8},{24,16},{32,24},{40,32},{48,40},{56,48},{64,56},{72,6... | collective-permute-start | bytes 196616 | tf_op jit(solution)/shard_map/ppermute | solution.py:410
  12.9 0.7 copy-done.3
  13.6 3.2 %hot.1 = bf16[512,8192]{1,0:T(8,128)(2,1)S(1)} custom-call(s32[64,128]{1,0:T(8,128)S(1)} %copy-done.3), custom_call_target="tpu_custom_call" | custom-call | flops 1000000000 | bytes 10000000 | tf_op jit(solution)/shard_map/hot/pallas_call | solution.py:438
  16.9 1.0 blocks.1
  18.0 11.9 %apply.2 = (f32[24,2048]{1,0:T(8,128)S(1)}, f32[24,512]{1,0:T(8,128)S(1)}, f32[24,512]{1,0:T(8,128)S(1)}, f32[1536,128]{1,0:T(8,128)S(1)}, f32[512,128]{1,0:T(8,128)S(1)}) custom-call(f32[2]{0:T(128)S(1)} %copy-done.7, f32[32,2048]{1,0:T(8,128)S(1)} %copy-done, f32[32,512]{1,0:T(8,128)S(1)} %collective-permute-done.low, ...), custom_call_target="tpu_custom_call" | custom-call | flops 1000000000 | bytes 10000000 | tf_op jit(solution)/shard_map/apply/pallas_call | solution.py:447
  29.9 1.9 %collective-permute-start.2 = (f32[24,512]{1,0:T(8,128)S(1)}, f32[24,512]{1,0:T(8,128)S(1)}, u32[]{:S(2)}, u32[]{:S(2)}) collective-permute-start(f32[24,512]{1,0:T(8,128)S(1)} %get-tuple-element.27), channel_id=1, source_target_pairs={{0,8},{8,16},{16,24},{24,32},{32,40},{40,48},{48,56},{56,64},{64,7... | collective-permute-start | bytes 147464 | tf_op jit(solution)/shard_map/ppermute | solution.py:410
  31.8 6.0 %collective-permute-start.3 = (f32[24,512]{1,0:T(8,128)S(1)}, f32[24,512]{1,0:T(8,128)S(1)}, u32[]{:S(2)}, u32[]{:S(2)}) collective-permute-start(f32[24,512]{1,0:T(8,128)S(1)} %get-tuple-element.28), channel_id=1, source_target_pairs={{8,0},{16,8},{24,16},{32,24},{40,32},{48,40},{56,48},{64,56},{72,6... | collective-permute-start | bytes 147464 | tf_op jit(solution)/shard_map/ppermute | solution.py:410
  37.8 0.1 collective-permute-done.2.from_low
  38.0 1.6 %collective-permute-done.3.from_up = f32[24,512]{1,0:T(8,128)S(1)} collective-permute-done((f32[24,512]{1,0:T(8,128)S(1)}, f32[24,512]{1,0:T(8,128)S(1)}, u32[]{:S(2)}, u32[]{:S(2)}) %collective-permute-start.3) | collective-permute-done | bytes 49184 | tf_op jit(solution)/shard_map/ppermute | solution.py:410
  39.6 1.2 finish.2
  40.8 1.9 %collective-permute-start.4 = (f32[24,512]{1,0:T(8,128)S(1)}, f32[24,512]{1,0:T(8,128)S(1)}, u32[]{:S(2)}, u32[]{:S(2)}) collective-permute-start(f32[24,512]{1,0:T(8,128)S(1)} %get-tuple-element.30), channel_id=1, source_target_pairs={{0,8},{8,16},{16,24},{24,32},{32,40},{40,48},{48,56},{56,64},{64,7... | collective-permute-start | bytes 147464 | tf_op jit(solution)/shard_map/ppermute | solution.py:410
  42.7 6.4 %collective-permute-start.5 = (f32[24,512]{1,0:T(8,128)S(1)}, f32[24,512]{1,0:T(8,128)S(1)}, u32[]{:S(2)}, u32[]{:S(2)}) collective-permute-start(f32[24,512]{1,0:T(8,128)S(1)} %get-tuple-element.31), channel_id=1, source_target_pairs={{8,0},{16,8},{24,16},{32,24},{40,32},{48,40},{56,48},{64,56},{72,6... | collective-permute-start | bytes 147464 | tf_op jit(solution)/shard_map/ppermute | solution.py:410
  49.1 0.1 collective-permute-done.4.low
  49.2 1.6 %collective-permute-done.5.up = f32[24,512]{1,0:T(8,128)S(1)} collective-permute-done((f32[24,512]{1,0:T(8,128)S(1)}, f32[24,512]{1,0:T(8,128)S(1)}, u32[]{:S(2)}, u32[]{:S(2)}) %collective-permute-start.5) | collective-permute-done | bytes 49184 | tf_op jit(solution)/shard_map/ppermute | solution.py:410
  50.8 10.9 %apply.3 = (f32[24,2048]{1,0:T(8,128)S(1)}, f32[24,512]{1,0:T(8,128)S(1)}, f32[24,512]{1,0:T(8,128)S(1)}, f32[1536,128]{1,0:T(8,128)S(1)}) custom-call(f32[2]{0:T(128)S(1)} %copy-done.7, f32[24,2048]{1,0:T(8,128)S(1)} %get-tuple-element.29.own.w, f32[24,512]{1,0:T(8,128)S(1)} %collective-permute-done.4.low, f32[24,512]{1,0:T(8,128)S(1)} %collective-permute-done.5.up, ...), custom_call_target="tpu_custom_call" | custom-call | flops 1000000000 | bytes 10000000 | tf_op jit(solution)/shard_map/apply/pallas_call | solution.py:447
  61.7 3.6 %collective-permute-start.6 = (f32[24,512]{1,0:T(8,128)S(1)}, f32[24,512]{1,0:T(8,128)S(1)}, u32[]{:S(2)}, u32[]{:S(2)}) collective-permute-start(f32[24,512]{1,0:T(8,128)S(1)} %get-tuple-element.35), channel_id=1, source_target_pairs={{0,8},{8,16},{16,24},{24,32},{32,40},{40,48},{48,56},{56,64},{64,7... | collective-permute-start | bytes 147464 | tf_op jit(solution)/shard_map/ppermute | solution.py:410
  65.3 4.8 %collective-permute-start.7 = (f32[24,512]{1,0:T(8,128)S(1)}, f32[24,512]{1,0:T(8,128)S(1)}, u32[]{:S(2)}, u32[]{:S(2)}) collective-permute-start(f32[24,512]{1,0:T(8,128)S(1)} %get-tuple-element.36), channel_id=1, source_target_pairs={{8,0},{16,8},{24,16},{32,24},{40,32},{48,40},{56,48},{64,56},{72,6... | collective-permute-start | bytes 147464 | tf_op jit(solution)/shard_map/ppermute | solution.py:410
  70.1 0.7 field.1.y
  70.8 0.1 early.1
  70.9 0.9 collective-permute-done.7.from_up
  71.8 1.2 finish.3
  73.0 3.4 %collective-permute-start.8 = (f32[24,512]{1,0:T(8,128)S(1)}, f32[24,512]{1,0:T(8,128)S(1)}, u32[]{:S(2)}, u32[]{:S(2)}) collective-permute-start(f32[24,512]{1,0:T(8,128)S(1)} %get-tuple-element.38), channel_id=1, source_target_pairs={{0,8},{8,16},{16,24},{24,32},{32,40},{40,48},{48,56},{56,64},{64,7... | collective-permute-start | bytes 147464 | tf_op jit(solution)/shard_map/ppermute | solution.py:410
  76.4 5.1 %collective-permute-start.9 = (f32[24,512]{1,0:T(8,128)S(1)}, f32[24,512]{1,0:T(8,128)S(1)}, u32[]{:S(2)}, u32[]{:S(2)}) collective-permute-start(f32[24,512]{1,0:T(8,128)S(1)} %get-tuple-element.39), channel_id=1, source_target_pairs={{8,0},{16,8},{24,16},{32,24},{40,32},{48,40},{56,48},{64,56},{72,6... | collective-permute-start | bytes 147464 | tf_op jit(solution)/shard_map/ppermute | solution.py:410
  81.5 2.5 %early_gradient.1.early = f32[8,40,128]{2,1,0:T(8,128)S(1)} custom-call(f32[1536,128]{1,0:T(8,128)S(1)} %get-tuple-element.25.got0, f32[1536,128]{1,0:T(8,128)S(1)} %get-tuple-element.32.got1, f32[256,128]{1,0:T(8,128)S(1)} %field.1.y, s32[8,128]{1,0:T(8,128)S(1)} %bitcast.15, f32[3,64,1024]{2,1,0:T(8,128)S(1)} %copy-done.8), custom_call_target="tpu_custom_call" | custom-call | flops 1000000000 | bytes 10000000 | tf_op jit(solution)/shard_map/early_gradient/pallas_call | solution.py:467
  84.1 6.7 %third.1 = (f32[1536,128]{1,0:T(8,128)S(1)}, f32[8,128]{1,0:T(8,128)S(1)}) custom-call(f32[2]{0:T(128)S(1)} %copy-done.7, f32[24,2048]{1,0:T(8,128)S(1)} %get-tuple-element.37.v, f32[24,512]{1,0:T(8,128)S(1)} %collective-permute-done.8.low, f32[24,512]{1,0:T(8,128)S(1)} %collective-permute-done.9.up, s32[64,128]{1,0:T(8,128)S(1)} %copy-done.4, ...), custom_call_target="tpu_custom_call" | custom-call | flops 1000000000 | bytes 10000000 | tf_op jit(solution)/shard_map/third/pallas_call | solution.py:471
  90.8 1.3 %late_gradient.1 = f32[8,64,128]{2,1,0:T(8,128)S(1)} custom-call(f32[8,40,128]{2,1,0:T(8,128)S(1)} %early_gradient.1.early, f32[1536,128]{1,0:T(8,128)S(1)} %get-tuple-element.40.got2, f32[256,128]{1,0:T(8,128)S(1)} %field.1.y, s32[8,128]{1,0:T(8,128)S(1)} %bitcast.16, f32[3,64,1024]{2,1,0:T(8,128)S(1)} %copy-done.8, f32[8,128]{1,0:T(8,128)S(1)} %get-tuple-element.41.line), custom_call_target="tpu_custom_call" | custom-call | flops 1000000000 | bytes 10000000 | tf_op jit(solution)/shard_map/late_gradient/pallas_call | solution.py:475
  92.1 11.8 %all_to_all.14.shares = f32[8,64,128]{2,1,0:T(8,128)S(1)} all-to-all(f32[8,64,128]{2,1,0:T(8,128)S(1)} %late_gradient.1), channel_id=1, replica_groups=mesh['mesh'=32,'harm'=8] {'harm'}, dimensions={0} | all-to-all | bytes 524288 | tf_op jit(solution)/shard_map/all_to_all | solution.py:478
  103.9 16.3 %all_to_all.15 = f32[32,128,1]{1,2,0:T(1,128)S(1)} all-to-all(f32[32,128,1]{1,2,0:T(1,128)S(1)} %bitcast.11), channel_id=1, replica_groups=mesh['mesh'=32,'harm'=8] {'mesh'}, dimensions={0} | all-to-all | bytes 32768 | tf_op jit(solution)/shard_map/all_to_all | solution.py:480
  120.1 1.0 last.1
  (24 shorter events, 0.1 us)
Async XLA Ops:
  2.9 15.0 %collective-permute-start = (f32[32,512]{1,0:T(8,128)}, f32[32,512]{1,0:T(8,128)S(1)}, u32[]{:S(2)}, u32[]{:S(2)}) collective-permute-start(f32[32,512]{1,0:T(8,128)} %get-tuple-element.23), channel_id=1, source_target_pairs={{0,8},{8,16},{16,24},{24,32},{32,40},{40,48},{48,56},{56,64},{64,7... | collective-permute-start | bytes 196616 | tf_op jit(solution)/shard_map/ppermute | solution.py:410
  6.7 10.1 %copy-start.1 = (f32[64,64,128]{2,1,0:T(8,128)S(1)}, f32[64,64,128]{2,1,0:T(8,128)}, u32[]{:S(2)}) copy-start(f32[64,64,128]{2,1,0:T(8,128)} %stiff.1) | copy-start | bytes 6291460
  6.7 10.1 %copy-start.2 = (f32[64,64,128]{2,1,0:T(8,128)S(1)}, f32[64,64,128]{2,1,0:T(8,128)}, u32[]{:S(2)}) copy-start(f32[64,64,128]{2,1,0:T(8,128)} %mass.1) | copy-start | bytes 6291460
  6.8 11.2 %collective-permute-start.1 = (f32[32,512]{1,0:T(8,128)}, f32[32,512]{1,0:T(8,128)S(1)}, u32[]{:S(2)}, u32[]{:S(2)}) collective-permute-start(f32[32,512]{1,0:T(8,128)} %get-tuple-element.24), channel_id=1, source_target_pairs={{8,0},{16,8},{24,16},{32,24},{40,32},{48,40},{56,48},{64,56},{72,6... | collective-permute-start | bytes 196616 | tf_op jit(solution)/shard_map/ppermute | solution.py:410
  12.9 0.8 copy-start.3
  13.6 3.2 %copy-start.7 = (f32[2]{0:T(128)S(1)}, f32[2]{0:T(128)}, u32[]{:S(2)}) copy-start(f32[2]{0:T(128)} %freq.7) | copy-start | bytes 28
  16.8 1.1 copy-start
  16.8 1.1 copy-start.4
  16.8 1.1 copy-start.5
  18.0 21.6 %copy-start.6 = (s32[1,2,512]{2,1,0:T(2,128)S(1)}, s32[1,2,512]{2,1,0:T(2,128)}, u32[]{:S(2)}) copy-start(s32[1,2,512]{2,1,0:T(2,128)} %param.17) | copy-start | bytes 12292
  29.9 8.1 %collective-permute-start.2 = (f32[24,512]{1,0:T(8,128)S(1)}, f32[24,512]{1,0:T(8,128)S(1)}, u32[]{:S(2)}, u32[]{:S(2)}) collective-permute-start(f32[24,512]{1,0:T(8,128)S(1)} %get-tuple-element.27), channel_id=1, source_target_pairs={{0,8},{8,16},{16,24},{24,32},{32,40},{40,48},{48,56},{56,64},{64,7... | collective-permute-start | bytes 147464 | tf_op jit(solution)/shard_map/ppermute | solution.py:410
  31.8 7.8 %collective-permute-start.3 = (f32[24,512]{1,0:T(8,128)S(1)}, f32[24,512]{1,0:T(8,128)S(1)}, u32[]{:S(2)}, u32[]{:S(2)}) collective-permute-start(f32[24,512]{1,0:T(8,128)S(1)} %get-tuple-element.28), channel_id=1, source_target_pairs={{8,0},{16,8},{24,16},{32,24},{40,32},{48,40},{56,48},{64,56},{72,6... | collective-permute-start | bytes 147464 | tf_op jit(solution)/shard_map/ppermute | solution.py:410
  40.8 8.4 %collective-permute-start.4 = (f32[24,512]{1,0:T(8,128)S(1)}, f32[24,512]{1,0:T(8,128)S(1)}, u32[]{:S(2)}, u32[]{:S(2)}) collective-permute-start(f32[24,512]{1,0:T(8,128)S(1)} %get-tuple-element.30), channel_id=1, source_target_pairs={{0,8},{8,16},{16,24},{24,32},{32,40},{40,48},{48,56},{56,64},{64,7... | collective-permute-start | bytes 147464 | tf_op jit(solution)/shard_map/ppermute | solution.py:410
  42.7 8.1 %collective-permute-start.5 = (f32[24,512]{1,0:T(8,128)S(1)}, f32[24,512]{1,0:T(8,128)S(1)}, u32[]{:S(2)}, u32[]{:S(2)}) collective-permute-start(f32[24,512]{1,0:T(8,128)S(1)} %get-tuple-element.31), channel_id=1, source_target_pairs={{8,0},{16,8},{24,16},{32,24},{40,32},{48,40},{56,48},{64,56},{72,6... | collective-permute-start | bytes 147464 | tf_op jit(solution)/shard_map/ppermute | solution.py:410
  61.7 19.8 %copy-start.8 = (f32[3,64,1024]{2,1,0:T(8,128)S(1)}, f32[3,64,1024]{2,1,0:T(8,128)}, u32[]{:S(2)}) copy-start(f32[3,64,1024]{2,1,0:T(8,128)} %node_shape.3) | copy-start | bytes 2359300
  61.7 19.8 %copy-start.9 = (s32[1024]{0:T(1024)S(1)}, s32[1024]{0:T(1024)}, u32[]{:S(2)}) copy-start(s32[1024]{0:T(1024)} %param.18) | copy-start | bytes 12292
  61.7 9.2 %collective-permute-start.6 = (f32[24,512]{1,0:T(8,128)S(1)}, f32[24,512]{1,0:T(8,128)S(1)}, u32[]{:S(2)}, u32[]{:S(2)}) collective-permute-start(f32[24,512]{1,0:T(8,128)S(1)} %get-tuple-element.35), channel_id=1, source_target_pairs={{0,8},{8,16},{16,24},{24,32},{32,40},{40,48},{48,56},{56,64},{64,7... | collective-permute-start | bytes 147464 | tf_op jit(solution)/shard_map/ppermute | solution.py:410
  65.3 6.6 %collective-permute-start.7 = (f32[24,512]{1,0:T(8,128)S(1)}, f32[24,512]{1,0:T(8,128)S(1)}, u32[]{:S(2)}, u32[]{:S(2)}) collective-permute-start(f32[24,512]{1,0:T(8,128)S(1)} %get-tuple-element.36), channel_id=1, source_target_pairs={{8,0},{16,8},{24,16},{32,24},{40,32},{48,40},{56,48},{64,56},{72,6... | collective-permute-start | bytes 147464 | tf_op jit(solution)/shard_map/ppermute | solution.py:410
  73.0 11.0 %collective-permute-start.8 = (f32[24,512]{1,0:T(8,128)S(1)}, f32[24,512]{1,0:T(8,128)S(1)}, u32[]{:S(2)}, u32[]{:S(2)}) collective-permute-start(f32[24,512]{1,0:T(8,128)S(1)} %get-tuple-element.38), channel_id=1, source_target_pairs={{0,8},{8,16},{16,24},{24,32},{32,40},{40,48},{48,56},{56,64},{64,7... | collective-permute-start | bytes 147464 | tf_op jit(solution)/shard_map/ppermute | solution.py:410
  76.4 7.7 %collective-permute-start.9 = (f32[24,512]{1,0:T(8,128)S(1)}, f32[24,512]{1,0:T(8,128)S(1)}, u32[]{:S(2)}, u32[]{:S(2)}) collective-permute-start(f32[24,512]{1,0:T(8,128)S(1)} %get-tuple-element.39), channel_id=1, source_target_pairs={{8,0},{16,8},{24,16},{32,24},{40,32},{48,40},{56,48},{64,56},{72,6... | collective-permute-start | bytes 147464 | tf_op jit(solution)/shard_map/ppermute | solution.py:410

commit v6 on v5

--- a/solution.py
+++ b/solution.py
@@ -70,12 +70,11 @@
         x = own[:, t * WIDE : (t + 1) * WIDE] if t < PARTS - 2 else (low if t == PARTS - 2 else up)[...]
         stack[t * 2 * count : (t + 1) * 2 * count, :] = pieces(x)
 
-    def body(c, carry):
-        cols = pl.ds(pl.multiple_of(c * CHUNK * LANES, CHUNK * LANES), CHUNK * LANES)
-        found = jnp.dot(stack[...], hot[:, cols], preferred_element_type=f32)
+    for c in range(EB // CHUNK):
+        found = jnp.dot(stack[...], hot[:, c * CHUNK * LANES : (c + 1) * CHUNK * LANES], preferred_element_type=f32)
         for jj in range(CHUNK):
             j = c * CHUNK + jj
-            high = conn[pl.ds(j, 1), :] >> 9
+            high = conn[j : j + 1, :] >> 9
             for out, first, rows in outs:
                 value = None
                 for t in range(PARTS):
@@ -83,10 +82,7 @@
                     lanes = slice(jj * LANES, (jj + 1) * LANES)
                     x = found[at : at + rows, lanes] + found[at + count : at + count + rows, lanes]
                     value = x if t == 0 else jnp.where(jnp.broadcast_to(high, x.shape) == t, x, value)
-                out[pl.ds(pl.multiple_of(j * rows, 8), rows), :] = value
-        return carry
-
-    lax.fori_loop(0, EB // CHUNK, body, 0)
+                out[j * rows : (j + 1) * rows, :] = value
 
 
 def product(blocks, got, out, per_harm, per_edge, wide):

time: 122 us -> 120 us (0.984)
  Pallas kernels: 43.9 us -> 42.1 us
  transfers between devices with their start and end apart: 10 -> 10, of which waited for: 5 -> 4; matrix products, arithmetic and copies ran while one was open for 0% -> 0% of each run, Pallas kernels for 6% -> 6%
where the time goes in v6:
time: 120 us; the launch traced here: 119 us
  starting transfers between devices  43 us (36%)
  Pallas kernels  42.1 us (35%)
  blocking collectives  28.3 us (24%)
  waiting for transfers between devices  4.21 us (4%)
    ppermute x10, starting transfers between devices, shifted(): lax.ppermute(x, 'mesh', [(i, i + by) for i in range(count) if 0 <= i + by...  43 us
    pallas_call x2, Pallas kernels, applied(): kernel_call(functools.partial(apply_kernel, with_field), 'apply', (arr(RO...  21.6 us
    all_to_all x1, blocking collectives, per_device(): lax.all_to_all(message.reshape(32 * LANES), 'mesh', 0, 0, tiled=True)  16.4 us
    all_to_all x1, blocking collectives, per_device(): shares = lax.all_to_all(grads, 'harm', 0, 0, tiled=True)  11.8 us
    pallas_call x1, Pallas kernels, per_device(): kernel_call(third_kernel, 'third', (got_shape, arr(8, LANES)), [SMEM] + [...  6.07 us
    ppermute x10, waiting for transfers between devices, shifted(): lax.ppermute(x, 'mesh', [(i, i + by) for i in range(count) if 0 <= i + by...  4.21 us
    pallas_call x1, Pallas kernels, per_device(): kernel_call(hot_kernel, 'hot', (jax.ShapeDtypeStruct((WIDE, EB * LANES),...  3.17 us
    pallas_call x1, Pallas kernels, per_device(): kernel_call(early_gradient_kernel, 'early_gradient', (arr(8, 40, LANES),)...  2.54 us
  transfers between devices with their start and end apart: 10, of which 4 were waited for; matrix products, arithmetic and copies ran while one was open for 0% of the time, Pallas kernels for 6%

profile of v6, /device:TPU:2, one launch (start us, length us, event | category | flops | bytes accessed | tf_op | source)
XLA Modules:
  0.0 119.4 jit_solution(8124825447735687854)
XLA Ops:
  0.6 2.3 %prep.1 = (f32[32,2048]{1,0:T(8,128)}, f32[32,512]{1,0:T(8,128)}, f32[32,512]{1,0:T(8,128)}) custom-call(f32[2,6,2,2048]{3,2,1,0:T(2,128)} %rhs_in.1, f32[2,2,2048]{2,1,0:T(2,128)} %field_in.1, s32[2,512]{1,0:T(2,128)} %bitcast.12), custom_call_target="tpu_custom_call" | custom-call | flops 1000000 | bytes 1000000 | tf_op jit(solution)/shard_map/prep/pallas_call | solution.py:423
  2.9 3.8 %collective-permute-start = (f32[32,512]{1,0:T(8,128)}, f32[32,512]{1,0:T(8,128)S(1)}, u32[]{:S(2)}, u32[]{:S(2)}) collective-permute-start(f32[32,512]{1,0:T(8,128)} %get-tuple-element.23), channel_id=1, source_target_pairs={{0,8},{8,16},{16,24},{24,32},{32,40},{40,48},{48,56},{56,64},{64,7... | collective-permute-start | bytes 196616 | tf_op jit(solution)/shard_map/ppermute | solution.py:406
  6.7 0.0 copy-start.2
  6.8 6.1 %collective-permute-start.1 = (f32[32,512]{1,0:T(8,128)}, f32[32,512]{1,0:T(8,128)S(1)}, u32[]{:S(2)}, u32[]{:S(2)}) collective-permute-start(f32[32,512]{1,0:T(8,128)} %get-tuple-element.24), channel_id=1, source_target_pairs={{8,0},{16,8},{24,16},{32,24},{40,32},{48,40},{56,48},{64,56},{72,6... | collective-permute-start | bytes 196616 | tf_op jit(solution)/shard_map/ppermute | solution.py:406
  12.9 0.0 copy-start.3
  12.9 0.7 copy-done.3
  13.6 3.2 %hot.1 = bf16[512,8192]{1,0:T(8,128)(2,1)S(1)} custom-call(s32[64,128]{1,0:T(8,128)S(1)} %copy-done.3), custom_call_target="tpu_custom_call" | custom-call | flops 1000000000 | bytes 10000000 | tf_op jit(solution)/shard_map/hot/pallas_call | solution.py:434
  16.9 1.0 blocks.1
  18.0 11.3 %apply.2 = (f32[24,2048]{1,0:T(8,128)S(1)}, f32[24,512]{1,0:T(8,128)S(1)}, f32[24,512]{1,0:T(8,128)S(1)}, f32[1536,128]{1,0:T(8,128)S(1)}, f32[512,128]{1,0:T(8,128)S(1)}) custom-call(f32[2]{0:T(128)S(1)} %copy-done.7, f32[32,2048]{1,0:T(8,128)S(1)} %copy-done, f32[32,512]{1,0:T(8,128)S(1)} %collective-permute-done.low, ...), custom_call_target="tpu_custom_call" | custom-call | flops 1000000000 | bytes 10000000 | tf_op jit(solution)/shard_map/apply/pallas_call | solution.py:443
  29.3 1.9 %collective-permute-start.2 = (f32[24,512]{1,0:T(8,128)S(1)}, f32[24,512]{1,0:T(8,128)S(1)}, u32[]{:S(2)}, u32[]{:S(2)}) collective-permute-start(f32[24,512]{1,0:T(8,128)S(1)} %get-tuple-element.27), channel_id=1, source_target_pairs={{0,8},{8,16},{16,24},{24,32},{32,40},{40,48},{48,56},{56,64},{64,7... | collective-permute-start | bytes 147464 | tf_op jit(solution)/shard_map/ppermute | solution.py:406
  31.2 6.0 %collective-permute-start.3 = (f32[24,512]{1,0:T(8,128)S(1)}, f32[24,512]{1,0:T(8,128)S(1)}, u32[]{:S(2)}, u32[]{:S(2)}) collective-permute-start(f32[24,512]{1,0:T(8,128)S(1)} %get-tuple-element.28), channel_id=1, source_target_pairs={{8,0},{16,8},{24,16},{32,24},{40,32},{48,40},{56,48},{64,56},{72,6... | collective-permute-start | bytes 147464 | tf_op jit(solution)/shard_map/ppermute | solution.py:406
  37.3 0.1 collective-permute-done.2.from_low
  37.4 1.6 %collective-permute-done.3.from_up = f32[24,512]{1,0:T(8,128)S(1)} collective-permute-done((f32[24,512]{1,0:T(8,128)S(1)}, f32[24,512]{1,0:T(8,128)S(1)}, u32[]{:S(2)}, u32[]{:S(2)}) %collective-permute-start.3) | collective-permute-done | bytes 49184 | tf_op jit(solution)/shard_map/ppermute | solution.py:406
  39.0 1.2 finish.2
  40.2 1.9 %collective-permute-start.4 = (f32[24,512]{1,0:T(8,128)S(1)}, f32[24,512]{1,0:T(8,128)S(1)}, u32[]{:S(2)}, u32[]{:S(2)}) collective-permute-start(f32[24,512]{1,0:T(8,128)S(1)} %get-tuple-element.30), channel_id=1, source_target_pairs={{0,8},{8,16},{16,24},{24,32},{32,40},{40,48},{48,56},{56,64},{64,7... | collective-permute-start | bytes 147464 | tf_op jit(solution)/shard_map/ppermute | solution.py:406
  42.1 6.5 %collective-permute-start.5 = (f32[24,512]{1,0:T(8,128)S(1)}, f32[24,512]{1,0:T(8,128)S(1)}, u32[]{:S(2)}, u32[]{:S(2)}) collective-permute-start(f32[24,512]{1,0:T(8,128)S(1)} %get-tuple-element.31), channel_id=1, source_target_pairs={{8,0},{16,8},{24,16},{32,24},{40,32},{48,40},{56,48},{64,56},{72,6... | collective-permute-start | bytes 147464 | tf_op jit(solution)/shard_map/ppermute | solution.py:406
  48.7 1.5 %collective-permute-done.5.up = f32[24,512]{1,0:T(8,128)S(1)} collective-permute-done((f32[24,512]{1,0:T(8,128)S(1)}, f32[24,512]{1,0:T(8,128)S(1)}, u32[]{:S(2)}, u32[]{:S(2)}) %collective-permute-start.5) | collective-permute-done | bytes 49184 | tf_op jit(solution)/shard_map/ppermute | solution.py:406
  50.2 10.3 %apply.3 = (f32[24,2048]{1,0:T(8,128)S(1)}, f32[24,512]{1,0:T(8,128)S(1)}, f32[24,512]{1,0:T(8,128)S(1)}, f32[1536,128]{1,0:T(8,128)S(1)}) custom-call(f32[2]{0:T(128)S(1)} %copy-done.7, f32[24,2048]{1,0:T(8,128)S(1)} %get-tuple-element.29.own.w, f32[24,512]{1,0:T(8,128)S(1)} %collective-permute-done.4.low, f32[24,512]{1,0:T(8,128)S(1)} %collective-permute-done.5.up, ...), custom_call_target="tpu_custom_call" | custom-call | flops 1000000000 | bytes 10000000 | tf_op jit(solution)/shard_map/apply/pallas_call | solution.py:443
  60.5 3.6 %collective-permute-start.6 = (f32[24,512]{1,0:T(8,128)S(1)}, f32[24,512]{1,0:T(8,128)S(1)}, u32[]{:S(2)}, u32[]{:S(2)}) collective-permute-start(f32[24,512]{1,0:T(8,128)S(1)} %get-tuple-element.35), channel_id=1, source_target_pairs={{0,8},{8,16},{16,24},{24,32},{32,40},{40,48},{48,56},{56,64},{64,7... | collective-permute-start | bytes 147464 | tf_op jit(solution)/shard_map/ppermute | solution.py:406
  64.1 4.8 %collective-permute-start.7 = (f32[24,512]{1,0:T(8,128)S(1)}, f32[24,512]{1,0:T(8,128)S(1)}, u32[]{:S(2)}, u32[]{:S(2)}) collective-permute-start(f32[24,512]{1,0:T(8,128)S(1)} %get-tuple-element.36), channel_id=1, source_target_pairs={{8,0},{16,8},{24,16},{32,24},{40,32},{48,40},{56,48},{64,56},{72,6... | collective-permute-start | bytes 147464 | tf_op jit(solution)/shard_map/ppermute | solution.py:406
  68.9 0.7 field.1.y
  69.7 0.1 early.1
  69.8 0.9 collective-permute-done.7.from_up
  70.7 1.2 finish.3
  71.9 3.4 %collective-permute-start.8 = (f32[24,512]{1,0:T(8,128)S(1)}, f32[24,512]{1,0:T(8,128)S(1)}, u32[]{:S(2)}, u32[]{:S(2)}) collective-permute-start(f32[24,512]{1,0:T(8,128)S(1)} %get-tuple-element.38), channel_id=1, source_target_pairs={{0,8},{8,16},{16,24},{24,32},{32,40},{40,48},{48,56},{56,64},{64,7... | collective-permute-start | bytes 147464 | tf_op jit(solution)/shard_map/ppermute | solution.py:406
  75.2 4.9 %collective-permute-start.9 = (f32[24,512]{1,0:T(8,128)S(1)}, f32[24,512]{1,0:T(8,128)S(1)}, u32[]{:S(2)}, u32[]{:S(2)}) collective-permute-start(f32[24,512]{1,0:T(8,128)S(1)} %get-tuple-element.39), channel_id=1, source_target_pairs={{8,0},{16,8},{24,16},{32,24},{40,32},{48,40},{56,48},{64,56},{72,6... | collective-permute-start | bytes 147464 | tf_op jit(solution)/shard_map/ppermute | solution.py:406
  80.2 2.5 %early_gradient.1.early = f32[8,40,128]{2,1,0:T(8,128)S(1)} custom-call(f32[1536,128]{1,0:T(8,128)S(1)} %get-tuple-element.25.got0, f32[1536,128]{1,0:T(8,128)S(1)} %get-tuple-element.32.got1, f32[256,128]{1,0:T(8,128)S(1)} %field.1.y, s32[8,128]{1,0:T(8,128)S(1)} %bitcast.15, f32[3,64,1024]{2,1,0:T(8,128)S(1)} %copy-done.8), custom_call_target="tpu_custom_call" | custom-call | flops 1000000000 | bytes 10000000 | tf_op jit(solution)/shard_map/early_gradient/pallas_call | solution.py:463
  82.8 6.1 %third.1 = (f32[1536,128]{1,0:T(8,128)S(1)}, f32[8,128]{1,0:T(8,128)S(1)}) custom-call(f32[2]{0:T(128)S(1)} %copy-done.7, f32[24,2048]{1,0:T(8,128)S(1)} %get-tuple-element.37.v, f32[24,512]{1,0:T(8,128)S(1)} %collective-permute-done.8.low, f32[24,512]{1,0:T(8,128)S(1)} %collective-permute-done.9.up, s32[64,128]{1,0:T(8,128)S(1)} %copy-done.4, ...), custom_call_target="tpu_custom_call" | custom-call | flops 1000000000 | bytes 10000000 | tf_op jit(solution)/shard_map/third/pallas_call | solution.py:467
  88.8 1.3 %late_gradient.1 = f32[8,64,128]{2,1,0:T(8,128)S(1)} custom-call(f32[8,40,128]{2,1,0:T(8,128)S(1)} %early_gradient.1.early, f32[1536,128]{1,0:T(8,128)S(1)} %get-tuple-element.40.got2, f32[256,128]{1,0:T(8,128)S(1)} %field.1.y, s32[8,128]{1,0:T(8,128)S(1)} %bitcast.16, f32[3,64,1024]{2,1,0:T(8,128)S(1)} %copy-done.8, f32[8,128]{1,0:T(8,128)S(1)} %get-tuple-element.41.line), custom_call_target="tpu_custom_call" | custom-call | flops 1000000000 | bytes 10000000 | tf_op jit(solution)/shard_map/late_gradient/pallas_call | solution.py:471
  90.1 11.8 %all_to_all.14.shares = f32[8,64,128]{2,1,0:T(8,128)S(1)} all-to-all(f32[8,64,128]{2,1,0:T(8,128)S(1)} %late_gradient.1), channel_id=1, replica_groups=mesh['mesh'=32,'harm'=8] {'harm'}, dimensions={0} | all-to-all | bytes 524288 | tf_op jit(solution)/shard_map/all_to_all | solution.py:474
  102.0 16.4 %all_to_all.15 = f32[32,128,1]{1,2,0:T(1,128)S(1)} all-to-all(f32[32,128,1]{1,2,0:T(1,128)S(1)} %bitcast.11), channel_id=1, replica_groups=mesh['mesh'=32,'harm'=8] {'mesh'}, dimensions={0} | all-to-all | bytes 32768 | tf_op jit(solution)/shard_map/all_to_all | solution.py:476
  118.4 1.0 last.1
  (24 shorter events, 0.1 us)
Async XLA Ops:
  2.9 15.0 %collective-permute-start = (f32[32,512]{1,0:T(8,128)}, f32[32,512]{1,0:T(8,128)S(1)}, u32[]{:S(2)}, u32[]{:S(2)}) collective-permute-start(f32[32,512]{1,0:T(8,128)} %get-tuple-element.23), channel_id=1, source_target_pairs={{0,8},{8,16},{16,24},{24,32},{32,40},{40,48},{48,56},{56,64},{64,7... | collective-permute-start | bytes 196616 | tf_op jit(solution)/shard_map/ppermute | solution.py:406
  6.7 10.1 %copy-start.1 = (f32[64,64,128]{2,1,0:T(8,128)S(1)}, f32[64,64,128]{2,1,0:T(8,128)}, u32[]{:S(2)}) copy-start(f32[64,64,128]{2,1,0:T(8,128)} %stiff.1) | copy-start | bytes 6291460
  6.7 10.1 %copy-start.2 = (f32[64,64,128]{2,1,0:T(8,128)S(1)}, f32[64,64,128]{2,1,0:T(8,128)}, u32[]{:S(2)}) copy-start(f32[64,64,128]{2,1,0:T(8,128)} %mass.1) | copy-start | bytes 6291460
  6.8 11.2 %collective-permute-start.1 = (f32[32,512]{1,0:T(8,128)}, f32[32,512]{1,0:T(8,128)S(1)}, u32[]{:S(2)}, u32[]{:S(2)}) collective-permute-start(f32[32,512]{1,0:T(8,128)} %get-tuple-element.24), channel_id=1, source_target_pairs={{8,0},{16,8},{24,16},{32,24},{40,32},{48,40},{56,48},{64,56},{72,6... | collective-permute-start | bytes 196616 | tf_op jit(solution)/shard_map/ppermute | solution.py:406
  12.9 0.8 copy-start.3
  13.6 3.2 %copy-start.7 = (f32[2]{0:T(128)S(1)}, f32[2]{0:T(128)}, u32[]{:S(2)}) copy-start(f32[2]{0:T(128)} %freq.7) | copy-start | bytes 28
  16.8 1.1 copy-start
  16.8 1.1 copy-start.4
  16.8 1.1 copy-start.5
  18.0 21.0 %copy-start.6 = (s32[1,2,512]{2,1,0:T(2,128)S(1)}, s32[1,2,512]{2,1,0:T(2,128)}, u32[]{:S(2)}) copy-start(s32[1,2,512]{2,1,0:T(2,128)} %param.17) | copy-start | bytes 12292
  29.3 8.1 %collective-permute-start.2 = (f32[24,512]{1,0:T(8,128)S(1)}, f32[24,512]{1,0:T(8,128)S(1)}, u32[]{:S(2)}, u32[]{:S(2)}) collective-permute-start(f32[24,512]{1,0:T(8,128)S(1)} %get-tuple-element.27), channel_id=1, source_target_pairs={{0,8},{8,16},{16,24},{24,32},{32,40},{40,48},{48,56},{56,64},{64,7... | collective-permute-start | bytes 147464 | tf_op jit(solution)/shard_map/ppermute | solution.py:406
  31.2 7.8 %collective-permute-start.3 = (f32[24,512]{1,0:T(8,128)S(1)}, f32[24,512]{1,0:T(8,128)S(1)}, u32[]{:S(2)}, u32[]{:S(2)}) collective-permute-start(f32[24,512]{1,0:T(8,128)S(1)} %get-tuple-element.28), channel_id=1, source_target_pairs={{8,0},{16,8},{24,16},{32,24},{40,32},{48,40},{56,48},{64,56},{72,6... | collective-permute-start | bytes 147464 | tf_op jit(solution)/shard_map/ppermute | solution.py:406
  40.2 8.5 %collective-permute-start.4 = (f32[24,512]{1,0:T(8,128)S(1)}, f32[24,512]{1,0:T(8,128)S(1)}, u32[]{:S(2)}, u32[]{:S(2)}) collective-permute-start(f32[24,512]{1,0:T(8,128)S(1)} %get-tuple-element.30), channel_id=1, source_target_pairs={{0,8},{8,16},{16,24},{24,32},{32,40},{40,48},{48,56},{56,64},{64,7... | collective-permute-start | bytes 147464 | tf_op jit(solution)/shard_map/ppermute | solution.py:406
  42.1 8.1 %collective-permute-start.5 = (f32[24,512]{1,0:T(8,128)S(1)}, f32[24,512]{1,0:T(8,128)S(1)}, u32[]{:S(2)}, u32[]{:S(2)}) collective-permute-start(f32[24,512]{1,0:T(8,128)S(1)} %get-tuple-element.31), channel_id=1, source_target_pairs={{8,0},{16,8},{24,16},{32,24},{40,32},{48,40},{56,48},{64,56},{72,6... | collective-permute-start | bytes 147464 | tf_op jit(solution)/shard_map/ppermute | solution.py:406
  60.5 19.7 %copy-start.8 = (f32[3,64,1024]{2,1,0:T(8,128)S(1)}, f32[3,64,1024]{2,1,0:T(8,128)}, u32[]{:S(2)}) copy-start(f32[3,64,1024]{2,1,0:T(8,128)} %node_shape.3) | copy-start | bytes 2359300
  60.5 19.7 %copy-start.9 = (s32[1024]{0:T(1024)S(1)}, s32[1024]{0:T(1024)}, u32[]{:S(2)}) copy-start(s32[1024]{0:T(1024)} %param.18) | copy-start | bytes 12292
  60.5 9.2 %collective-permute-start.6 = (f32[24,512]{1,0:T(8,128)S(1)}, f32[24,512]{1,0:T(8,128)S(1)}, u32[]{:S(2)}, u32[]{:S(2)}) collective-permute-start(f32[24,512]{1,0:T(8,128)S(1)} %get-tuple-element.35), channel_id=1, source_target_pairs={{0,8},{8,16},{16,24},{24,32},{32,40},{40,48},{48,56},{56,64},{64,7... | collective-permute-start | bytes 147464 | tf_op jit(solution)/shard_map/ppermute | solution.py:406
  64.1 6.6 %collective-permute-start.7 = (f32[24,512]{1,0:T(8,128)S(1)}, f32[24,512]{1,0:T(8,128)S(1)}, u32[]{:S(2)}, u32[]{:S(2)}) collective-permute-start(f32[24,512]{1,0:T(8,128)S(1)} %get-tuple-element.36), channel_id=1, source_target_pairs={{8,0},{16,8},{24,16},{32,24},{40,32},{48,40},{56,48},{64,56},{72,6... | collective-permute-start | bytes 147464 | tf_op jit(solution)/shard_map/ppermute | solution.py:406
  71.9 10.9 %collective-permute-start.8 = (f32[24,512]{1,0:T(8,128)S(1)}, f32[24,512]{1,0:T(8,128)S(1)}, u32[]{:S(2)}, u32[]{:S(2)}) collective-permute-start(f32[24,512]{1,0:T(8,128)S(1)} %get-tuple-element.38), channel_id=1, source_target_pairs={{0,8},{8,16},{16,24},{24,32},{32,40},{40,48},{48,56},{56,64},{64,7... | collective-permute-start | bytes 147464 | tf_op jit(solution)/shard_map/ppermute | solution.py:406
  75.2 7.5 %collective-permute-start.9 = (f32[24,512]{1,0:T(8,128)S(1)}, f32[24,512]{1,0:T(8,128)S(1)}, u32[]{:S(2)}, u32[]{:S(2)}) collective-permute-start(f32[24,512]{1,0:T(8,128)S(1)} %get-tuple-element.39), channel_id=1, source_target_pairs={{8,0},{16,8},{24,16},{32,24},{40,32},{48,40},{56,48},{64,56},{72,6... | collective-permute-start | bytes 147464 | tf_op jit(solution)/shard_map/ppermute | solution.py:406

commit v7 on v6

--- a/solution.py
+++ b/solution.py
@@ -92,7 +92,7 @@
             def inner(i, sums):
                 ks = []
                 for q in range(wide):
-                    rows = pl.ds(pl.multiple_of((jt * wide + q) * 8, 8), 8)
+                    rows = pl.ds((jt * wide + q) * 8, 8)
                     ks.append(blocks[h, i, rows, :])
                 new = []
                 for r in range(per_harm):
@@ -102,14 +102,15 @@
                 return tuple(new)
 
             zero = jnp.zeros((8, LANES), f32)
-            sums = lax.fori_loop(0, EB, inner, (zero,) * (per_harm * wide), unroll=8)
+            sums = lax.fori_loop(0, EB, inner, (zero,) * (per_harm * wide), unroll=16)
             for r in range(per_harm):
                 for q in range(wide):
                     at = (h * per_harm + r) * EB + (jt * wide + q) * 8
-                    out[pl.ds(pl.multiple_of(at, 8), 8), :] = sums[r * wide + q]
+                    out[pl.ds(at, 8), :] = sums[r * wide + q]
             return carry
 
-        lax.fori_loop(0, EB // (8 * wide), outer, 0)
+        for jt in range(EB // (8 * wide)):
+            outer(jt, 0)
 
 
 def pieces(x):

time: 120 us -> 120 us (level)
  no operation moved by 1% of the time
where the time goes in v7:
time: 120 us; the launch traced here: 119 us
  starting transfers between devices  43 us (36%)
  Pallas kernels  41.7 us (35%)
  blocking collectives  28.3 us (24%)
  waiting for transfers between devices  4.26 us (4%)
    ppermute x10, starting transfers between devices, shifted(): lax.ppermute(x, 'mesh', [(i, i + by) for i in range(count) if 0 <= i + by...  43 us
    pallas_call x2, Pallas kernels, applied(): kernel_call(functools.partial(apply_kernel, with_field), 'apply', (arr(RO...  21.2 us
    all_to_all x1, blocking collectives, per_device(): lax.all_to_all(message.reshape(32 * LANES), 'mesh', 0, 0, tiled=True)  16.5 us
    all_to_all x1, blocking collectives, per_device(): shares = lax.all_to_all(grads, 'harm', 0, 0, tiled=True)  11.8 us
    pallas_call x1, Pallas kernels, per_device(): kernel_call(third_kernel, 'third', (got_shape, arr(8, LANES)), [SMEM] + [...  6.08 us
    ppermute x10, waiting for transfers between devices, shifted(): lax.ppermute(x, 'mesh', [(i, i + by) for i in range(count) if 0 <= i + by...  4.26 us
    pallas_call x1, Pallas kernels, per_device(): kernel_call(hot_kernel, 'hot', (jax.ShapeDtypeStruct((WIDE, EB * LANES),...  3.17 us
    pallas_call x1, Pallas kernels, per_device(): kernel_call(early_gradient_kernel, 'early_gradient', (arr(8, 40, LANES),)...  2.54 us
  transfers between devices with their start and end apart: 10, of which 4 were waited for; matrix products, arithmetic and copies ran while one was open for 0% of the time, Pallas kernels for 6%

profile of v7, /device:TPU:2, one launch (start us, length us, event | category | flops | bytes accessed | tf_op | source)
XLA Modules:
  0.0 119.0 jit_solution(12512643404714858769)
XLA Ops:
  0.6 2.3 %prep.1 = (f32[32,2048]{1,0:T(8,128)}, f32[32,512]{1,0:T(8,128)}, f32[32,512]{1,0:T(8,128)}) custom-call(f32[2,6,2,2048]{3,2,1,0:T(2,128)} %rhs_in.1, f32[2,2,2048]{2,1,0:T(2,128)} %field_in.1, s32[2,512]{1,0:T(2,128)} %bitcast.12), custom_call_target="tpu_custom_call" | custom-call | flops 1000000 | bytes 1000000 | tf_op jit(solution)/shard_map/prep/pallas_call | solution.py:424
  2.9 3.8 %collective-permute-start = (f32[32,512]{1,0:T(8,128)}, f32[32,512]{1,0:T(8,128)S(1)}, u32[]{:S(2)}, u32[]{:S(2)}) collective-permute-start(f32[32,512]{1,0:T(8,128)} %get-tuple-element.23), channel_id=1, source_target_pairs={{0,8},{8,16},{16,24},{24,32},{32,40},{40,48},{48,56},{56,64},{64,7... | collective-permute-start | bytes 196616 | tf_op jit(solution)/shard_map/ppermute | solution.py:407
  6.7 0.0 copy-start.2
  6.8 6.1 %collective-permute-start.1 = (f32[32,512]{1,0:T(8,128)}, f32[32,512]{1,0:T(8,128)S(1)}, u32[]{:S(2)}, u32[]{:S(2)}) collective-permute-start(f32[32,512]{1,0:T(8,128)} %get-tuple-element.24), channel_id=1, source_target_pairs={{8,0},{16,8},{24,16},{32,24},{40,32},{48,40},{56,48},{64,56},{72,6... | collective-permute-start | bytes 196616 | tf_op jit(solution)/shard_map/ppermute | solution.py:407
  12.9 0.0 copy-start.3
  12.9 0.7 copy-done.3
  13.6 3.2 %hot.1 = bf16[512,8192]{1,0:T(8,128)(2,1)S(1)} custom-call(s32[64,128]{1,0:T(8,128)S(1)} %copy-done.3), custom_call_target="tpu_custom_call" | custom-call | flops 1000000000 | bytes 10000000 | tf_op jit(solution)/shard_map/hot/pallas_call | solution.py:435
  16.9 1.0 blocks.1
  18.0 11.1 %apply.2 = (f32[24,2048]{1,0:T(8,128)S(1)}, f32[24,512]{1,0:T(8,128)S(1)}, f32[24,512]{1,0:T(8,128)S(1)}, f32[1536,128]{1,0:T(8,128)S(1)}, f32[512,128]{1,0:T(8,128)S(1)}) custom-call(f32[2]{0:T(128)S(1)} %copy-done.7, f32[32,2048]{1,0:T(8,128)S(1)} %copy-done, f32[32,512]{1,0:T(8,128)S(1)} %collective-permute-done.low, ...), custom_call_target="tpu_custom_call" | custom-call | flops 1000000000 | bytes 10000000 | tf_op jit(solution)/shard_map/apply/pallas_call | solution.py:444
  29.1 1.9 %collective-permute-start.2 = (f32[24,512]{1,0:T(8,128)S(1)}, f32[24,512]{1,0:T(8,128)S(1)}, u32[]{:S(2)}, u32[]{:S(2)}) collective-permute-start(f32[24,512]{1,0:T(8,128)S(1)} %get-tuple-element.27), channel_id=1, source_target_pairs={{0,8},{8,16},{16,24},{24,32},{32,40},{40,48},{48,56},{56,64},{64,7... | collective-permute-start | bytes 147464 | tf_op jit(solution)/shard_map/ppermute | solution.py:407
  31.0 6.0 %collective-permute-start.3 = (f32[24,512]{1,0:T(8,128)S(1)}, f32[24,512]{1,0:T(8,128)S(1)}, u32[]{:S(2)}, u32[]{:S(2)}) collective-permute-start(f32[24,512]{1,0:T(8,128)S(1)} %get-tuple-element.28), channel_id=1, source_target_pairs={{8,0},{16,8},{24,16},{32,24},{40,32},{48,40},{56,48},{64,56},{72,6... | collective-permute-start | bytes 147464 | tf_op jit(solution)/shard_map/ppermute | solution.py:407
  37.1 0.1 collective-permute-done.2.from_low
  37.2 1.6 %collective-permute-done.3.from_up = f32[24,512]{1,0:T(8,128)S(1)} collective-permute-done((f32[24,512]{1,0:T(8,128)S(1)}, f32[24,512]{1,0:T(8,128)S(1)}, u32[]{:S(2)}, u32[]{:S(2)}) %collective-permute-start.3) | collective-permute-done | bytes 49184 | tf_op jit(solution)/shard_map/ppermute | solution.py:407
  38.8 1.2 %finish.2 = (f32[24,2048]{1,0:T(8,128)S(1)}, f32[24,512]{1,0:T(8,128)S(1)}, f32[24,512]{1,0:T(8,128)S(1)}) custom-call(f32[24,2048]{1,0:T(8,128)S(1)} %get-tuple-element.26.p, s32[2,512]{1,0:T(2,128)S(1)} %bitcast.13, f32[24,512]{1,0:T(8,128)S(1)} %collective-permute-done.2.from_low, f32[24,512]{1,0:T(8,128)S(1)} %collective-permute-done.3.from_up), custom_call_target="tpu_custom_call" | custom-call | flops 10000000 | bytes 1000000 | tf_op jit(solution)/shard_map/finish/pallas_call | solution.py:456
  40.0 1.9 %collective-permute-start.4 = (f32[24,512]{1,0:T(8,128)S(1)}, f32[24,512]{1,0:T(8,128)S(1)}, u32[]{:S(2)}, u32[]{:S(2)}) collective-permute-start(f32[24,512]{1,0:T(8,128)S(1)} %get-tuple-element.30), channel_id=1, source_target_pairs={{0,8},{8,16},{16,24},{24,32},{32,40},{40,48},{48,56},{56,64},{64,7... | collective-permute-start | bytes 147464 | tf_op jit(solution)/shard_map/ppermute | solution.py:407
  41.9 6.5 %collective-permute-start.5 = (f32[24,512]{1,0:T(8,128)S(1)}, f32[24,512]{1,0:T(8,128)S(1)}, u32[]{:S(2)}, u32[]{:S(2)}) collective-permute-start(f32[24,512]{1,0:T(8,128)S(1)} %get-tuple-element.31), channel_id=1, source_target_pairs={{8,0},{16,8},{24,16},{32,24},{40,32},{48,40},{56,48},{64,56},{72,6... | collective-permute-start | bytes 147464 | tf_op jit(solution)/shard_map/ppermute | solution.py:407
  48.5 1.5 %collective-permute-done.5.up = f32[24,512]{1,0:T(8,128)S(1)} collective-permute-done((f32[24,512]{1,0:T(8,128)S(1)}, f32[24,512]{1,0:T(8,128)S(1)}, u32[]{:S(2)}, u32[]{:S(2)}) %collective-permute-start.5) | collective-permute-done | bytes 49184 | tf_op jit(solution)/shard_map/ppermute | solution.py:407
  50.0 10.1 %apply.3 = (f32[24,2048]{1,0:T(8,128)S(1)}, f32[24,512]{1,0:T(8,128)S(1)}, f32[24,512]{1,0:T(8,128)S(1)}, f32[1536,128]{1,0:T(8,128)S(1)}) custom-call(f32[2]{0:T(128)S(1)} %copy-done.7, f32[24,2048]{1,0:T(8,128)S(1)} %get-tuple-element.29.own.w, f32[24,512]{1,0:T(8,128)S(1)} %collective-permute-done.4.low, f32[24,512]{1,0:T(8,128)S(1)} %collective-permute-done.5.up, ...), custom_call_target="tpu_custom_call" | custom-call | flops 1000000000 | bytes 10000000 | tf_op jit(solution)/shard_map/apply/pallas_call | solution.py:444
  60.2 3.6 %collective-permute-start.6 = (f32[24,512]{1,0:T(8,128)S(1)}, f32[24,512]{1,0:T(8,128)S(1)}, u32[]{:S(2)}, u32[]{:S(2)}) collective-permute-start(f32[24,512]{1,0:T(8,128)S(1)} %get-tuple-element.35), channel_id=1, source_target_pairs={{0,8},{8,16},{16,24},{24,32},{32,40},{40,48},{48,56},{56,64},{64,7... | collective-permute-start | bytes 147464 | tf_op jit(solution)/shard_map/ppermute | solution.py:407
  63.8 4.8 %collective-permute-start.7 = (f32[24,512]{1,0:T(8,128)S(1)}, f32[24,512]{1,0:T(8,128)S(1)}, u32[]{:S(2)}, u32[]{:S(2)}) collective-permute-start(f32[24,512]{1,0:T(8,128)S(1)} %get-tuple-element.36), channel_id=1, source_target_pairs={{8,0},{16,8},{24,16},{32,24},{40,32},{48,40},{56,48},{64,56},{72,6... | collective-permute-start | bytes 147464 | tf_op jit(solution)/shard_map/ppermute | solution.py:407
  68.6 0.7 field.1.y
  69.2 0.1 early.1
  69.3 1.0 collective-permute-done.7.from_up
  70.3 1.2 %finish.3 = (f32[24,2048]{1,0:T(8,128)S(1)}, f32[24,512]{1,0:T(8,128)S(1)}, f32[24,512]{1,0:T(8,128)S(1)}) custom-call(f32[24,2048]{1,0:T(8,128)S(1)} %get-tuple-element.34.p, s32[2,512]{1,0:T(2,128)S(1)} %bitcast.14, f32[24,512]{1,0:T(8,128)S(1)} %collective-permute-done.6.from_low, f32[24,512]{1,0:T(8,128)S(1)} %collective-permute-done.7.from_up), custom_call_target="tpu_custom_call" | custom-call | flops 10000000 | bytes 1000000 | tf_op jit(solution)/shard_map/finish/pallas_call | solution.py:456
  71.5 3.4 %collective-permute-start.8 = (f32[24,512]{1,0:T(8,128)S(1)}, f32[24,512]{1,0:T(8,128)S(1)}, u32[]{:S(2)}, u32[]{:S(2)}) collective-permute-start(f32[24,512]{1,0:T(8,128)S(1)} %get-tuple-element.38), channel_id=1, source_target_pairs={{0,8},{8,16},{16,24},{24,32},{32,40},{40,48},{48,56},{56,64},{64,7... | collective-permute-start | bytes 147464 | tf_op jit(solution)/shard_map/ppermute | solution.py:407
  74.9 4.9 %collective-permute-start.9 = (f32[24,512]{1,0:T(8,128)S(1)}, f32[24,512]{1,0:T(8,128)S(1)}, u32[]{:S(2)}, u32[]{:S(2)}) collective-permute-start(f32[24,512]{1,0:T(8,128)S(1)} %get-tuple-element.39), channel_id=1, source_target_pairs={{8,0},{16,8},{24,16},{32,24},{40,32},{48,40},{56,48},{64,56},{72,6... | collective-permute-start | bytes 147464 | tf_op jit(solution)/shard_map/ppermute | solution.py:407
  79.8 2.5 %early_gradient.1.early = f32[8,40,128]{2,1,0:T(8,128)S(1)} custom-call(f32[1536,128]{1,0:T(8,128)S(1)} %get-tuple-element.25.got0, f32[1536,128]{1,0:T(8,128)S(1)} %get-tuple-element.32.got1, f32[256,128]{1,0:T(8,128)S(1)} %field.1.y, s32[8,128]{1,0:T(8,128)S(1)} %bitcast.15, f32[3,64,1024]{2,1,0:T(8,128)S(1)} %copy-done.8), custom_call_target="tpu_custom_call" | custom-call | flops 1000000000 | bytes 10000000 | tf_op jit(solution)/shard_map/early_gradient/pallas_call | solution.py:464
  82.4 6.1 %third.1 = (f32[1536,128]{1,0:T(8,128)S(1)}, f32[8,128]{1,0:T(8,128)S(1)}) custom-call(f32[2]{0:T(128)S(1)} %copy-done.7, f32[24,2048]{1,0:T(8,128)S(1)} %get-tuple-element.37.v, f32[24,512]{1,0:T(8,128)S(1)} %collective-permute-done.8.low, f32[24,512]{1,0:T(8,128)S(1)} %collective-permute-done.9.up, s32[64,128]{1,0:T(8,128)S(1)} %copy-done.4, ...), custom_call_target="tpu_custom_call" | custom-call | flops 1000000000 | bytes 10000000 | tf_op jit(solution)/shard_map/third/pallas_call | solution.py:468
  88.5 1.3 %late_gradient.1 = f32[8,64,128]{2,1,0:T(8,128)S(1)} custom-call(f32[8,40,128]{2,1,0:T(8,128)S(1)} %early_gradient.1.early, f32[1536,128]{1,0:T(8,128)S(1)} %get-tuple-element.40.got2, f32[256,128]{1,0:T(8,128)S(1)} %field.1.y, s32[8,128]{1,0:T(8,128)S(1)} %bitcast.16, f32[3,64,1024]{2,1,0:T(8,128)S(1)} %copy-done.8, f32[8,128]{1,0:T(8,128)S(1)} %get-tuple-element.41.line), custom_call_target="tpu_custom_call" | custom-call | flops 1000000000 | bytes 10000000 | tf_op jit(solution)/shard_map/late_gradient/pallas_call | solution.py:472
  89.8 11.8 %all_to_all.14.shares = f32[8,64,128]{2,1,0:T(8,128)S(1)} all-to-all(f32[8,64,128]{2,1,0:T(8,128)S(1)} %late_gradient.1), channel_id=1, replica_groups=mesh['mesh'=32,'harm'=8] {'harm'}, dimensions={0} | all-to-all | bytes 524288 | tf_op jit(solution)/shard_map/all_to_all | solution.py:475
  101.6 16.5 %all_to_all.15 = f32[32,128,1]{1,2,0:T(1,128)S(1)} all-to-all(f32[32,128,1]{1,2,0:T(1,128)S(1)} %bitcast.11), channel_id=1, replica_groups=mesh['mesh'=32,'harm'=8] {'mesh'}, dimensions={0} | all-to-all | bytes 32768 | tf_op jit(solution)/shard_map/all_to_all | solution.py:477
  118.0 1.0 last.1
  (24 shorter events, 0.1 us)
Async XLA Ops:
  2.9 15.0 %collective-permute-start = (f32[32,512]{1,0:T(8,128)}, f32[32,512]{1,0:T(8,128)S(1)}, u32[]{:S(2)}, u32[]{:S(2)}) collective-permute-start(f32[32,512]{1,0:T(8,128)} %get-tuple-element.23), channel_id=1, source_target_pairs={{0,8},{8,16},{16,24},{24,32},{32,40},{40,48},{48,56},{56,64},{64,7... | collective-permute-start | bytes 196616 | tf_op jit(solution)/shard_map/ppermute | solution.py:407
  6.7 10.1 %copy-start.1 = (f32[64,64,128]{2,1,0:T(8,128)S(1)}, f32[64,64,128]{2,1,0:T(8,128)}, u32[]{:S(2)}) copy-start(f32[64,64,128]{2,1,0:T(8,128)} %stiff.1) | copy-start | bytes 6291460
  6.7 10.1 %copy-start.2 = (f32[64,64,128]{2,1,0:T(8,128)S(1)}, f32[64,64,128]{2,1,0:T(8,128)}, u32[]{:S(2)}) copy-start(f32[64,64,128]{2,1,0:T(8,128)} %mass.1) | copy-start | bytes 6291460
  6.8 11.2 %collective-permute-start.1 = (f32[32,512]{1,0:T(8,128)}, f32[32,512]{1,0:T(8,128)S(1)}, u32[]{:S(2)}, u32[]{:S(2)}) collective-permute-start(f32[32,512]{1,0:T(8,128)} %get-tuple-element.24), channel_id=1, source_target_pairs={{8,0},{16,8},{24,16},{32,24},{40,32},{48,40},{56,48},{64,56},{72,6... | collective-permute-start | bytes 196616 | tf_op jit(solution)/shard_map/ppermute | solution.py:407
  12.9 0.8 copy-start.3
  13.6 3.2 %copy-start.7 = (f32[2]{0:T(128)S(1)}, f32[2]{0:T(128)}, u32[]{:S(2)}) copy-start(f32[2]{0:T(128)} %freq.7) | copy-start | bytes 28
  16.8 1.1 copy-start
  16.8 1.1 copy-start.4
  16.8 1.1 copy-start.5
  18.0 20.9 %copy-start.6 = (s32[1,2,512]{2,1,0:T(2,128)S(1)}, s32[1,2,512]{2,1,0:T(2,128)}, u32[]{:S(2)}) copy-start(s32[1,2,512]{2,1,0:T(2,128)} %param.17) | copy-start | bytes 12292
  29.1 8.1 %collective-permute-start.2 = (f32[24,512]{1,0:T(8,128)S(1)}, f32[24,512]{1,0:T(8,128)S(1)}, u32[]{:S(2)}, u32[]{:S(2)}) collective-permute-start(f32[24,512]{1,0:T(8,128)S(1)} %get-tuple-element.27), channel_id=1, source_target_pairs={{0,8},{8,16},{16,24},{24,32},{32,40},{40,48},{48,56},{56,64},{64,7... | collective-permute-start | bytes 147464 | tf_op jit(solution)/shard_map/ppermute | solution.py:407
  31.0 7.8 %collective-permute-start.3 = (f32[24,512]{1,0:T(8,128)S(1)}, f32[24,512]{1,0:T(8,128)S(1)}, u32[]{:S(2)}, u32[]{:S(2)}) collective-permute-start(f32[24,512]{1,0:T(8,128)S(1)} %get-tuple-element.28), channel_id=1, source_target_pairs={{8,0},{16,8},{24,16},{32,24},{40,32},{48,40},{56,48},{64,56},{72,6... | collective-permute-start | bytes 147464 | tf_op jit(solution)/shard_map/ppermute | solution.py:407
  40.0 8.5 %collective-permute-start.4 = (f32[24,512]{1,0:T(8,128)S(1)}, f32[24,512]{1,0:T(8,128)S(1)}, u32[]{:S(2)}, u32[]{:S(2)}) collective-permute-start(f32[24,512]{1,0:T(8,128)S(1)} %get-tuple-element.30), channel_id=1, source_target_pairs={{0,8},{8,16},{16,24},{24,32},{32,40},{40,48},{48,56},{56,64},{64,7... | collective-permute-start | bytes 147464 | tf_op jit(solution)/shard_map/ppermute | solution.py:407
  41.9 8.1 %collective-permute-start.5 = (f32[24,512]{1,0:T(8,128)S(1)}, f32[24,512]{1,0:T(8,128)S(1)}, u32[]{:S(2)}, u32[]{:S(2)}) collective-permute-start(f32[24,512]{1,0:T(8,128)S(1)} %get-tuple-element.31), channel_id=1, source_target_pairs={{8,0},{16,8},{24,16},{32,24},{40,32},{48,40},{56,48},{64,56},{72,6... | collective-permute-start | bytes 147464 | tf_op jit(solution)/shard_map/ppermute | solution.py:407
  60.1 19.7 %copy-start.8 = (f32[3,64,1024]{2,1,0:T(8,128)S(1)}, f32[3,64,1024]{2,1,0:T(8,128)}, u32[]{:S(2)}) copy-start(f32[3,64,1024]{2,1,0:T(8,128)} %node_shape.3) | copy-start | bytes 2359300
  60.1 19.7 %copy-start.9 = (s32[1024]{0:T(1024)S(1)}, s32[1024]{0:T(1024)}, u32[]{:S(2)}) copy-start(s32[1024]{0:T(1024)} %param.18) | copy-start | bytes 12292
  60.2 9.2 %collective-permute-start.6 = (f32[24,512]{1,0:T(8,128)S(1)}, f32[24,512]{1,0:T(8,128)S(1)}, u32[]{:S(2)}, u32[]{:S(2)}) collective-permute-start(f32[24,512]{1,0:T(8,128)S(1)} %get-tuple-element.35), channel_id=1, source_target_pairs={{0,8},{8,16},{16,24},{24,32},{32,40},{40,48},{48,56},{56,64},{64,7... | collective-permute-start | bytes 147464 | tf_op jit(solution)/shard_map/ppermute | solution.py:407
  63.8 6.6 %collective-permute-start.7 = (f32[24,512]{1,0:T(8,128)S(1)}, f32[24,512]{1,0:T(8,128)S(1)}, u32[]{:S(2)}, u32[]{:S(2)}) collective-permute-start(f32[24,512]{1,0:T(8,128)S(1)} %get-tuple-element.36), channel_id=1, source_target_pairs={{8,0},{16,8},{24,16},{32,24},{40,32},{48,40},{56,48},{64,56},{72,6... | collective-permute-start | bytes 147464 | tf_op jit(solution)/shard_map/ppermute | solution.py:407
  71.5 10.9 %collective-permute-start.8 = (f32[24,512]{1,0:T(8,128)S(1)}, f32[24,512]{1,0:T(8,128)S(1)}, u32[]{:S(2)}, u32[]{:S(2)}) collective-permute-start(f32[24,512]{1,0:T(8,128)S(1)} %get-tuple-element.38), channel_id=1, source_target_pairs={{0,8},{8,16},{16,24},{24,32},{32,40},{40,48},{48,56},{56,64},{64,7... | collective-permute-start | bytes 147464 | tf_op jit(solution)/shard_map/ppermute | solution.py:407
  74.9 7.5 %collective-permute-start.9 = (f32[24,512]{1,0:T(8,128)S(1)}, f32[24,512]{1,0:T(8,128)S(1)}, u32[]{:S(2)}, u32[]{:S(2)}) collective-permute-start(f32[24,512]{1,0:T(8,128)S(1)} %get-tuple-element.39), channel_id=1, source_target_pairs={{8,0},{16,8},{24,16},{32,24},{40,32},{48,40},{56,48},{64,56},{72,6... | collective-permute-start | bytes 147464 | tf_op jit(solution)/shard_map/ppermute | solution.py:407
